TPU v7x, 32 devices: a whole 2x2x4 slice. The times are simulated.
32 devices in a mesh: src: 8 (over y, x, core), dst: 4 (over z).
Axes of the slice: x: 2, y: 2, z: 4, core: 2. Of those that a mesh axis runs over, the one named last changes fastest.
Arguments:
- src_table: float32 [400, 8192], P(None, ('src', 'dst')), may hold values from -3 to 3
- src_state: float32 [8192], P(('src', 'dst')), may hold values from 0.01 to 0.1
- dst_table: float32 [400, 8192], P(None, ('src', 'dst')), may hold values from -3 to 3
- dst_state: float32 [8192], P(('src', 'dst')), may hold values from 0.01 to 0.1
- spare_table: float32 [400, 8192], P(None, ('src', 'dst')), may hold values from -3 to 3
- spare_state: float32 [8192], P(('src', 'dst')), may hold values from 0.01 to 0.1
- relations: float32 [400, 16], replicated, may hold values from -1 to 1
- rel_state: float32 [400, 16], replicated, may hold values from 5 to 51
- edge_rows: int32 [2, 2, 8192], P(None, None, ('src', 'dst')), may hold values from 0 to 255
- edge_rel: int32 [2, 8192], P(None, ('src', 'dst')), may hold values from 0 to 15
- counts: int32 [2, 32], P(None, ('src', 'dst')), may hold values from 48 to 256, as said below
- negatives: int32 [2, 16384], P(None, ('src', 'dst')), may hold values from 0 to 255
Outputs:
- src_out: float32 [400, 8192], P(None, ('src', 'dst'))
- src_state_out: float32 [8192], P(('src', 'dst'))
- dst_out: float32 [400, 8192], P(None, ('src', 'dst'))
- dst_state_out: float32 [8192], P(('src', 'dst'))
- spare_out: float32 [400, 8192], P(None, ('src', 'dst'))
- spare_state_out: float32 [8192], P(('src', 'dst'))
- relations_out: float32 [400, 16], replicated
- rel_state_out: float32 [400, 16], replicated
Inputs may be any that keep to these rules, and one draw needn't show every extreme that they name: `edge_rows`: local columns of a bucket's source slab (first row) and destination slab (second row). `counts`: in each round some bucket holds exactly 256 valid edges and some exactly 48; edge slots at or past a bucket's count are padding.
All inputs are finite; a program needn't handle non-finite values.
Results may differ from a plain program's by a relative error of at most 0.0003.
Values sent between devices are 32-bit elements; how exact they have to be, the bound alone decides.
No kernel may reach another device: no remote copies, remote signals or barrier semaphores. Data moves between devices by JAX's collectives and lax.ppermute only.
A program may use at most 64 MiB of HBM per device.

v0:
```python
import jax
import jax.numpy as jnp
from jax import lax
from jax.sharding import PartitionSpec as P

ROW_RATE = 0.25
REL_RATE = 0.5
NEG_WEIGHT = 0.0625
PRECISE = lax.Precision.HIGHEST


def swapped(array, axis, stride):
    return lax.ppermute(array, axis, [(i, i ^ 1 << stride) for i in range(lax.axis_size(axis))])


def passed_along(array, axis, by):
    count = lax.axis_size(axis)
    return lax.ppermute(array, axis, [(i, (i + by) % count) for i in range(count)])


def column_onehot(index, length):
    return (index[None, :] == lax.broadcasted_iota(jnp.int32, (length, index.shape[0]), 0)).astype(
        jnp.float32
    )


def fetch_cols(table, index):
    return jnp.take(table, index, axis=1)


def add_cols(running, index, values):
    return running.at[:, index].add(values)


def negative_terms(query, valid_mask, neg_cols):
    neg_scores = lax.dot_general(query, neg_cols, (((0,), (0,)), ((), ())), precision=PRECISE)
    neg_grad = jnp.where(valid_mask[:, None], NEG_WEIGHT * jax.nn.sigmoid(neg_scores), 0.0)
    back_query = lax.dot_general(neg_cols, neg_grad, (((1,), (1,)), ((), ())), precision=PRECISE)
    back_table = jnp.dot(query, neg_grad, precision=PRECISE)
    return (back_query, back_table)


def bucket(table_src, table_dst, relations, edge_pairs, rel_ids, live_count, negatives):
    source = edge_pairs[0]
    target = edge_pairs[1]
    edge_total = source.shape[0]
    rel_onehot = column_onehot(rel_ids, relations.shape[1])
    rel_cols = jnp.dot(relations, rel_onehot, precision=PRECISE)
    src_cols = fetch_cols(table_src, source)
    query = src_cols * rel_cols
    dst_cols = fetch_cols(table_dst, target)
    neg_cols = fetch_cols(table_dst, negatives)
    positive = jnp.sum(query * dst_cols, axis=0)
    valid_mask = lax.broadcasted_iota(jnp.int32, (edge_total,), 0) < live_count
    pos_grad = jnp.where(valid_mask, -jax.nn.sigmoid(-positive), 0.0)
    back_query, back_table = negative_terms(query, valid_mask, neg_cols)
    query_grad = dst_cols * pos_grad[None, :] + back_query
    src_grad = add_cols(jnp.zeros_like(table_src), source, query_grad * rel_cols)
    rel_grad = lax.dot_general(
        query_grad * src_cols, rel_onehot, (((1,), (1,)), ((), ())), precision=PRECISE
    )
    dst_grad = add_cols(
        add_cols(jnp.zeros_like(table_dst), target, query * pos_grad[None, :]),
        negatives,
        back_table,
    )
    return (src_grad, dst_grad, rel_grad)


def row_step(table, state, gradient):
    new_state = state + jnp.mean(gradient * gradient, axis=0)
    return (table - ROW_RATE * gradient / jnp.sqrt(new_state)[None, :], new_state)


def per_device(
    src_table,
    src_state,
    dst_table,
    dst_state,
    spare_table,
    spare_state,
    relations,
    rel_state,
    edge_rows,
    edge_rel,
    counts,
    negatives,
):
    spare_in, spare_acc = swapped((spare_table, spare_state), "dst", 0)
    src_grad, dst_grad, rel_first = bucket(
        src_table, dst_table, relations, edge_rows[0], edge_rel[0], counts[0, 0], negatives[0]
    )
    dst_next, dst_acc = row_step(dst_table, dst_state, dst_grad)
    src_next, src_acc = row_step(src_table, src_state, src_grad)
    moved_src, moved_acc = passed_along((src_next, src_acc), "src", 1)
    second_grad, spare_grad, rel_second = bucket(
        moved_src, spare_in, relations, edge_rows[1], edge_rel[1], counts[1, 0], negatives[1]
    )
    src_out, src_state_out = row_step(moved_src, moved_acc, second_grad)
    spare_out, spare_state_out = row_step(spare_in, spare_acc, spare_grad)
    rel_total = lax.psum(rel_first + rel_second, ("src", "dst"))
    rel_state_out = rel_state + rel_total * rel_total
    relations_out = relations - REL_RATE * rel_total / jnp.sqrt(rel_state_out)
    return (
        src_out,
        src_state_out,
        dst_next,
        dst_acc,
        spare_out,
        spare_state_out,
        relations_out,
        rel_state_out,
    )


def solution(mesh):
    in_specs = (
        P(None, ("src", "dst")),
        P(("src", "dst")),
        P(None, ("src", "dst")),
        P(("src", "dst")),
        P(None, ("src", "dst")),
        P(("src", "dst")),
        P(),
        P(),
        P(None, None, ("src", "dst")),
        P(None, ("src", "dst")),
        P(None, ("src", "dst")),
        P(None, ("src", "dst")),
    )
    out_specs = (
        P(None, ("src", "dst")),
        P(("src", "dst")),
        P(None, ("src", "dst")),
        P(("src", "dst")),
        P(None, ("src", "dst")),
        P(("src", "dst")),
        P(),
        P(),
    )
    return jax.shard_map(
        per_device, mesh=mesh, in_specs=in_specs, out_specs=out_specs, check_vma=False
    )
```

profile of v0, /device:TPU:0, one launch (start us, length us, event | category | flops | bytes accessed | tf_op | source)
XLA Modules:
  0.0 115.2 jit_solution(795749581461652857)
XLA Ops:
  0.7 3.1 %collective-permute-start.3 = (f32[256]{0:T(256)}, f32[256]{0:T(256)}, u32[]{:S(2)}, u32[]{:S(2)}) collective-permute-start(f32[256]{0:T(256)} %param.21), channel_id=1, source_target_pairs={{0,1},{1,0},{2,3},{3,2},{4,5},{5,4},{6,7},{7,6},{8,9},{9,8},{10,11... | collective-permute-start | bytes 3080 | tf_op jit(solution)/shard_map/ppermute | solution.py:13
  3.7 2.0 %copy.46 = f32[400,256]{0,1:T(8,128)} copy(f32[400,256]{1,0:T(8,128)} %param.20) | data formatting | bytes 819200 | tf_op args[4]
  13.2 1.1 fusion.30
  15.0 2.3 %gather_fusion.2 = f32[512,400]{1,0:T(8,128)} fusion(f32[400,256]{0,1:T(8,128)S(1)} %copy.39, s32[1024]{0:T(1024)S(1)} %pad_clamp_fusion.3), kind=kCustom, calls=%fused_computation.1.clone | custom fusion | bytes 1640448 | tf_op jit(solution)/shard_map/jit(_take)/gather | solution.py:28
  17.4 3.3 %fusion.9 = f32[256,512]{1,0:T(8,128)S(1)} fusion(f32[400,256]{1,0:T(8,128)S(1)} %get-tuple-element.39, f32[512,400]{1,0:T(8,128)} %gather_fusion.2, pred[512]{0:T(512)(128)(4,1)S(1)} %compare_and_fusion.3, pred[256]{0:T(512)(128)(4,1)S(1)} %iota_compare_fusion.7), kind=kOutput, calls=%fused_computation.23 | convolution fusion | flops 630005760 | bytes 1753856 | tf_op jit(solution)/shard_map/dot_general | solution.py:36
  20.7 1.9 %convolution_add_fusion = f32[400,256]{1,0:T(8,128)S(1)} fusion(f32[256,512]{1,0:T(8,128)S(1)} %fusion.9, f32[512,400]{1,0:T(8,128)S(1)} %copy-done.1, pred[512]{0:T(512)(128)(4,1)S(1)} %compare_and_fusion.3, f32[256,400]{0,1:T(8,128)S(1)} %copy.40, f32[256]{0:T(256)S(1)} %negate_select_fusion.1, pred[256]{0:T(512)(128)(4,1)S(1)} %compare_and_fusion.5), kind=kOutput, calls=%fused_computation.26 | convolution fusion | flops 629657600 | bytes 2164480 | tf_op jit(solution)/shard_map/dot_general | solution.py:38
  23.5 1.0 copy.44
  24.5 2.7 %scatter_custom_fusion = f32[400,256]{0,1:T(8,128)S(1)} fusion(s32[256]{0:T(256)S(1)} %bitcast.110, f32[256,400]{1,0:T(8,128)} %copy.44, f32[]{:T(128)} %constant.24.clone.1), kind=kCustom, calls=%fused_computation.77 | custom fusion | flops 102400 | bytes 410112 | tf_op jit(solution)/shard_map/scatter-add | solution.py:32
  29.4 2.0 %collective-permute-start = (f32[400,256]{0,1:T(8,128)}, f32[400,256]{0,1:T(8,128)S(1)}, u32[]{:S(2)}, u32[]{:S(2)}) collective-permute-start(f32[400,256]{0,1:T(8,128)} %divide_subtract_fusion.3), channel_id=1, source_target_pairs={{0,4},{4,8},{8,12},{12,16},{16,20},{20,24},{24,28},{28,0},{1,5},{5... | collective-permute-start | bytes 1228808 | tf_op jit(solution)/shard_map/ppermute | solution.py:18
  31.5 2.8 %fusion.64 = f32[512,400]{1,0:T(8,128)} fusion(f32[256,512]{1,0:T(8,128)S(1)} %copy-done.3, f32[400,256]{1,0:T(8,128)S(1)} %get-tuple-element.39), kind=kOutput, calls=%fused_computation.137 | convolution fusion | flops 629145600 | bytes 1753088 | tf_op jit(solution)/shard_map/dot_general | solution.py:39
  35.3 2.7 %scatter_custom_fusion.2 = f32[400,256]{0,1:T(8,128)S(1)} fusion(s32[256]{0:T(256)S(1)} %bitcast.109, f32[256,400]{1,0:T(8,128)} %copy.50, f32[]{:T(128)} %constant.24.clone.1), kind=kCustom, calls=%fused_computation.73 | custom fusion | flops 102400 | bytes 410112 | tf_op jit(solution)/shard_map/scatter-add | solution.py:32
  38.1 4.7 %scatter_fusion = f32[400,256]{0,1:T(8,128)S(1)} fusion(f32[400,256]{0,1:T(8,128)S(1)} %scatter_custom_fusion.2, s32[512]{0:T(512)S(1)} %bitcast.102, f32[512,400]{1,0:T(8,128)} %fusion.64), kind=kCustom, calls=%fused_computation.9 | custom fusion | flops 204800 | bytes 2459648 | tf_op jit(solution)/shard_map/scatter-add | solution.py:32
  48.4 1.1 fusion.27
  49.5 1.6 %gather_fusion.5 = f32[512,400]{1,0:T(8,128)S(1)} fusion(f32[400,256]{0,1:T(8,128)S(1)} %collective-permute-done.1, s32[1024]{0:T(1024)S(1)} %pad_clamp_fusion), kind=kCustom, calls=%fused_computation.5.clone | custom fusion | bytes 1640448 | tf_op jit(solution)/shard_map/jit(_take)/gather | solution.py:28
  51.1 2.0 %fusion.4 = f32[256,512]{1,0:T(8,128)S(1)} fusion(f32[400,256]{1,0:T(8,128)S(1)} %get-tuple-element.35, f32[512,400]{1,0:T(8,128)S(1)} %gather_fusion.5, pred[512]{0:T(512)(128)(4,1)S(1)} %compare_and_fusion, pred[256]{0:T(512)(128)(4,1)S(1)} %iota_compare_fusion.6), kind=kOutput, calls=%fused_computation.17 | convolution fusion | flops 630005760 | bytes 1753856 | tf_op jit(solution)/shard_map/dot_general | solution.py:36
  53.2 1.9 %fusion.10 = f32[400,256]{1,0:T(8,128)S(1)} fusion(f32[256,512]{1,0:T(8,128)S(1)} %fusion.4, f32[512,400]{1,0:T(8,128)S(1)} %gather_fusion.5, pred[512]{0:T(512)(128)(4,1)S(1)} %compare_and_fusion), kind=kOutput, calls=%fused_computation.28 | convolution fusion | flops 629350400 | bytes 1753600 | tf_op jit(solution)/shard_map/dot_general | solution.py:38
  55.1 2.8 %fusion.65 = f32[512,400]{1,0:T(8,128)} fusion(f32[256,512]{1,0:T(8,128)S(1)} %fusion.4, f32[400,256]{1,0:T(8,128)S(1)} %get-tuple-element.35), kind=kOutput, calls=%fused_computation.138 | convolution fusion | flops 629145600 | bytes 1753088 | tf_op jit(solution)/shard_map/dot_general | solution.py:39
  59.7 1.0 copy.53
  60.7 2.7 %scatter_custom_fusion.4 = f32[400,256]{0,1:T(8,128)S(1)} fusion(s32[256]{0:T(256)} %bitcast.108, f32[256,400]{1,0:T(8,128)} %copy.53, f32[]{:T(128)} %constant.24.clone.1), kind=kCustom, calls=%fused_computation.71 | custom fusion | flops 102400 | bytes 410112 | tf_op jit(solution)/shard_map/scatter-add | solution.py:32
  63.4 4.1 %scatter_fusion.1 = f32[400,256]{0,1:T(8,128)S(1)} fusion(f32[400,256]{0,1:T(8,128)S(1)} %scatter_custom_fusion.4, s32[512]{0:T(512)S(1)} %bitcast.101, f32[512,400]{1,0:T(8,128)S(1)} %copy-done), kind=kCustom, calls=%fused_computation.11 | custom fusion | flops 204800 | bytes 2459648 | tf_op jit(solution)/shard_map/scatter-add | solution.py:32
  67.8 2.3 %scatter_custom_fusion.1 = f32[400,256]{0,1:T(8,128)S(1)} fusion(s32[256]{0:T(256)} %bitcast.107, f32[256,400]{1,0:T(8,128)S(1)} %copy.49, f32[]{:T(128)} %constant.24.clone.1), kind=kCustom, calls=%fused_computation.75 | custom fusion | flops 102400 | bytes 410112 | tf_op jit(solution)/shard_map/scatter-add | solution.py:32
  70.3 1.2 %fusion.56 = (f32[256]{0:T(256)S(1)}, f32[256]{0:T(256)}) fusion(f32[256]{0:T(256)} %collective-permute-done.3, f32[256]{0:T(256)S(1)} %multiply_reduce_fusion), kind=kLoop, calls=%fused_computation.129 | loop fusion | flops 512 | bytes 4096 | tf_op jit(solution)/shard_map/sqrt | solution.py:72
  71.6 39.7 %psum.7 = f32[400,16]{0,1:T(8,128)S(1)} all-reduce(f32[400,16]{0,1:T(8,128)S(1)} %convolution_add_fusion.1), channel_id=1, replica_groups=mesh['src'=8,'dst'=4] {'src','dst'}, use_global_device_ids=true, to_apply=%region_12.15 | all-reduce | flops 6400 | bytes 51200 | tf_op jit(solution)/shard_map/psum | solution.py:101
  112.3 1.2 %fusion.58 = (f32[256]{0:T(256)S(1)}, f32[256]{0:T(256)}) fusion(f32[256]{0:T(256)} %collective-permute-done.2, f32[256]{0:T(256)S(1)} %multiply_reduce_fusion.2), kind=kLoop, calls=%fused_computation.131 | loop fusion | flops 512 | bytes 4096 | tf_op jit(solution)/shard_map/sqrt | solution.py:72
  (97 shorter events, 22.5 us)
Async XLA Ops:
  0.6 5.2 %copy-start.11 = (s32[2,2,256]{2,1,0:T(2,128)S(1)}, s32[2,2,256]{2,1,0:T(2,128)}, u32[]{:S(2)}) copy-start(s32[2,2,256]{2,1,0:T(2,128)} %param.24) | copy-start | bytes 12292
  0.6 8.5 %copy-start.7 = (f32[400,256]{1,0:T(8,128)S(1)}, f32[400,256]{1,0:T(8,128)}, u32[]{:S(2)}) copy-start(f32[400,256]{1,0:T(8,128)} %param.18) | copy-start | bytes 1228804
  0.7 69.6 %collective-permute-start.3 = (f32[256]{0:T(256)}, f32[256]{0:T(256)}, u32[]{:S(2)}, u32[]{:S(2)}) collective-permute-start(f32[256]{0:T(256)} %param.21), channel_id=1, source_target_pairs={{0,1},{1,0},{2,3},{3,2},{4,5},{5,4},{6,7},{7,6},{8,9},{9,8},{10,11... | collective-permute-start | bytes 3080 | tf_op jit(solution)/shard_map/ppermute | solution.py:13
  5.8 40.3 %collective-permute-start.1 = (f32[400,256]{0,1:T(8,128)}, f32[400,256]{0,1:T(8,128)S(1)}, u32[]{:S(2)}, u32[]{:S(2)}) collective-permute-start(f32[400,256]{0,1:T(8,128)} %copy.46), channel_id=1, source_target_pairs={{0,1},{1,0},{2,3},{3,2},{4,5},{5,4},{6,7},{7,6},{8,9},{9,8},{10,11... | collective-permute-start | bytes 1228808 | tf_op jit(solution)/shard_map/ppermute | solution.py:13
  6.4 0.7 copy-start.12
  7.1 0.7 copy-start.14
  8.4 0.7 copy-start.13
  10.3 1.0 copy-start.8
  12.5 0.8 copy-start.9
  17.4 3.4 %copy-start.1 = (f32[512,400]{1,0:T(8,128)S(1)}, f32[512,400]{1,0:T(8,128)}, u32[]{:S(2)}) copy-start(f32[512,400]{1,0:T(8,128)} %gather_fusion.2) | copy-start | bytes 2457604
  20.7 1.9 %copy-start.2 = (f32[256,512]{1,0:T(8,128)}, f32[256,512]{1,0:T(8,128)S(1)}, u32[]{:S(2)}) copy-start(f32[256,512]{1,0:T(8,128)S(1)} %fusion.9) | copy-start | bytes 1572868
  20.7 1.9 %copy-start.6 = (f32[400,256]{1,0:T(8,128)S(1)}, f32[400,256]{1,0:T(8,128)}, u32[]{:S(2)}) copy-start(f32[400,256]{1,0:T(8,128)} %get-tuple-element.58) | copy-start | bytes 1228804
  27.2 0.7 copy-start.15
  28.5 83.8 %collective-permute-start.2 = (f32[256]{0:T(256)}, f32[256]{0:T(256)}, u32[]{:S(2)}, u32[]{:S(2)}) collective-permute-start(f32[256]{0:T(256)} %get-tuple-element.37), channel_id=1, source_target_pairs={{0,4},{4,8},{8,12},{12,16},{16,20},{20,24},{24,28},{28,0},{1,5},{5... | collective-permute-start | bytes 3080 | tf_op jit(solution)/shard_map/ppermute | solution.py:18
  28.5 3.0 %copy-start.3 = (f32[256,512]{1,0:T(8,128)S(1)}, f32[256,512]{1,0:T(8,128)}, u32[]{:S(2)}) copy-start(f32[256,512]{1,0:T(8,128)} %copy-done.2) | copy-start | bytes 1572868
  29.4 17.8 %collective-permute-start = (f32[400,256]{0,1:T(8,128)}, f32[400,256]{0,1:T(8,128)S(1)}, u32[]{:S(2)}, u32[]{:S(2)}) collective-permute-start(f32[400,256]{0,1:T(8,128)} %divide_subtract_fusion.3), channel_id=1, source_target_pairs={{0,4},{4,8},{8,12},{12,16},{16,20},{20,24},{24,28},{28,0},{1,5},{5... | collective-permute-start | bytes 1228808 | tf_op jit(solution)/shard_map/ppermute | solution.py:18
  31.5 2.8 %copy-start.4 = (f32[256,400]{0,1:T(8,128)S(1)}, f32[256,400]{0,1:T(8,128)}, u32[]{:S(2)}) copy-start(f32[256,400]{0,1:T(8,128)} %get-tuple-element.60) | copy-start | bytes 1228804
  42.8 0.7 copy-start.16
  58.5 1.0 copy-start.5
  59.6 3.8 %copy-start = (f32[512,400]{1,0:T(8,128)S(1)}, f32[512,400]{1,0:T(8,128)}, u32[]{:S(2)}) copy-start(f32[512,400]{1,0:T(8,128)} %fusion.65) | copy-start | bytes 2457604
  113.7 0.9 copy-start.10
where the time goes:
time: 116 us; the launch traced here: 115 us
  blocking collectives  39.7 us (34%)
  other arithmetic  29.5 us (25%)
  local copies, waits for them, and re-layouts  22 us (19%)
  matrix products  17.7 us (15%)
  starting transfers between devices  5.14 us (4%)
    psum x1, blocking collectives, per_device(): rel_total = lax.psum(rel_first + rel_second, ('src', 'dst'))  39.7 us
    scatter-add x6, other arithmetic, add_cols(): return running.at[:, index].add(values)  19.2 us
    unnamed x40, local copies, waits for them, and re-layouts  9.68 us
    gather x10, local copies, waits for them, and re-layouts, fetch_cols(): return jnp.take(table, index, axis=1)  8.53 us
    dot_general x2, matrix products, negative_terms(): back_table = jnp.dot(query, neg_grad, precision=PRECISE)  5.6 us
    dot_general x2, matrix products, negative_terms(): lax.dot_general(query, neg_cols, (((0,), (0,)), ((), ())), precision=PREC...  5.37 us
    dot_general x2, matrix products, negative_terms(): lax.dot_general(neg_cols, neg_grad, (((1,), (1,)), ((), ())), precision=P...  3.8 us
    sqrt x4, other arithmetic, row_step(): jnp.sqrt(new_state)[None, :]  3.59 us
  transfers between devices with their start and end apart: 4, of which 0 were waited for; matrix products, arithmetic and copies ran while one was open for 54% of the time, Pallas kernels for 0%

commit v1 on v0

v1 whole, which is shorter than its diff:
```python
import jax
import jax.numpy as jnp
from jax import lax
from jax.experimental import pallas as pl
from jax.experimental.pallas import tpu as pltpu
from jax.sharding import PartitionSpec as P

ROW_RATE = 0.25
REL_RATE = 0.5
NEG_WEIGHT = 0.0625
F32 = jnp.float32
BF16 = jnp.bfloat16
NN = (((1,), (0,)), ((), ()))
NT = (((1,), (1,)), ((), ()))
TN = (((0,), (0,)), ((), ()))
VMEM = pl.BlockSpec(memory_space=pltpu.VMEM)
HBM = pl.BlockSpec(memory_space=pltpu.HBM)


def swapped(array, axis, stride):
    return lax.ppermute(array, axis, [(i, i ^ 1 << stride) for i in range(lax.axis_size(axis))])


def passed_along(array, axis, by):
    count = lax.axis_size(axis)
    return lax.ppermute(array, axis, [(i, (i + by) % count) for i in range(count)])


def radices(count):
    steps = []
    while count > 1:
        steps.append(4 if count % 4 == 0 else 2)
        count //= steps[-1]
    return steps


def exchanged_terms(array):
    n_src, n_dst = lax.axis_size("src"), lax.axis_size("dst")
    steps = [("src", 1, 2)]
    for axis, count, stride in (("src", n_src // 2, 2), ("dst", n_dst, 1)):
        for radix in radices(count):
            steps.append((axis, stride, radix))
            stride *= radix
    terms = [array]
    for axis, stride, radix in steps:
        array = tree_sum(terms)
        count = lax.axis_size(axis)
        terms = [array]
        for k in range(1, radix):
            terms.append(lax.ppermute(array, axis, [(i, i ^ k * stride) for i in range(count)]))
    return terms


def tree_sum(terms):
    while len(terms) > 1:
        terms = [a + b for a, b in zip(terms[::2], terms[1::2])]
    return terms[0]


def packed_shape(rels, features):
    whole, rest = divmod(features, 128)
    assert rest * rels <= 8 * 128 and rels % 8 == 0
    return (whole * rels + (8 if rest else 0), 128)


def pack(out, values):
    rels, features = values.shape
    whole, rest = divmod(features, 128)
    for k in range(whole):
        out[k * rels : (k + 1) * rels, :] = values[:, k * 128 : (k + 1) * 128]
    if rest:
        tail = [values[8 * k : 8 * (k + 1), whole * 128 :] for k in range(rels // 8)]
        tail.append(jnp.zeros((8, 128 - rest * len(tail)), F32))
        out[whole * rels :, :] = jnp.concatenate(tail, axis=1)


def unpack(packed, rels, features):
    whole, rest = divmod(features, 128)
    parts = [packed[k * rels : (k + 1) * rels, :] for k in range(whole)]
    if rest:
        tail = packed[whole * rels :, :]
        tails = [tail[:, k * rest : (k + 1) * rest] for k in range(rels // 8)]
        parts.append(jnp.concatenate(tails, axis=0))
    return jnp.concatenate(parts, axis=1)


def halves(x):
    high = x.astype(BF16)
    return high, (x - high.astype(F32)).astype(BF16)


def dot(a, b, dims):
    return lax.dot_general(a, b, dims, preferred_element_type=F32)


def dot_split(a, b, dims):
    return dot(a[0], b[0], dims) + dot(a[0], b[1], dims) + dot(a[1], b[0], dims)


def dot_left(a, b, dims):
    return dot(a[0], b, dims) + dot(a[1], b, dims)


def dot_right(a, b, dims):
    return dot(a, b[0], dims) + dot(a, b[1], dims)


def onehot(index, length):
    return index == lax.broadcasted_iota(jnp.int32, (length, index.shape[1]), 0)


def as_bf16(mask):
    return jnp.where(mask, 1.0, 0.0).astype(BF16)


def negative_weight(negatives, rows, edges):
    ones = jnp.ones((negatives.shape[1], edges), BF16)
    return NEG_WEIGHT * dot(as_bf16(onehot(negatives, rows)), ones, NN)


def coefficients(query, table_rows, weight, at_target, valid):
    scores = dot_split(table_rows, halves(query), NN)
    positive = jnp.sum(jnp.where(at_target, scores, 0.0), axis=0, keepdims=True)
    pos_grad = jnp.where(valid, -1.0 / (1.0 + jnp.exp(positive)), 0.0)
    neg_grad = jnp.where(valid, weight / (1.0 + jnp.exp(-scores)), 0.0)
    return neg_grad + jnp.where(at_target, pos_grad, 0.0)


def row_step(table, state, gradient):
    new_state = state + jnp.sum(gradient * gradient, axis=0, keepdims=True) * (1.0 / table.shape[0])
    return table - gradient * (ROW_RATE / jnp.sqrt(new_state)), new_state


def hot_relations(round_id, edge_rel, rels):
    return as_bf16(onehot(edge_rel[round_id : round_id + 1, :], rels))


def edge_parts(round_id, rows_of_table, rel, edge_rows, edge_rel, counts, negatives):
    edges = edge_rows.shape[2]
    rel_hot = hot_relations(round_id, edge_rel, rel.shape[0])
    src_hot = as_bf16(onehot(edge_rows[round_id, 0:1, :], rows_of_table))
    at_target = onehot(edge_rows[round_id, 1:2, :], rows_of_table)
    rel_cols = dot_left(halves(rel[...]), rel_hot, TN)
    place = lax.broadcasted_iota(jnp.int32, (1, edges), 1)
    valid = place < counts[:, round_id : round_id + 1]
    weight = negative_weight(negatives[round_id : round_id + 1, :], rows_of_table, edges)
    return src_hot, at_target, rel_cols, valid, weight


def first_front_kernel(
    src_hbm, state_hbm, dst_hbm, rel_hbm, rows_hbm, rels_hbm, counts_hbm, negs_hbm,
    moved_out, query_out, coef_out, product_out,
    src, src_state, dst, rel, rows, rels, counts, negs, sems,
):
    pairs = [
        (rows_hbm, rows), (rels_hbm, rels), (rel_hbm, rel), (counts_hbm, counts),
        (negs_hbm, negs), (dst_hbm, dst), (src_hbm, src), (state_hbm, src_state),
    ]
    copies = [pltpu.make_async_copy(a, b, sems.at[i]) for i, (a, b) in enumerate(pairs)]
    for copy in copies:
        copy.start()
    for copy in copies[:5]:
        copy.wait()
    features, columns = src.shape
    src_hot, at_target, rel_cols, valid, weight = edge_parts(
        0, columns, rel, rows, rels, counts, negs
    )
    copies[5].wait()
    table_dst = halves(dst[...])
    table_rows = halves(dst[...].T)
    copies[6].wait()
    src_cols = dot_left(halves(src[...]), src_hot, NN)
    query = src_cols * rel_cols
    coef = coefficients(query, table_rows, weight, at_target, valid)
    query_grad = dot_split(table_dst, halves(coef), NN)
    src_grad = dot_left(halves(query_grad * rel_cols), src_hot, NT)
    copies[7].wait()
    table, state = row_step(src[...], src_state[...], src_grad)
    moved_out[0:features, :] = table
    moved_out[features:, :] = jnp.broadcast_to(state, (moved_out.shape[0] - features, columns))
    query_out[...] = query
    coef_out[...] = coef
    product_out[...] = query_grad * src_cols


def first_back_kernel(
    dst, dst_state, query, coef, product, rel, rows, rels, counts, negs,
    spare_state, table_out, state_out, rel_first_out, rel_cols_out, weight_out, live_out, spare_out,
):
    grad = dot_split(halves(query[...]), halves(coef[...]), NT)
    table_out[...], state_out[...] = row_step(dst[...], dst_state[...], grad)
    edges, columns = rows.shape[2], dst.shape[1]
    rel_first_out[...] = dot_right(
        hot_relations(0, rels, rel.shape[0]), halves(product[...]), NT
    )
    rel_cols_out[...] = dot_left(halves(rel[...]), hot_relations(1, rels, rel.shape[0]), TN)
    weight_out[...] = negative_weight(negs[1:2, :], columns, edges)
    place = lax.broadcasted_iota(jnp.int32, (1, edges), 1)
    live_out[...] = jnp.where(place < counts[:, 1:2], 1.0, 0.0)
    spare_out[...] = spare_state[...]


def spare_kernel(spare, rows_high, rows_low, high, low):
    rows_high[...], rows_low[...] = halves(spare[...].T)
    high[...], low[...] = halves(spare[...])


def second_front_kernel(
    moved, rows_high, rows_low, high, low, rel_cols, weight, live, rows, rels, rel_first,
    state, query_out, coef_out, scaled_out, rel_out, state_out,
):
    features, columns = high.shape
    rel_hot = hot_relations(1, rels, rel_first.shape[0])
    src_hot = as_bf16(onehot(rows[1, 0:1, :], columns))
    at_target = onehot(rows[1, 1:2, :], columns)
    valid = live[...] > 0.0
    src_cols = dot_left(halves(moved[0:features, :]), src_hot, NN)
    query = src_cols * rel_cols[...]
    coef = coefficients(query, (rows_high[...], rows_low[...]), weight[...], at_target, valid)
    query_grad = dot_split((high[...], low[...]), halves(coef), NN)
    pack(rel_out, rel_first[...] + dot_right(rel_hot, halves(query_grad * src_cols), NT))
    state_out[...] = state[...]
    query_out[...] = query
    coef_out[...] = coef
    scaled_out[...] = query_grad * rel_cols[...]


def second_back_kernel(
    moved, spare, spare_state, rows, query, coef, scaled, src_out, src_acc, spare_out, spare_acc
):
    features = spare.shape[0]
    src_hot = as_bf16(onehot(rows[1, 0:1, :], spare.shape[1]))
    src_grad = dot_left(halves(scaled[...]), src_hot, NT)
    src_out[...], src_acc[...] = row_step(
        moved[0:features, :], moved[features : features + 1, :], src_grad
    )
    spare_grad = dot_split(halves(query[...]), halves(coef[...]), NT)
    spare_out[...], spare_acc[...] = row_step(spare[...], spare_state[...], spare_grad)


def relation_kernel(rel, rel_state, *refs):
    terms, (rel_out, state_out) = refs[:-2], refs[-2:]
    total = unpack(tree_sum([term[...] for term in terms]), *rel.shape)
    state = rel_state[...] + total * total
    state_out[...] = state
    rel_out[...] = rel[...] - REL_RATE * total / jnp.sqrt(state)


def call(kernel, in_specs, outs, flops, args, scratch=()):
    shapes = [a if isinstance(a, jax.ShapeDtypeStruct) else jax.ShapeDtypeStruct(a, F32) for a in outs]
    return pl.pallas_call(
        kernel,
        in_specs=in_specs,
        out_specs=[VMEM] * len(outs),
        out_shape=shapes,
        scratch_shapes=list(scratch),
        compiler_params=pltpu.CompilerParams(vmem_limit_bytes=40 * 1024 * 1024),
        cost_estimate=pl.CostEstimate(
            flops=flops, bytes_accessed=sum(a.size * 4 for a in args), transcendentals=0
        ),
    )(*args)


def per_device(
    src_table,
    src_state,
    dst_table,
    dst_state,
    spare_table,
    spare_state,
    relations,
    rel_state,
    edge_rows,
    edge_rel,
    counts,
    negatives,
):
    features, rows = src_table.shape
    edges = edge_rows.shape[2]
    rels = relations.shape[1]
    work = 2 * features * rows * edges
    rel = relations.T
    live = counts.T
    spare_in = swapped(spare_table, "dst", 0)
    operands = [
        src_table, src_state.reshape(1, rows), dst_table, rel, edge_rows, edge_rel, live, negatives,
    ]
    moved_first, query, coef, product = call(
        first_front_kernel,
        [HBM] * 8,
        [(features + 8, rows), (features, edges), (rows, edges), (features, edges)],
        400 * work,
        [pltpu.with_memory_space_constraint(a, pltpu.HBM) for a in operands],
        [pltpu.VMEM(a.shape, a.dtype) for a in operands]
        + [pltpu.SemaphoreType.DMA((len(operands),))],
    )
    moved = passed_along(moved_first, "src", 1)
    dst_next, dst_acc, rel_first, rel_cols, weight, valid, spare_acc = call(
        first_back_kernel,
        [VMEM] * 11,
        [
            (features, rows), (1, rows), (rels, features), (features, edges), (rows, edges),
            (1, edges), (1, rows),
        ],
        3 * work,
        [
            dst_table, dst_state.reshape(1, rows), query, coef, product,
            rel, edge_rows, edge_rel, live, negatives, spare_state.reshape(1, rows),
        ],
    )
    spare_acc_in = swapped(spare_acc, "dst", 0)
    spare_parts = call(
        spare_kernel,
        [VMEM],
        [jax.ShapeDtypeStruct((rows, features), BF16)] * 2
        + [jax.ShapeDtypeStruct((features, rows), BF16)] * 2,
        100 * work,
        [spare_in],
    )
    query, coef, scaled, rel_both, spare_acc_in = call(
        second_front_kernel,
        [VMEM] * 12,
        [
            (features, edges), (rows, edges), (features, edges), packed_shape(rels, features),
            (1, rows),
        ],
        12 * work,
        [
            moved, *spare_parts, rel_cols, weight, valid, edge_rows, edge_rel, rel_first,
            spare_acc_in,
        ],
    )
    src_out, src_state_out, spare_out, spare_state_out = call(
        second_back_kernel,
        [VMEM] * 7,
        [(features, rows), (1, rows), (features, rows), (1, rows)],
        5 * work,
        [moved, spare_in, spare_acc_in, edge_rows, query, coef, scaled],
    )
    terms = exchanged_terms(rel_both)
    relations_out, rel_state_out = call(
        relation_kernel,
        [VMEM] * (2 + len(terms)),
        [(rels, features), (rels, features)],
        rels * features,
        [rel, rel_state.T, *terms],
    )
    return (
        src_out,
        src_state_out.reshape(rows),
        dst_next,
        dst_acc.reshape(rows),
        spare_out,
        spare_state_out.reshape(rows),
        relations_out.T,
        rel_state_out.T,
    )


def solution(mesh):
    in_specs = (
        P(None, ("src", "dst")),
        P(("src", "dst")),
        P(None, ("src", "dst")),
        P(("src", "dst")),
        P(None, ("src", "dst")),
        P(("src", "dst")),
        P(),
        P(),
        P(None, None, ("src", "dst")),
        P(None, ("src", "dst")),
        P(None, ("src", "dst")),
        P(None, ("src", "dst")),
    )
    out_specs = (
        P(None, ("src", "dst")),
        P(("src", "dst")),
        P(None, ("src", "dst")),
        P(("src", "dst")),
        P(None, ("src", "dst")),
        P(("src", "dst")),
        P(),
        P(),
    )
    return jax.shard_map(
        per_device, mesh=mesh, in_specs=in_specs, out_specs=out_specs, check_vma=False
    )
```

time: 116 us -> 33 us (0.28)
  blocking collectives: 39.7 us -> 0 us
  other arithmetic: 29.5 us -> 0.01 us
  local copies, waits for them, and re-layouts: 22 us -> 0.66 us
  matrix products: 17.7 us -> 0 us
  waiting for transfers between devices: 0.01 us -> 11.5 us
  Pallas kernels: 0 us -> 8.77 us
  starting transfers between devices: 5.14 us -> 11.1 us
    psum x1 -> x0, blocking collectives: 39.7 us -> none  [per_device(): rel_total = lax.psum(rel_first + rel_second, ('src', 'dst'))]
    scatter-add x6 -> x0, other arithmetic: 19.2 us -> none  [add_cols(): return running.at[:, index].add(values)]
    dot_general x10 -> x0, matrix products: 17.7 us -> none  [the longest x2 5.6 us: negative_terms(): back_table = jnp.dot(query, neg_grad, precision=PRECISE)]
    unnamed x40 -> x18, local copies, waits for them, and re-layouts: 9.68 us -> 0.66 us
    pallas_call x0 -> x6, Pallas kernels: none -> 8.77 us  [call(): pl.pallas_call(kernel, in_specs=in_specs, out_specs=[VMEM] * len(outs), o...]
    gather x10 -> x0, local copies, waits for them, and re-layouts: 8.53 us -> none  [fetch_cols(): return jnp.take(table, index, axis=1)]
    ppermute x0 -> x7, starting transfers between devices: none -> 7.94 us  [exchanged_terms(): lax.ppermute(array, axis, [(i, i ^ k * stride) for i in range(count)])]
    ppermute x0 -> x7, waiting for transfers between devices: none -> 5.51 us  [exchanged_terms(): lax.ppermute(array, axis, [(i, i ^ k * stride) for i in range(count)])]
  transfers between devices with their start and end apart: 4 -> 10, of which waited for: 0 -> 7; matrix products, arithmetic and copies ran while one was open for 54% -> 0% of each run, Pallas kernels for 0% -> 19%
where the time goes in v1:
time: 33 us; the launch traced here: 32.8 us
  waiting for transfers between devices  11.5 us (35%)
  starting transfers between devices  11.1 us (34%)
  Pallas kernels  8.77 us (27%)
  between operations  0.77 us (2%)
  local copies, waits for them, and re-layouts  0.66 us (2%)
    pallas_call x6, Pallas kernels, call(): pl.pallas_call(kernel, in_specs=in_specs, out_specs=[VMEM] * len(outs), o...  8.77 us
    ppermute x7, starting transfers between devices, exchanged_terms(): lax.ppermute(array, axis, [(i, i ^ k * stride) for i in range(count)])  7.94 us
    ppermute x7, waiting for transfers between devices, exchanged_terms(): lax.ppermute(array, axis, [(i, i ^ k * stride) for i in range(count)])  5.51 us
    ppermute x2, waiting for transfers between devices, swapped(): lax.ppermute(array, axis, [(i, i ^ 1 << stride) for i in range(lax.axis_s...  4.14 us
    ppermute x2, starting transfers between devices, swapped(): lax.ppermute(array, axis, [(i, i ^ 1 << stride) for i in range(lax.axis_s...  3.13 us
    ppermute x1, waiting for transfers between devices, passed_along(): lax.ppermute(array, axis, [(i, (i + by) % count) for i in range(count)])  1.83 us
    unnamed x18, local copies, waits for them, and re-layouts  0.66 us
  transfers between devices with their start and end apart: 10, of which 7 were waited for; matrix products, arithmetic and copies ran while one was open for 0% of the time, Pallas kernels for 19%

profile of v1, /device:TPU:0, one launch (start us, length us, event | category | flops | bytes accessed | tf_op | source)
XLA Modules:
  0.0 32.8 jit_solution(3103767999450093954)
XLA Ops:
  0.6 3.1 %collective-permute-start.1 = (f32[400,256]{1,0:T(8,128)}, f32[400,256]{1,0:T(8,128)S(1)}, u32[]{:S(2)}, u32[]{:S(2)}) collective-permute-start(f32[400,256]{1,0:T(8,128)} %param.16), channel_id=1, source_target_pairs={{0,1},{1,0},{2,3},{3,2},{4,5},{5,4},{6,7},{7,6},{8,9},{9,8},{10,11... | collective-permute-start | bytes 1228808 | tf_op jit(solution)/shard_map/ppermute | solution.py:21
  3.7 3.3 %shard_map.179 = (f32[408,256]{1,0:T(8,128)S(1)}, f32[400,256]{1,0:T(8,128)S(1)}, f32[256,256]{1,0:T(8,128)S(1)}, f32[400,256]{1,0:T(8,128)S(1)}) custom-call(f32[400,256]{1,0:T(8,128)} %src_hbm.1, f32[1,256]{1,0:T(1,128)} %bitcast.21, f32[400,256]{1,0:T(8,128)} %dst.1, f32[16,400]{1,0:T(8,128)} %bitcast.11, s32[2,2,256]{2,1,0:T(2,128)} %rows.5, ...), custom_call_target="tpu_custom_call" | custom-call | flops 20971520000 | bytes 856072 | tf_op jit(solution)/shard_map/pallas_call | solution.py:251
  7.1 0.1 collective-permute-start
  7.2 0.6 %copy-done.4 = s32[2,512]{1,0:T(2,128)S(1)} copy-done((s32[2,512]{1,0:T(2,128)S(1)}, s32[2,512]{1,0:T(2,128)}, u32[]{:S(2)}) %copy-start.4) | copy-done | bytes 4120
  7.8 0.0 copy-done.3
  7.9 0.0 copy-done.6
  7.9 1.4 %shard_map.181 = (f32[400,256]{1,0:T(8,128)}, f32[1,256]{1,0:T(1,128)}, f32[16,400]{1,0:T(8,128)S(1)}, f32[400,256]{1,0:T(8,128)S(1)}, f32[256,256]{1,0:T(8,128)...) custom-call(f32[400,256]{1,0:T(8,128)S(1)} %copy-done, f32[1,256]{1,0:T(1,128)S(1)} %bitcast.15, ...), custom_call_target="tpu_custom_call" | custom-call | flops 157286400 | bytes 1528840 | tf_op jit(solution)/shard_map/pallas_call | solution.py:251
  9.2 0.0 collective-permute-start.2
  9.3 4.1 %collective-permute-done.1.spare = f32[400,256]{1,0:T(8,128)S(1)} collective-permute-done((f32[400,256]{1,0:T(8,128)}, f32[400,256]{1,0:T(8,128)S(1)}, u32[]{:S(2)}, u32[]{:S(2)}) %collective-permute-start.1) | collective-permute-done | bytes 409632 | tf_op jit(solution)/shard_map/ppermute | solution.py:21
  13.4 0.3 shard_map.180
  13.7 1.8 %collective-permute-done.moved = f32[408,256]{1,0:T(8,128)S(1)} collective-permute-done((f32[408,256]{1,0:T(8,128)S(1)}, f32[408,256]{1,0:T(8,128)S(1)}, u32[]{:S(2)}, u32[]{:S(2)}) %collective-permute-start) | collective-permute-done | bytes 417824 | tf_op jit(solution)/shard_map/ppermute | solution.py:26
  15.5 1.7 %shard_map.182 = (f32[400,256]{1,0:T(8,128)S(1)}, f32[256,256]{1,0:T(8,128)S(1)}, f32[400,256]{1,0:T(8,128)S(1)}, f32[56,128]{1,0:T(8,128)S(1)}, f32[1,256]{1,0:T(1,128)S(1)}) custom-call(f32[408,256]{1,0:T(8,128)S(1)} %collective-permute-done.moved, bf16[256,400]{1,0:T(8,128)(2,1)S(1)} %get-tuple-element.35.rows_high, ...), custom_call_target="tpu_custom_call" | custom-call | flops 629145600 | bytes 2761728 | tf_op jit(solution)/shard_map/pallas_call | solution.py:251
  17.2 1.2 %collective-permute-done.3 = f32[56,128]{1,0:T(8,128)S(1)} collective-permute-done((f32[56,128]{1,0:T(8,128)S(1)}, f32[56,128]{1,0:T(8,128)S(1)}, u32[]{:S(2)}, u32[]{:S(2)}) %collective-permute-start.3) | collective-permute-done | bytes 28704 | tf_op jit(solution)/shard_map/ppermute | solution.py:50
  18.4 1.5 %collective-permute-start.6 = (f32[56,128]{1,0:T(8,128)S(1)}, f32[56,128]{1,0:T(8,128)S(1)}, u32[]{:S(2)}, u32[]{:S(2)}) collective-permute-start(f32[56,128]{1,0:T(8,128)S(1)} %add.12), channel_id=1, source_target_pairs={{0,24},{4,28},{8,16},{12,20},{16,8},{20,12},{24,0},{28,4},{1,25},{... | collective-permute-start | bytes 86024 | tf_op jit(solution)/shard_map/ppermute | solution.py:50
  20.0 0.5 %collective-permute-start.5 = (f32[56,128]{1,0:T(8,128)S(1)}, f32[56,128]{1,0:T(8,128)S(1)}, u32[]{:S(2)}, u32[]{:S(2)}) collective-permute-start(f32[56,128]{1,0:T(8,128)S(1)} %add.12), channel_id=1, source_target_pairs={{0,16},{4,20},{8,24},{12,28},{16,0},{20,4},{24,8},{28,12},{1,17},{... | collective-permute-start | bytes 86024 | tf_op jit(solution)/shard_map/ppermute | solution.py:50
  20.5 1.4 %collective-permute-start.4 = (f32[56,128]{1,0:T(8,128)S(1)}, f32[56,128]{1,0:T(8,128)S(1)}, u32[]{:S(2)}, u32[]{:S(2)}) collective-permute-start(f32[56,128]{1,0:T(8,128)S(1)} %add.12), channel_id=1, source_target_pairs={{0,8},{4,12},{8,0},{12,4},{16,24},{20,28},{24,16},{28,20},{1,9},{5... | collective-permute-start | bytes 86024 | tf_op jit(solution)/shard_map/ppermute | solution.py:50
  21.9 1.3 %collective-permute-done.6 = f32[56,128]{1,0:T(8,128)S(1)} collective-permute-done((f32[56,128]{1,0:T(8,128)S(1)}, f32[56,128]{1,0:T(8,128)S(1)}, u32[]{:S(2)}, u32[]{:S(2)}) %collective-permute-start.6) | collective-permute-done | bytes 28704 | tf_op jit(solution)/shard_map/ppermute | solution.py:50
  23.2 0.6 %collective-permute-done.5 = f32[56,128]{1,0:T(8,128)S(1)} collective-permute-done((f32[56,128]{1,0:T(8,128)S(1)}, f32[56,128]{1,0:T(8,128)S(1)}, u32[]{:S(2)}, u32[]{:S(2)}) %collective-permute-start.5) | collective-permute-done | bytes 28704 | tf_op jit(solution)/shard_map/ppermute | solution.py:50
  23.8 0.5 %collective-permute-done.4 = f32[56,128]{1,0:T(8,128)S(1)} collective-permute-done((f32[56,128]{1,0:T(8,128)S(1)}, f32[56,128]{1,0:T(8,128)S(1)}, u32[]{:S(2)}, u32[]{:S(2)}) %collective-permute-start.4) | collective-permute-done | bytes 28704 | tf_op jit(solution)/shard_map/ppermute | solution.py:50
  24.4 2.9 %collective-permute-start.9 = (f32[56,128]{1,0:T(8,128)S(1)}, f32[56,128]{1,0:T(8,128)S(1)}, u32[]{:S(2)}, u32[]{:S(2)}) collective-permute-start(f32[56,128]{1,0:T(8,128)S(1)} %add_add_fusion.refs_0_), channel_id=1, source_target_pairs={{0,3},{1,2},{2,1},{3,0},{4,7},{5,6},{6,5},{7,4},{8,11},{9,10},{10,... | collective-permute-start | bytes 86024 | tf_op jit(solution)/shard_map/ppermute | solution.py:50
  27.3 1.5 %collective-permute-start.7 = (f32[56,128]{1,0:T(8,128)S(1)}, f32[56,128]{1,0:T(8,128)S(1)}, u32[]{:S(2)}, u32[]{:S(2)}) collective-permute-start(f32[56,128]{1,0:T(8,128)S(1)} %add_add_fusion.refs_0_), channel_id=1, source_target_pairs={{0,1},{1,0},{2,3},{3,2},{4,5},{5,4},{6,7},{7,6},{8,9},{9,8},{10,11... | collective-permute-start | bytes 86024 | tf_op jit(solution)/shard_map/ppermute | solution.py:50
  28.8 1.4 %shard_map.183 = (f32[400,256]{1,0:T(8,128)}, f32[1,256]{1,0:T(1,128)}, f32[400,256]{1,0:T(8,128)}, f32[1,256]{1,0:T(1,128)}) custom-call(f32[408,256]{1,0:T(8,128)S(1)} %collective-permute-done.moved, f32[400,256]{1,0:T(8,128)S(1)} %collective-permute-done.1.spare, f32[1,256]{1,0:T(1,128)S(1)} %get-tuple-element.47.spare_state, s32[2,2,256]{2,1,0:T(2,128)S(1)} %copy-done.3, ...), custom_call_target="tpu_custom_call" | custom-call | flops 262144000 | bytes 1913856 | tf_op jit(solution)/shard_map/pallas_call | solution.py:251
  30.3 1.8 %collective-permute-done.8.refs_2_ = f32[56,128]{1,0:T(8,128)S(1)} collective-permute-done((f32[56,128]{1,0:T(8,128)S(1)}, f32[56,128]{1,0:T(8,128)S(1)}, u32[]{:S(2)}, u32[]{:S(2)}) %collective-permute-start.8) | collective-permute-done | bytes 28704 | tf_op jit(solution)/shard_map/ppermute | solution.py:50
  32.1 0.7 %shard_map.184 = (f32[16,400]{1,0:T(8,128)}, f32[16,400]{1,0:T(8,128)}) custom-call(f32[16,400]{1,0:T(8,128)S(1)} %bitcast.13, f32[16,400]{1,0:T(8,128)S(1)} %bitcast.14, f32[56,128]{1,0:T(8,128)S(1)} %add_add_fusion.refs_0_, f32[56,128]{1,0:T(8,128)S(1)} %collective-permute-done.7.refs_1_, f32[56,128]{1,0:T(8,128)S(1)} %collective-permute-done.8.refs_2_, ...), custom_call_target="tpu_custom_call" | custom-call | flops 6400 | bytes 165888 | tf_op jit(solution)/shard_map/pallas_call | solution.py:251
  (22 shorter events, 0.1 us)
Async XLA Ops:
  0.6 12.8 %collective-permute-start.1 = (f32[400,256]{1,0:T(8,128)}, f32[400,256]{1,0:T(8,128)S(1)}, u32[]{:S(2)}, u32[]{:S(2)}) collective-permute-start(f32[400,256]{1,0:T(8,128)} %param.16), channel_id=1, source_target_pairs={{0,1},{1,0},{2,3},{3,2},{4,5},{5,4},{6,7},{7,6},{8,9},{9,8},{10,11... | collective-permute-start | bytes 1228808 | tf_op jit(solution)/shard_map/ppermute | solution.py:21
  3.7 3.5 %copy-start = (f32[400,256]{1,0:T(8,128)S(1)}, f32[400,256]{1,0:T(8,128)}, u32[]{:S(2)}) copy-start(f32[400,256]{1,0:T(8,128)} %dst.1) | copy-start | bytes 1228804
  3.7 3.5 %copy-start.1 = (f32[400,16]{0,1:T(8,128)S(1)}, f32[400,16]{0,1:T(8,128)}, u32[]{:S(2)}) copy-start(f32[400,16]{0,1:T(8,128)} %param.18) | copy-start | bytes 76804
  3.7 3.5 %copy-start.5 = (s32[2,256]{1,0:T(2,128)S(1)}, s32[2,256]{1,0:T(2,128)}, u32[]{:S(2)}) copy-start(s32[2,256]{1,0:T(2,128)} %rels.3) | copy-start | bytes 6148
  3.7 3.5 %copy-start.7 = (f32[256]{0:T(256)S(1)}, f32[256]{0:T(256)}, u32[]{:S(2)}) copy-start(f32[256]{0:T(256)} %param.17) | copy-start | bytes 3076
  3.7 3.5 %copy-start.8 = (s32[2,1]{0,1:T(1,128)S(1)}, s32[2,1]{0,1:T(1,128)}, u32[]{:S(2)}) copy-start(s32[2,1]{0,1:T(1,128)} %param.22) | copy-start | bytes 28
  7.1 8.4 %collective-permute-start = (f32[408,256]{1,0:T(8,128)S(1)}, f32[408,256]{1,0:T(8,128)S(1)}, u32[]{:S(2)}, u32[]{:S(2)}) collective-permute-start(f32[408,256]{1,0:T(8,128)S(1)} %get-tuple-element.34), channel_id=1, source_target_pairs={{0,4},{4,8},{8,12},{12,16},{16,20},{20,24},{24,28},{28,0},{1,5},{5... | collective-permute-start | bytes 1253384 | tf_op jit(solution)/shard_map/ppermute | solution.py:26
  7.2 0.7 %copy-start.4 = (s32[2,512]{1,0:T(2,128)S(1)}, s32[2,512]{1,0:T(2,128)}, u32[]{:S(2)}) copy-start(s32[2,512]{1,0:T(2,128)} %negs.1) | copy-start | bytes 12292
  7.2 0.7 %copy-start.3 = (s32[2,2,256]{2,1,0:T(2,128)S(1)}, s32[2,2,256]{2,1,0:T(2,128)}, u32[]{:S(2)}) copy-start(s32[2,2,256]{2,1,0:T(2,128)} %rows.5) | copy-start | bytes 12292
  7.2 0.7 %copy-start.6 = (f32[256]{0:T(256)S(1)}, f32[256]{0:T(256)}, u32[]{:S(2)}) copy-start(f32[256]{0:T(256)} %param.15) | copy-start | bytes 3076
  9.2 4.4 %collective-permute-start.2 = (f32[1,256]{1,0:T(1,128)S(1)}, f32[1,256]{1,0:T(1,128)S(1)}, u32[]{:S(2)}, u32[]{:S(2)}) collective-permute-start(f32[1,256]{1,0:T(1,128)S(1)} %get-tuple-element.46), channel_id=1, source_target_pairs={{0,1},{1,0},{2,3},{3,2},{4,5},{5,4},{6,7},{7,6},{8,9},{9,8},{10,11... | collective-permute-start | bytes 3080 | tf_op jit(solution)/shard_map/ppermute | solution.py:21
  17.2 1.2 %collective-permute-start.3 = (f32[56,128]{1,0:T(8,128)S(1)}, f32[56,128]{1,0:T(8,128)S(1)}, u32[]{:S(2)}, u32[]{:S(2)}) collective-permute-start(f32[56,128]{1,0:T(8,128)S(1)} %get-tuple-element.57), channel_id=1, source_target_pairs={{0,4},{4,0},{8,12},{12,8},{16,20},{20,16},{24,28},{28,24},{1,5},{5... | collective-permute-start | bytes 86024 | tf_op jit(solution)/shard_map/ppermute | solution.py:50
  18.4 4.8 %collective-permute-start.6 = (f32[56,128]{1,0:T(8,128)S(1)}, f32[56,128]{1,0:T(8,128)S(1)}, u32[]{:S(2)}, u32[]{:S(2)}) collective-permute-start(f32[56,128]{1,0:T(8,128)S(1)} %add.12), channel_id=1, source_target_pairs={{0,24},{4,28},{8,16},{12,20},{16,8},{20,12},{24,0},{28,4},{1,25},{... | collective-permute-start | bytes 86024 | tf_op jit(solution)/shard_map/ppermute | solution.py:50
  20.0 3.9 %collective-permute-start.5 = (f32[56,128]{1,0:T(8,128)S(1)}, f32[56,128]{1,0:T(8,128)S(1)}, u32[]{:S(2)}, u32[]{:S(2)}) collective-permute-start(f32[56,128]{1,0:T(8,128)S(1)} %add.12), channel_id=1, source_target_pairs={{0,16},{4,20},{8,24},{12,28},{16,0},{20,4},{24,8},{28,12},{1,17},{... | collective-permute-start | bytes 86024 | tf_op jit(solution)/shard_map/ppermute | solution.py:50
  20.5 3.9 %collective-permute-start.4 = (f32[56,128]{1,0:T(8,128)S(1)}, f32[56,128]{1,0:T(8,128)S(1)}, u32[]{:S(2)}, u32[]{:S(2)}) collective-permute-start(f32[56,128]{1,0:T(8,128)S(1)} %add.12), channel_id=1, source_target_pairs={{0,8},{4,12},{8,0},{12,4},{16,24},{20,28},{24,16},{28,20},{1,9},{5... | collective-permute-start | bytes 86024 | tf_op jit(solution)/shard_map/ppermute | solution.py:50
  24.4 5.9 %collective-permute-start.9 = (f32[56,128]{1,0:T(8,128)S(1)}, f32[56,128]{1,0:T(8,128)S(1)}, u32[]{:S(2)}, u32[]{:S(2)}) collective-permute-start(f32[56,128]{1,0:T(8,128)S(1)} %add_add_fusion.refs_0_), channel_id=1, source_target_pairs={{0,3},{1,2},{2,1},{3,0},{4,7},{5,6},{6,5},{7,4},{8,11},{9,10},{10,... | collective-permute-start | bytes 86024 | tf_op jit(solution)/shard_map/ppermute | solution.py:50
  27.3 4.8 %collective-permute-start.8 = (f32[56,128]{1,0:T(8,128)S(1)}, f32[56,128]{1,0:T(8,128)S(1)}, u32[]{:S(2)}, u32[]{:S(2)}) collective-permute-start(f32[56,128]{1,0:T(8,128)S(1)} %add_add_fusion.refs_0_), channel_id=1, source_target_pairs={{0,2},{1,3},{2,0},{3,1},{4,6},{5,7},{6,4},{7,5},{8,10},{9,11},{10,... | collective-permute-start | bytes 86024 | tf_op jit(solution)/shard_map/ppermute | solution.py:50
  27.3 4.8 %collective-permute-start.7 = (f32[56,128]{1,0:T(8,128)S(1)}, f32[56,128]{1,0:T(8,128)S(1)}, u32[]{:S(2)}, u32[]{:S(2)}) collective-permute-start(f32[56,128]{1,0:T(8,128)S(1)} %add_add_fusion.refs_0_), channel_id=1, source_target_pairs={{0,1},{1,0},{2,3},{3,2},{4,5},{5,4},{6,7},{7,6},{8,9},{9,8},{10,11... | collective-permute-start | bytes 86024 | tf_op jit(solution)/shard_map/ppermute | solution.py:50
  28.8 3.3 %copy-start.2 = (f32[400,16]{0,1:T(8,128)S(1)}, f32[400,16]{0,1:T(8,128)}, u32[]{:S(2)}) copy-start(f32[400,16]{0,1:T(8,128)} %param.19) | copy-start | bytes 76804

commit v2 on v1

--- a/solution.py
+++ b/solution.py
@@ -26,32 +26,61 @@
     return lax.ppermute(array, axis, [(i, (i + by) % count) for i in range(count)])
 
 
-def radices(count):
+def sent(array, flips):
+    n_src, n_dst = lax.axis_size("src"), lax.axis_size("dst")
+    pairs = []
+    for u in range(n_src):
+        for w in range(n_dst):
+            src_flip, dst_flip = flips[u % 2]
+            pairs.append((u * n_dst + w, (u ^ src_flip) * n_dst + (w ^ dst_flip)))
+    return lax.ppermute(array, ("src", "dst"), pairs)
+
+
+def core_swapped(array):
+    return sent(array, ((1, 0), (1, 0)))
+
+
+def digits(count, unit):
     steps = []
     while count > 1:
-        steps.append(4 if count % 4 == 0 else 2)
-        count //= steps[-1]
+        radix = 4 if count % 4 == 0 else 2
+        steps.append((radix, unit))
+        count, unit = count // radix, unit * radix
     return steps
 
 
 def exchanged_terms(array):
-    n_src, n_dst = lax.axis_size("src"), lax.axis_size("dst")
-    steps = [("src", 1, 2)]
-    for axis, count, stride in (("src", n_src // 2, 2), ("dst", n_dst, 1)):
-        for radix in radices(count):
-            steps.append((axis, stride, radix))
-            stride *= radix
-    terms = [array]
-    for axis, stride, radix in steps:
-        array = tree_sum(terms)
-        count = lax.axis_size(axis)
-        terms = [array]
-        for k in range(1, radix):
-            terms.append(lax.ppermute(array, axis, [(i, i ^ k * stride) for i in range(count)]))
-    return terms
+    steps = [(0, r, u) for r, u in digits(lax.axis_size("src") // 2, 2)]
+    steps += [(1, r, u) for r, u in digits(lax.axis_size("dst"), 1)]
+    terms = None
+    for axis, radix, unit in steps:
+
+        def flip(k):
+            return (0, k * unit) if axis else (k * unit, 0)
+
+        if terms is None:
+            one = sent(array, (flip(1), flip(1)))
+            array = array + core_swapped(array)
+            if radix == 4:
+                two = sent(array, (flip(2), flip(2)))
+                three = sent(array, (flip(3), flip(3)))
+                (late,) = call(add_kernel, [VMEM] * 2, [array.shape], 10**9, [two, three])
+                terms = ((array, one + core_swapped(one)), (late,))
+            else:
+                terms = ((array,), (one + core_swapped(one),))
+            continue
+        array = tree_sum([tree_sum(pair) for pair in terms])
+        if radix == 4:
+            odd = sent(array, (flip(1), flip(3)))
+            two = sent(array, (flip(2), flip(2)))
+            terms = ((array, two), (odd, core_swapped(odd)))
+        else:
+            terms = ((array,), (sent(array, (flip(1), flip(1))),))
+    return [term for pair in terms for term in pair]
 
 
 def tree_sum(terms):
+    terms = list(terms)
     while len(terms) > 1:
         terms = [a + b for a, b in zip(terms[::2], terms[1::2])]
     return terms[0]
@@ -118,12 +147,17 @@
     return NEG_WEIGHT * dot(as_bf16(onehot(negatives, rows)), ones, NN)
 
 
-def coefficients(query, table_rows, weight, at_target, valid):
-    scores = dot_split(table_rows, halves(query), NN)
-    positive = jnp.sum(jnp.where(at_target, scores, 0.0), axis=0, keepdims=True)
-    pos_grad = jnp.where(valid, -1.0 / (1.0 + jnp.exp(positive)), 0.0)
-    neg_grad = jnp.where(valid, weight / (1.0 + jnp.exp(-scores)), 0.0)
-    return neg_grad + jnp.where(at_target, pos_grad, 0.0)
+def coefficient_parts(round_id, columns, edge_rows, counts, negatives):
+    edges = edge_rows.shape[2]
+    weight = negative_weight(negatives[round_id : round_id + 1, :], columns, edges)
+    valid = lax.broadcasted_iota(jnp.int32, (1, edges), 1) < counts[:, round_id : round_id + 1]
+    hit = jnp.where(onehot(edge_rows[round_id, 1:2, :], columns), 1.0, 0.0)
+    scale = jnp.where(valid, 0.5 * (weight + hit), 0.0)
+    return scale, scale - jnp.where(valid, hit, 0.0)
+
+
+def coefficients(query, table_rows, scale, base):
+    return scale * jnp.tanh(0.5 * dot_split(table_rows, query, NN)) + base
 
 
 def row_step(table, state, gradient):
@@ -135,21 +169,9 @@
     return as_bf16(onehot(edge_rel[round_id : round_id + 1, :], rels))
 
 
-def edge_parts(round_id, rows_of_table, rel, edge_rows, edge_rel, counts, negatives):
-    edges = edge_rows.shape[2]
-    rel_hot = hot_relations(round_id, edge_rel, rel.shape[0])
-    src_hot = as_bf16(onehot(edge_rows[round_id, 0:1, :], rows_of_table))
-    at_target = onehot(edge_rows[round_id, 1:2, :], rows_of_table)
-    rel_cols = dot_left(halves(rel[...]), rel_hot, TN)
-    place = lax.broadcasted_iota(jnp.int32, (1, edges), 1)
-    valid = place < counts[:, round_id : round_id + 1]
-    weight = negative_weight(negatives[round_id : round_id + 1, :], rows_of_table, edges)
-    return src_hot, at_target, rel_cols, valid, weight
-
-
 def first_front_kernel(
     src_hbm, state_hbm, dst_hbm, rel_hbm, rows_hbm, rels_hbm, counts_hbm, negs_hbm,
-    moved_out, query_out, coef_out, product_out,
+    top_out, bottom_out, query_out, coef_out, product_out,
     src, src_state, dst, rel, rows, rels, counts, negs, sems,
 ):
     pairs = [
@@ -162,22 +184,24 @@
     for copy in copies[:5]:
         copy.wait()
     features, columns = src.shape
-    src_hot, at_target, rel_cols, valid, weight = edge_parts(
-        0, columns, rel, rows, rels, counts, negs
-    )
+    src_hot = as_bf16(onehot(rows[0, 0:1, :], columns))
+    rel_cols = dot_left(halves(rel[...]), hot_relations(0, rels, rel.shape[0]), TN)
+    scale, base = coefficient_parts(0, columns, rows, counts, negs)
     copies[5].wait()
     table_dst = halves(dst[...])
     table_rows = halves(dst[...].T)
     copies[6].wait()
     src_cols = dot_left(halves(src[...]), src_hot, NN)
     query = src_cols * rel_cols
-    coef = coefficients(query, table_rows, weight, at_target, valid)
+    coef = coefficients(halves(query), table_rows, scale, base)
     query_grad = dot_split(table_dst, halves(coef), NN)
     src_grad = dot_left(halves(query_grad * rel_cols), src_hot, NT)
     copies[7].wait()
     table, state = row_step(src[...], src_state[...], src_grad)
-    moved_out[0:features, :] = table
-    moved_out[features:, :] = jnp.broadcast_to(state, (moved_out.shape[0] - features, columns))
+    top, rest = top_out.shape[0], features - top_out.shape[0]
+    top_out[...] = table[0:top, :]
+    bottom_out[0:rest, :] = table[top:, :]
+    bottom_out[rest:, :] = jnp.broadcast_to(state, (bottom_out.shape[0] - rest, columns))
     query_out[...] = query
     coef_out[...] = coef
     product_out[...] = query_grad * src_cols
@@ -185,57 +209,55 @@
 
 def first_back_kernel(
     dst, dst_state, query, coef, product, rel, rows, rels, counts, negs,
-    spare_state, table_out, state_out, rel_first_out, rel_cols_out, weight_out, live_out, spare_out,
+    spare_state, table_out, state_out, rel_first_out, rel_cols_out, scale_out, base_out, spare_out,
 ):
     grad = dot_split(halves(query[...]), halves(coef[...]), NT)
     table_out[...], state_out[...] = row_step(dst[...], dst_state[...], grad)
-    edges, columns = rows.shape[2], dst.shape[1]
     rel_first_out[...] = dot_right(
         hot_relations(0, rels, rel.shape[0]), halves(product[...]), NT
     )
     rel_cols_out[...] = dot_left(halves(rel[...]), hot_relations(1, rels, rel.shape[0]), TN)
-    weight_out[...] = negative_weight(negs[1:2, :], columns, edges)
-    place = lax.broadcasted_iota(jnp.int32, (1, edges), 1)
-    live_out[...] = jnp.where(place < counts[:, 1:2], 1.0, 0.0)
+    scale_out[...], base_out[...] = coefficient_parts(1, dst.shape[1], rows, counts, negs)
     spare_out[...] = spare_state[...]
 
 
-def spare_kernel(spare, rows_high, rows_low, high, low):
-    rows_high[...], rows_low[...] = halves(spare[...].T)
-    high[...], low[...] = halves(spare[...])
+def second_gather_kernel(top, bottom, rel_cols, rows, src_cols_out, high_out, low_out):
+    half, features = top.shape[0], rel_cols.shape[0]
+    src_hot = as_bf16(onehot(rows[1, 0:1, :], top.shape[1]))
+    for low, high, values in ((0, half, top[...]), (half, features, bottom[0 : features - half, :])):
+        src_cols = dot_left(halves(values), src_hot, NN)
+        src_cols_out[low:high, :] = src_cols
+    high_out[...], low_out[...] = halves(src_cols_out[...] * rel_cols[...])
 
 
 def second_front_kernel(
-    moved, rows_high, rows_low, high, low, rel_cols, weight, live, rows, rels, rel_first,
-    state, query_out, coef_out, scaled_out, rel_out, state_out,
+    spare, src_cols, high, low, rel_cols, scale, base, rels, rel_first, state,
+    coef_out, scaled_out, rel_out, state_out,
 ):
-    features, columns = high.shape
     rel_hot = hot_relations(1, rels, rel_first.shape[0])
-    src_hot = as_bf16(onehot(rows[1, 0:1, :], columns))
-    at_target = onehot(rows[1, 1:2, :], columns)
-    valid = live[...] > 0.0
-    src_cols = dot_left(halves(moved[0:features, :]), src_hot, NN)
-    query = src_cols * rel_cols[...]
-    coef = coefficients(query, (rows_high[...], rows_low[...]), weight[...], at_target, valid)
-    query_grad = dot_split((high[...], low[...]), halves(coef), NN)
-    pack(rel_out, rel_first[...] + dot_right(rel_hot, halves(query_grad * src_cols), NT))
+    coef = coefficients((high[...], low[...]), halves(spare[...].T), scale[...], base[...])
+    query_grad = dot_split(halves(spare[...]), halves(coef), NN)
+    pack(rel_out, rel_first[...] + dot_right(rel_hot, halves(query_grad * src_cols[...]), NT))
     state_out[...] = state[...]
-    query_out[...] = query
     coef_out[...] = coef
     scaled_out[...] = query_grad * rel_cols[...]
 
 
 def second_back_kernel(
-    moved, spare, spare_state, rows, query, coef, scaled, src_out, src_acc, spare_out, spare_acc
+    top, bottom, spare, spare_state, rows, high, low, coef, scaled,
+    src_out, src_acc, spare_out, spare_acc,
 ):
-    features = spare.shape[0]
+    rest = spare.shape[0] - top.shape[0]
     src_hot = as_bf16(onehot(rows[1, 0:1, :], spare.shape[1]))
     src_grad = dot_left(halves(scaled[...]), src_hot, NT)
-    src_out[...], src_acc[...] = row_step(
-        moved[0:features, :], moved[features : features + 1, :], src_grad
-    )
-    spare_grad = dot_split(halves(query[...]), halves(coef[...]), NT)
+    moved = jnp.concatenate([top[...], bottom[0:rest, :]], axis=0)
+    src_out[...], src_acc[...] = row_step(moved, bottom[rest : rest + 1, :], src_grad)
+    spare_grad = dot_split((high[...], low[...]), halves(coef[...]), NT)
     spare_out[...], spare_acc[...] = row_step(spare[...], spare_state[...], spare_grad)
+
+
+def add_kernel(left, right, out):
+    out[...] = left[...] + right[...]
 
 
 def relation_kernel(rel, rel_state, *refs):
@@ -285,22 +307,26 @@
     operands = [
         src_table, src_state.reshape(1, rows), dst_table, rel, edge_rows, edge_rel, live, negatives,
     ]
-    moved_first, query, coef, product = call(
+    half = features // 16 * 8
+    top, bottom, query, coef, product = call(
         first_front_kernel,
         [HBM] * 8,
-        [(features + 8, rows), (features, edges), (rows, edges), (features, edges)],
+        [
+            (half, rows), (features - half + 8, rows), (features, edges), (rows, edges),
+            (features, edges),
+        ],
         400 * work,
         [pltpu.with_memory_space_constraint(a, pltpu.HBM) for a in operands],
         [pltpu.VMEM(a.shape, a.dtype) for a in operands]
         + [pltpu.SemaphoreType.DMA((len(operands),))],
     )
-    moved = passed_along(moved_first, "src", 1)
-    dst_next, dst_acc, rel_first, rel_cols, weight, valid, spare_acc = call(
+    top, bottom = passed_along((top, bottom), "src", 1)
+    dst_next, dst_acc, rel_first, rel_cols, scale, base, spare_acc = call(
         first_back_kernel,
         [VMEM] * 11,
         [
             (features, rows), (1, rows), (rels, features), (features, edges), (rows, edges),
-            (1, edges), (1, rows),
+            (rows, edges), (1, rows),
         ],
         3 * work,
         [
@@ -309,33 +335,29 @@
         ],
     )
     spare_acc_in = swapped(spare_acc, "dst", 0)
-    spare_parts = call(
-        spare_kernel,
-        [VMEM],
-        [jax.ShapeDtypeStruct((rows, features), BF16)] * 2
-        + [jax.ShapeDtypeStruct((features, rows), BF16)] * 2,
-        100 * work,
-        [spare_in],
-    )
-    query, coef, scaled, rel_both, spare_acc_in = call(
+    src_cols, high, low = call(
+        second_gather_kernel,
+        [VMEM] * 4,
+        [(features, edges)] + [jax.ShapeDtypeStruct((features, edges), BF16)] * 2,
+        2 * work,
+        [top, bottom, rel_cols, edge_rows],
+    )
+    coef, scaled, rel_both, spare_acc_in = call(
         second_front_kernel,
-        [VMEM] * 12,
+        [VMEM] * 10,
+        [(rows, edges), (features, edges), packed_shape(rels, features), (1, rows)],
+        10 * work,
         [
-            (features, edges), (rows, edges), (features, edges), packed_shape(rels, features),
-            (1, rows),
-        ],
-        12 * work,
-        [
-            moved, *spare_parts, rel_cols, weight, valid, edge_rows, edge_rel, rel_first,
+            spare_in, src_cols, high, low, rel_cols, scale, base, edge_rel, rel_first,
             spare_acc_in,
         ],
     )
     src_out, src_state_out, spare_out, spare_state_out = call(
         second_back_kernel,
-        [VMEM] * 7,
+        [VMEM] * 9,
         [(features, rows), (1, rows), (features, rows), (1, rows)],
         5 * work,
-        [moved, spare_in, spare_acc_in, edge_rows, query, coef, scaled],
+        [top, bottom, spare_in, spare_acc_in, edge_rows, high, low, coef, scaled],
     )
     terms = exchanged_terms(rel_both)
     relations_out, rel_state_out = call(

time: 33 us -> 30.7 us (0.930)
  waiting for transfers between devices: 11.5 us -> 9.5 us
  Pallas kernels: 8.77 us -> 8.33 us
    ppermute x2, waiting for transfers between devices: 4.14 us -> 0.01 us  [swapped(): lax.ppermute(array, axis, [(i, i ^ 1 << stride) for i in range(lax.axis_s...]
    ppermute x1 -> x2, waiting for transfers between devices: 1.83 us -> 4.23 us  [passed_along(): lax.ppermute(array, axis, [(i, (i + by) % count) for i in range(count)])]
    ppermute x7 -> x8, starting transfers between devices: 7.94 us -> 6.11 us  [sent(): return lax.ppermute(array, ('src', 'dst'), pairs)]
    ppermute x1 -> x2, starting transfers between devices: 0.06 us -> 1.64 us  [passed_along(): lax.ppermute(array, axis, [(i, (i + by) % count) for i in range(count)])]
    pallas_call x6 -> x7, Pallas kernels: 8.77 us -> 8.33 us  [call(): pl.pallas_call(kernel, in_specs=in_specs, out_specs=[VMEM] * len(outs), o...]
    ppermute x2, starting transfers between devices: 3.13 us -> 3.54 us  [swapped(): lax.ppermute(array, axis, [(i, i ^ 1 << stride) for i in range(lax.axis_s...]
    ppermute x7 -> x8, waiting for transfers between devices: 5.51 us -> 5.27 us  [sent(): return lax.ppermute(array, ('src', 'dst'), pairs)]
  transfers between devices with their start and end apart: 10 -> 12, of which waited for: 7 -> 7; matrix products, arithmetic and copies ran while one was open for 0% -> 0% of each run, Pallas kernels for 19% -> 21%
where the time goes in v2:
time: 30.7 us; the launch traced here: 30.6 us
  starting transfers between devices  11.3 us (37%)
  waiting for transfers between devices  9.5 us (31%)
  Pallas kernels  8.33 us (27%)
  between operations  0.75 us (2%)
  local copies, waits for them, and re-layouts  0.69 us (2%)
    pallas_call x7, Pallas kernels, call(): pl.pallas_call(kernel, in_specs=in_specs, out_specs=[VMEM] * len(outs), o...  8.33 us
    ppermute x8, starting transfers between devices, sent(): return lax.ppermute(array, ('src', 'dst'), pairs)  6.11 us
    ppermute x8, waiting for transfers between devices, sent(): return lax.ppermute(array, ('src', 'dst'), pairs)  5.27 us
    ppermute x2, waiting for transfers between devices, passed_along(): lax.ppermute(array, axis, [(i, (i + by) % count) for i in range(count)])  4.23 us
    ppermute x2, starting transfers between devices, swapped(): lax.ppermute(array, axis, [(i, i ^ 1 << stride) for i in range(lax.axis_s...  3.54 us
    ppermute x2, starting transfers between devices, passed_along(): lax.ppermute(array, axis, [(i, (i + by) % count) for i in range(count)])  1.64 us
    unnamed x18, local copies, waits for them, and re-layouts  0.69 us
  transfers between devices with their start and end apart: 12, of which 7 were waited for; matrix products, arithmetic and copies ran while one was open for 0% of the time, Pallas kernels for 21%

profile of v2, /device:TPU:0, one launch (start us, length us, event | category | flops | bytes accessed | tf_op | source)
XLA Modules:
  0.0 30.6 jit_solution(3821196879415165025)
XLA Ops:
  0.6 3.1 %collective-permute-start.2 = (f32[400,256]{1,0:T(8,128)}, f32[400,256]{1,0:T(8,128)S(1)}, u32[]{:S(2)}, u32[]{:S(2)}) collective-permute-start(f32[400,256]{1,0:T(8,128)} %param.16), channel_id=1, source_target_pairs={{0,1},{1,0},{2,3},{3,2},{4,5},{5,4},{6,7},{7,6},{8,9},{9,8},{10,11... | collective-permute-start | bytes 1228808 | tf_op jit(solution)/shard_map/ppermute | solution.py:21
  3.7 3.3 %shard_map.179 = (f32[200,256]{1,0:T(8,128)S(1)}, f32[208,256]{1,0:T(8,128)S(1)}, f32[400,256]{1,0:T(8,128)S(1)}, f32[256,256]{1,0:T(8,128)S(1)}, f32[400,256]{1,0:T(8,128)S(1)}) custom-call(f32[400,256]{1,0:T(8,128)} %src_hbm.1, f32[1,256]{1,0:T(1,128)} %bitcast.21, f32[400,256]{1,0:T(8,128)} %dst.1, f32[16,400]{1,0:T(8,128)} %bitcast.11, ...), custom_call_target="tpu_custom_call" | custom-call | flops 20971520000 | bytes 856072 | tf_op jit(solution)/shard_map/pallas_call | solution.py:273
  7.0 0.1 collective-permute-start.1
  7.1 1.6 %collective-permute-start = (f32[200,256]{1,0:T(8,128)S(1)}, f32[200,256]{1,0:T(8,128)S(1)}, u32[]{:S(2)}, u32[]{:S(2)}) collective-permute-start(f32[200,256]{1,0:T(8,128)S(1)} %get-tuple-element.33), channel_id=1, source_target_pairs={{0,4},{4,8},{8,12},{12,16},{16,20},{20,24},{24,28},{28,0},{1,5},{5... | collective-permute-start | bytes 614408 | tf_op jit(solution)/shard_map/ppermute | solution.py:26
  8.7 0.6 %copy-done.2 = s32[2,2,256]{2,1,0:T(2,128)S(1)} copy-done((s32[2,2,256]{2,1,0:T(2,128)S(1)}, s32[2,2,256]{2,1,0:T(2,128)}, u32[]{:S(2)}) %copy-start.2) | copy-done | bytes 4120
  9.4 0.0 copy-done.6
  9.4 1.4 %shard_map.180 = (f32[400,256]{1,0:T(8,128)}, f32[1,256]{1,0:T(1,128)}, f32[16,400]{1,0:T(8,128)S(1)}, f32[400,256]{1,0:T(8,128)S(1)}, f32[256,256]{1,0:T(8,128)...) custom-call(f32[400,256]{1,0:T(8,128)S(1)} %copy-done, f32[1,256]{1,0:T(1,128)S(1)} %bitcast.15, ...), custom_call_target="tpu_custom_call" | custom-call | flops 157286400 | bytes 1528840 | tf_op jit(solution)/shard_map/pallas_call | solution.py:273
  10.8 0.4 %collective-permute-start.3 = (f32[1,256]{1,0:T(1,128)S(1)}, f32[1,256]{1,0:T(1,128)S(1)}, u32[]{:S(2)}, u32[]{:S(2)}) collective-permute-start(f32[1,256]{1,0:T(1,128)S(1)} %get-tuple-element.45), channel_id=1, source_target_pairs={{0,1},{1,0},{2,3},{3,2},{4,5},{5,4},{6,7},{7,6},{8,9},{9,8},{10,11... | collective-permute-start | bytes 3080 | tf_op jit(solution)/shard_map/ppermute | solution.py:21
  11.2 4.2 %collective-permute-done.top = f32[200,256]{1,0:T(8,128)S(1)} collective-permute-done((f32[200,256]{1,0:T(8,128)S(1)}, f32[200,256]{1,0:T(8,128)S(1)}, u32[]{:S(2)}, u32[]{:S(2)}) %collective-permute-start) | collective-permute-done | bytes 204832 | tf_op jit(solution)/shard_map/ppermute | solution.py:26
  15.4 0.3 shard_map.181
  15.8 1.3 %shard_map.182 = (f32[256,256]{1,0:T(8,128)S(1)}, f32[400,256]{1,0:T(8,128)S(1)}, f32[56,128]{1,0:T(8,128)S(1)}, f32[1,256]{1,0:T(1,128)S(1)}) custom-call(f32[400,256]{1,0:T(8,128)S(1)} %collective-permute-done.2.spare, f32[400,256]{1,0:T(8,128)S(1)} %get-tuple-element.39.src_cols, bf16[400,256]{1,0:T(8,128)(2,1)S(1)} %get-tuple-element.40.high, ...), custom_call_target="tpu_custom_call" | custom-call | flops 524288000 | bytes 2600960 | tf_op jit(solution)/shard_map/pallas_call | solution.py:273
  17.0 0.6 %collective-permute-start.5 = (f32[56,128]{1,0:T(8,128)S(1)}, f32[56,128]{1,0:T(8,128)S(1)}, u32[]{:S(2)}, u32[]{:S(2)}) collective-permute-start(f32[56,128]{1,0:T(8,128)S(1)} %get-tuple-element.55), channel_id=1, source_target_pairs={{0,8},{1,9},{2,10},{3,11},{4,12},{5,13},{6,14},{7,15},{8,0},{9,1},... | collective-permute-start | bytes 86024 | tf_op jit(solution)/shard_map/ppermute | solution.py:36
  17.7 0.6 %collective-permute-done.4 = f32[56,128]{1,0:T(8,128)S(1)} collective-permute-done((f32[56,128]{1,0:T(8,128)S(1)}, f32[56,128]{1,0:T(8,128)S(1)}, u32[]{:S(2)}, u32[]{:S(2)}) %collective-permute-start.4) | collective-permute-done | bytes 28704 | tf_op jit(solution)/shard_map/ppermute | solution.py:36
  18.3 1.9 %collective-permute-start.8 = (f32[56,128]{1,0:T(8,128)S(1)}, f32[56,128]{1,0:T(8,128)S(1)}, u32[]{:S(2)}, u32[]{:S(2)}) collective-permute-start(f32[56,128]{1,0:T(8,128)S(1)} %add.12), channel_id=1, source_target_pairs={{0,24},{1,25},{2,26},{3,27},{4,28},{5,29},{6,30},{7,31},{8,16},{9,... | collective-permute-start | bytes 86024 | tf_op jit(solution)/shard_map/ppermute | solution.py:36
  20.1 0.5 %collective-permute-start.7 = (f32[56,128]{1,0:T(8,128)S(1)}, f32[56,128]{1,0:T(8,128)S(1)}, u32[]{:S(2)}, u32[]{:S(2)}) collective-permute-start(f32[56,128]{1,0:T(8,128)S(1)} %add.12), channel_id=1, source_target_pairs={{0,16},{1,17},{2,18},{3,19},{4,20},{5,21},{6,22},{7,23},{8,24},{9,... | collective-permute-start | bytes 86024 | tf_op jit(solution)/shard_map/ppermute | solution.py:36
  20.6 0.3 collective-permute-done.5
  20.9 2.2 %collective-permute-done.8.right = f32[56,128]{1,0:T(8,128)S(1)} collective-permute-done((f32[56,128]{1,0:T(8,128)S(1)}, f32[56,128]{1,0:T(8,128)S(1)}, u32[]{:S(2)}, u32[]{:S(2)}) %collective-permute-start.8) | collective-permute-done | bytes 28704 | tf_op jit(solution)/shard_map/ppermute | solution.py:36
  23.1 0.8 %collective-permute-done.7.left = f32[56,128]{1,0:T(8,128)S(1)} collective-permute-done((f32[56,128]{1,0:T(8,128)S(1)}, f32[56,128]{1,0:T(8,128)S(1)}, u32[]{:S(2)}, u32[]{:S(2)}) %collective-permute-start.7) | collective-permute-done | bytes 28704 | tf_op jit(solution)/shard_map/ppermute | solution.py:36
  24.0 0.5 %collective-permute-start.10 = (f32[56,128]{1,0:T(8,128)S(1)}, f32[56,128]{1,0:T(8,128)S(1)}, u32[]{:S(2)}, u32[]{:S(2)}) collective-permute-start(f32[56,128]{1,0:T(8,128)S(1)} %add_add_fusion.refs_0_), channel_id=1, source_target_pairs={{0,1},{1,0},{2,3},{3,2},{4,7},{5,6},{6,5},{7,4},{8,9},{9,8},{10,11... | collective-permute-start | bytes 86024 | tf_op jit(solution)/shard_map/ppermute | solution.py:36
  24.5 2.6 %collective-permute-start.9 = (f32[56,128]{1,0:T(8,128)S(1)}, f32[56,128]{1,0:T(8,128)S(1)}, u32[]{:S(2)}, u32[]{:S(2)}) collective-permute-start(f32[56,128]{1,0:T(8,128)S(1)} %add_add_fusion.refs_0_), channel_id=1, source_target_pairs={{0,2},{1,3},{2,0},{3,1},{4,6},{5,7},{6,4},{7,5},{8,10},{9,11},{10,... | collective-permute-start | bytes 86024 | tf_op jit(solution)/shard_map/ppermute | solution.py:36
  27.1 1.1 %collective-permute-done.10.refs_2_ = f32[56,128]{1,0:T(8,128)S(1)} collective-permute-done((f32[56,128]{1,0:T(8,128)S(1)}, f32[56,128]{1,0:T(8,128)S(1)}, u32[]{:S(2)}, u32[]{:S(2)}) %collective-permute-start.10) | collective-permute-done | bytes 28704 | tf_op jit(solution)/shard_map/ppermute | solution.py:36
  28.3 1.4 %shard_map.183 = (f32[400,256]{1,0:T(8,128)}, f32[1,256]{1,0:T(1,128)}, f32[400,256]{1,0:T(8,128)}, f32[1,256]{1,0:T(1,128)}) custom-call(f32[200,256]{1,0:T(8,128)S(1)} %collective-permute-done.top, f32[208,256]{1,0:T(8,128)S(1)} %collective-permute-done.1.bottom, f32[400,256]{1,0:T(8,128)S(1)} %collective-permute-done.2.spare, ...), custom_call_target="tpu_custom_call" | custom-call | flops 262144000 | bytes 2323456 | tf_op jit(solution)/shard_map/pallas_call | solution.py:273
  29.7 0.2 collective-permute-done.9.refs_1_
  29.9 0.7 %shard_map.185 = (f32[16,400]{1,0:T(8,128)}, f32[16,400]{1,0:T(8,128)}) custom-call(f32[16,400]{1,0:T(8,128)S(1)} %bitcast.13, f32[16,400]{1,0:T(8,128)S(1)} %bitcast.14, f32[56,128]{1,0:T(8,128)S(1)} %add_add_fusion.refs_0_, f32[56,128]{1,0:T(8,128)S(1)} %collective-permute-done.9.refs_1_, f32[56,128]{1,0:T(8,128)S(1)} %collective-permute-done.10.refs_2_, ...), custom_call_target="tpu_custom_call" | custom-call | flops 6400 | bytes 165888 | tf_op jit(solution)/shard_map/pallas_call | solution.py:273
  (27 shorter events, 0.1 us)
Async XLA Ops:
  0.6 15.1 %collective-permute-start.2 = (f32[400,256]{1,0:T(8,128)}, f32[400,256]{1,0:T(8,128)S(1)}, u32[]{:S(2)}, u32[]{:S(2)}) collective-permute-start(f32[400,256]{1,0:T(8,128)} %param.16), channel_id=1, source_target_pairs={{0,1},{1,0},{2,3},{3,2},{4,5},{5,4},{6,7},{7,6},{8,9},{9,8},{10,11... | collective-permute-start | bytes 1228808 | tf_op jit(solution)/shard_map/ppermute | solution.py:21
  3.7 5.0 %copy-start = (f32[400,256]{1,0:T(8,128)S(1)}, f32[400,256]{1,0:T(8,128)}, u32[]{:S(2)}) copy-start(f32[400,256]{1,0:T(8,128)} %dst.1) | copy-start | bytes 1228804
  3.7 5.0 %copy-start.1 = (f32[400,16]{0,1:T(8,128)S(1)}, f32[400,16]{0,1:T(8,128)}, u32[]{:S(2)}) copy-start(f32[400,16]{0,1:T(8,128)} %param.18) | copy-start | bytes 76804
  3.7 5.0 %copy-start.7 = (f32[256]{0:T(256)S(1)}, f32[256]{0:T(256)}, u32[]{:S(2)}) copy-start(f32[256]{0:T(256)} %param.17) | copy-start | bytes 3076
  3.7 5.0 %copy-start.8 = (s32[2,1]{0,1:T(1,128)S(1)}, s32[2,1]{0,1:T(1,128)}, u32[]{:S(2)}) copy-start(s32[2,1]{0,1:T(1,128)} %param.22) | copy-start | bytes 28
  7.0 8.4 %collective-permute-start.1 = (f32[208,256]{1,0:T(8,128)S(1)}, f32[208,256]{1,0:T(8,128)S(1)}, u32[]{:S(2)}, u32[]{:S(2)}) collective-permute-start(f32[208,256]{1,0:T(8,128)S(1)} %get-tuple-element.34), channel_id=1, source_target_pairs={{0,4},{4,8},{8,12},{12,16},{16,20},{20,24},{24,28},{28,0},{1,5},{5... | collective-permute-start | bytes 638984 | tf_op jit(solution)/shard_map/ppermute | solution.py:26
  7.1 1.6 %copy-start.5 = (s32[2,512]{1,0:T(2,128)S(1)}, s32[2,512]{1,0:T(2,128)}, u32[]{:S(2)}) copy-start(s32[2,512]{1,0:T(2,128)} %negs.1) | copy-start | bytes 12292
  7.1 8.3 %collective-permute-start = (f32[200,256]{1,0:T(8,128)S(1)}, f32[200,256]{1,0:T(8,128)S(1)}, u32[]{:S(2)}, u32[]{:S(2)}) collective-permute-start(f32[200,256]{1,0:T(8,128)S(1)} %get-tuple-element.33), channel_id=1, source_target_pairs={{0,4},{4,8},{8,12},{12,16},{16,20},{20,24},{24,28},{28,0},{1,5},{5... | collective-permute-start | bytes 614408 | tf_op jit(solution)/shard_map/ppermute | solution.py:26
  8.7 0.7 %copy-start.2 = (s32[2,2,256]{2,1,0:T(2,128)S(1)}, s32[2,2,256]{2,1,0:T(2,128)}, u32[]{:S(2)}) copy-start(s32[2,2,256]{2,1,0:T(2,128)} %rows.5) | copy-start | bytes 12292
  8.7 0.7 %copy-start.4 = (s32[2,256]{1,0:T(2,128)S(1)}, s32[2,256]{1,0:T(2,128)}, u32[]{:S(2)}) copy-start(s32[2,256]{1,0:T(2,128)} %rels.3) | copy-start | bytes 6148
  8.7 0.7 %copy-start.6 = (f32[256]{0:T(256)S(1)}, f32[256]{0:T(256)}, u32[]{:S(2)}) copy-start(f32[256]{0:T(256)} %param.15) | copy-start | bytes 3076
  10.8 5.0 %collective-permute-start.3 = (f32[1,256]{1,0:T(1,128)S(1)}, f32[1,256]{1,0:T(1,128)S(1)}, u32[]{:S(2)}, u32[]{:S(2)}) collective-permute-start(f32[1,256]{1,0:T(1,128)S(1)} %get-tuple-element.45), channel_id=1, source_target_pairs={{0,1},{1,0},{2,3},{3,2},{4,5},{5,4},{6,7},{7,6},{8,9},{9,8},{10,11... | collective-permute-start | bytes 3080 | tf_op jit(solution)/shard_map/ppermute | solution.py:21
  17.0 1.2 %collective-permute-start.4 = (f32[56,128]{1,0:T(8,128)S(1)}, f32[56,128]{1,0:T(8,128)S(1)}, u32[]{:S(2)}, u32[]{:S(2)}) collective-permute-start(f32[56,128]{1,0:T(8,128)S(1)} %get-tuple-element.55), channel_id=1, source_target_pairs={{0,4},{1,5},{2,6},{3,7},{4,0},{5,1},{6,2},{7,3},{8,12},{9,13},{10,... | collective-permute-start | bytes 86024 | tf_op jit(solution)/shard_map/ppermute | solution.py:36
  17.0 3.9 %collective-permute-start.5 = (f32[56,128]{1,0:T(8,128)S(1)}, f32[56,128]{1,0:T(8,128)S(1)}, u32[]{:S(2)}, u32[]{:S(2)}) collective-permute-start(f32[56,128]{1,0:T(8,128)S(1)} %get-tuple-element.55), channel_id=1, source_target_pairs={{0,8},{1,9},{2,10},{3,11},{4,12},{5,13},{6,14},{7,15},{8,0},{9,1},... | collective-permute-start | bytes 86024 | tf_op jit(solution)/shard_map/ppermute | solution.py:36
  18.3 4.9 %collective-permute-start.8 = (f32[56,128]{1,0:T(8,128)S(1)}, f32[56,128]{1,0:T(8,128)S(1)}, u32[]{:S(2)}, u32[]{:S(2)}) collective-permute-start(f32[56,128]{1,0:T(8,128)S(1)} %add.12), channel_id=1, source_target_pairs={{0,24},{1,25},{2,26},{3,27},{4,28},{5,29},{6,30},{7,31},{8,16},{9,... | collective-permute-start | bytes 86024 | tf_op jit(solution)/shard_map/ppermute | solution.py:36
  20.1 3.9 %collective-permute-start.7 = (f32[56,128]{1,0:T(8,128)S(1)}, f32[56,128]{1,0:T(8,128)S(1)}, u32[]{:S(2)}, u32[]{:S(2)}) collective-permute-start(f32[56,128]{1,0:T(8,128)S(1)} %add.12), channel_id=1, source_target_pairs={{0,16},{1,17},{2,18},{3,19},{4,20},{5,21},{6,22},{7,23},{8,24},{9,... | collective-permute-start | bytes 86024 | tf_op jit(solution)/shard_map/ppermute | solution.py:36
  20.9 3.1 %collective-permute-start.6 = (f32[56,128]{1,0:T(8,128)S(1)}, f32[56,128]{1,0:T(8,128)S(1)}, u32[]{:S(2)}, u32[]{:S(2)}) collective-permute-start(f32[56,128]{1,0:T(8,128)S(1)} %collective-permute-done.5), channel_id=1, source_target_pairs={{0,4},{1,5},{2,6},{3,7},{4,0},{5,1},{6,2},{7,3},{8,12},{9,13},{10,... | collective-permute-start | bytes 86024 | tf_op jit(solution)/shard_map/ppermute | solution.py:36
  24.0 4.2 %collective-permute-start.10 = (f32[56,128]{1,0:T(8,128)S(1)}, f32[56,128]{1,0:T(8,128)S(1)}, u32[]{:S(2)}, u32[]{:S(2)}) collective-permute-start(f32[56,128]{1,0:T(8,128)S(1)} %add_add_fusion.refs_0_), channel_id=1, source_target_pairs={{0,1},{1,0},{2,3},{3,2},{4,7},{5,6},{6,5},{7,4},{8,9},{9,8},{10,11... | collective-permute-start | bytes 86024 | tf_op jit(solution)/shard_map/ppermute | solution.py:36
  24.5 5.3 %collective-permute-start.9 = (f32[56,128]{1,0:T(8,128)S(1)}, f32[56,128]{1,0:T(8,128)S(1)}, u32[]{:S(2)}, u32[]{:S(2)}) collective-permute-start(f32[56,128]{1,0:T(8,128)S(1)} %add_add_fusion.refs_0_), channel_id=1, source_target_pairs={{0,2},{1,3},{2,0},{3,1},{4,6},{5,7},{6,4},{7,5},{8,10},{9,11},{10,... | collective-permute-start | bytes 86024 | tf_op jit(solution)/shard_map/ppermute | solution.py:36
  28.2 1.6 %collective-permute-start.11 = (f32[56,128]{1,0:T(8,128)S(1)}, f32[56,128]{1,0:T(8,128)S(1)}, u32[]{:S(2)}, u32[]{:S(2)}) collective-permute-start(f32[56,128]{1,0:T(8,128)S(1)} %collective-permute-done.10.refs_2_), channel_id=1, source_target_pairs={{0,4},{1,5},{2,6},{3,7},{4,0},{5,1},{6,2},{7,3},{8,12},{9,13},{10,... | collective-permute-start | bytes 86024 | tf_op jit(solution)/shard_map/ppermute | solution.py:36
  28.3 1.6 %copy-start.3 = (f32[400,16]{0,1:T(8,128)S(1)}, f32[400,16]{0,1:T(8,128)}, u32[]{:S(2)}) copy-start(f32[400,16]{0,1:T(8,128)} %param.19) | copy-start | bytes 76804

commit v3 on v2

--- a/solution.py
+++ b/solution.py
@@ -1,3 +1,5 @@
+import functools
+
 import jax
 import jax.numpy as jnp
 from jax import lax
@@ -122,16 +124,27 @@
     return lax.dot_general(a, b, dims, preferred_element_type=F32)
 
 
+def stacked(parts, dims, side):
+    return jnp.concatenate(parts, axis=dims[0][side][0])
+
+
 def dot_split(a, b, dims):
-    return dot(a[0], b[0], dims) + dot(a[0], b[1], dims) + dot(a[1], b[0], dims)
+    if a[0].shape[dims[0][0][0]] % 128:
+        return dot(a[0], b[0], dims) + dot(a[0], b[1], dims) + dot(a[1], b[0], dims)
+    left = stacked((a[0], a[0], a[1]), dims, 0)
+    return dot(left, stacked((b[0], b[1], b[0]), dims, 1), dims)
 
 
 def dot_left(a, b, dims):
-    return dot(a[0], b, dims) + dot(a[1], b, dims)
+    if a[0].shape[dims[0][0][0]] % 128:
+        return dot(a[0], b, dims) + dot(a[1], b, dims)
+    return dot(stacked(a, dims, 0), stacked((b, b), dims, 1), dims)
 
 
 def dot_right(a, b, dims):
-    return dot(a, b[0], dims) + dot(a, b[1], dims)
+    if b[0].shape[dims[0][1][0]] % 128:
+        return dot(a, b[0], dims) + dot(a, b[1], dims)
+    return dot(stacked((a, a), dims, 0), stacked(b, dims, 1), dims)
 
 
 def onehot(index, length):
@@ -169,39 +182,61 @@
     return as_bf16(onehot(edge_rel[round_id : round_id + 1, :], rels))
 
 
-def first_front_kernel(
-    src_hbm, state_hbm, dst_hbm, rel_hbm, rows_hbm, rels_hbm, counts_hbm, negs_hbm,
-    top_out, bottom_out, query_out, coef_out, product_out,
-    src, src_state, dst, rel, rows, rels, counts, negs, sems,
+def core_of_chip():
+    return lax.rem(lax.axis_index("src"), 2)
+
+
+def first_front_kernel(core, *refs):
+    given, refs = (refs[:3], refs[3:]) if core == 0 else ((), refs)
+
+    @pl.when(core_of_chip() == core)
+    def _():
+        first_front(*refs)
+
+    if given:
+
+        @pl.when(core_of_chip() != core)
+        def _():
+            for value, out in zip(given, refs[-12:-9]):
+                out[...] = value[...]
+
+
+def first_front(
+    src_hbm, state_hbm, dst_hbm, rel_hbm, rows_hbm, rels_hbm, counts_hbm, negs_hbm, *refs
 ):
-    pairs = [
-        (rows_hbm, rows), (rels_hbm, rels), (rel_hbm, rel), (counts_hbm, counts),
-        (negs_hbm, negs), (dst_hbm, dst), (src_hbm, src), (state_hbm, src_state),
+    *moved_outs, query_out, coef_out, product_out = refs[:-9]
+    src, src_state, dst, rel, rows, rels, counts, negs, sems = refs[-9:]
+    features, columns = src.shape
+    small = [
+        (rows_hbm, rows), (rels_hbm, rels), (rel_hbm, rel), (counts_hbm, counts), (negs_hbm, negs),
     ]
+    slabs = [(dst_hbm, dst), (src_hbm, src)]
+    pairs = small + slabs + [(state_hbm, src_state)]
     copies = [pltpu.make_async_copy(a, b, sems.at[i]) for i, (a, b) in enumerate(pairs)]
     for copy in copies:
         copy.start()
-    for copy in copies[:5]:
+    for_dst, for_src, for_state = copies[len(small) :]
+    for copy in copies[: len(small)]:
         copy.wait()
-    features, columns = src.shape
     src_hot = as_bf16(onehot(rows[0, 0:1, :], columns))
     rel_cols = dot_left(halves(rel[...]), hot_relations(0, rels, rel.shape[0]), TN)
     scale, base = coefficient_parts(0, columns, rows, counts, negs)
-    copies[5].wait()
+    for_dst.wait()
     table_dst = halves(dst[...])
     table_rows = halves(dst[...].T)
-    copies[6].wait()
+    for_src.wait()
     src_cols = dot_left(halves(src[...]), src_hot, NN)
     query = src_cols * rel_cols
     coef = coefficients(halves(query), table_rows, scale, base)
     query_grad = dot_split(table_dst, halves(coef), NN)
     src_grad = dot_left(halves(query_grad * rel_cols), src_hot, NT)
-    copies[7].wait()
+    for_state.wait()
     table, state = row_step(src[...], src_state[...], src_grad)
-    top, rest = top_out.shape[0], features - top_out.shape[0]
-    top_out[...] = table[0:top, :]
-    bottom_out[0:rest, :] = table[top:, :]
-    bottom_out[rest:, :] = jnp.broadcast_to(state, (bottom_out.shape[0] - rest, columns))
+    moved = jnp.concatenate([table, jnp.broadcast_to(state, (24, columns))], axis=0)
+    low = 0
+    for out in moved_outs:
+        out[...] = moved[low : low + out.shape[0], :]
+        low += out.shape[0]
     query_out[...] = query
     coef_out[...] = coef
     product_out[...] = query_grad * src_cols
@@ -221,13 +256,20 @@
     spare_out[...] = spare_state[...]
 
 
-def second_gather_kernel(top, bottom, rel_cols, rows, src_cols_out, high_out, low_out):
-    half, features = top.shape[0], rel_cols.shape[0]
-    src_hot = as_bf16(onehot(rows[1, 0:1, :], top.shape[1]))
-    for low, high, values in ((0, half, top[...]), (half, features, bottom[0 : features - half, :])):
-        src_cols = dot_left(halves(values), src_hot, NN)
-        src_cols_out[low:high, :] = src_cols
-    high_out[...], low_out[...] = halves(src_cols_out[...] * rel_cols[...])
+def second_gather_kernel(count, *refs):
+    across, within = refs[:count], refs[count:-6]
+    rel_cols, rows, moved_out, src_cols_out, high_out, low_out = refs[-6:]
+    moved = jnp.where(
+        core_of_chip() == 0,
+        jnp.concatenate([part[...] for part in across], axis=0)[0 : moved_out.shape[0], :],
+        jnp.concatenate([part[...] for part in within], axis=0)[0 : moved_out.shape[0], :],
+    )
+    features, columns = src_cols_out.shape[0], moved.shape[1]
+    src_hot = as_bf16(onehot(rows[1, 0:1, :], columns))
+    src_cols = dot_left(halves(moved[0:features, :]), src_hot, NN)
+    high_out[...], low_out[...] = halves(src_cols * rel_cols[...])
+    src_cols_out[...] = src_cols
+    moved_out[...] = moved
 
 
 def second_front_kernel(
@@ -244,14 +286,15 @@
 
 
 def second_back_kernel(
-    top, bottom, spare, spare_state, rows, high, low, coef, scaled,
+    moved, spare, spare_state, rows, high, low, coef, scaled,
     src_out, src_acc, spare_out, spare_acc,
 ):
-    rest = spare.shape[0] - top.shape[0]
+    features = spare.shape[0]
     src_hot = as_bf16(onehot(rows[1, 0:1, :], spare.shape[1]))
     src_grad = dot_left(halves(scaled[...]), src_hot, NT)
-    moved = jnp.concatenate([top[...], bottom[0:rest, :]], axis=0)
-    src_out[...], src_acc[...] = row_step(moved, bottom[rest : rest + 1, :], src_grad)
+    src_out[...], src_acc[...] = row_step(
+        moved[0:features, :], moved[features : features + 1, :], src_grad
+    )
     spare_grad = dot_split((high[...], low[...]), halves(coef[...]), NT)
     spare_out[...], spare_acc[...] = row_step(spare[...], spare_state[...], spare_grad)
 
@@ -281,6 +324,11 @@
             flops=flops, bytes_accessed=sum(a.size * 4 for a in args), transcendentals=0
         ),
     )(*args)
+
+
+def cut(length, parts):
+    step = -(-length // (8 * parts)) * 8
+    return [min(step, length - low) for low in range(0, length, step)]
 
 
 def per_device(
@@ -307,20 +355,25 @@
     operands = [
         src_table, src_state.reshape(1, rows), dst_table, rel, edge_rows, edge_rel, live, negatives,
     ]
-    half = features // 16 * 8
-    top, bottom, query, coef, product = call(
-        first_front_kernel,
-        [HBM] * 8,
-        [
-            (half, rows), (features - half + 8, rows), (features, edges), (rows, edges),
-            (features, edges),
-        ],
-        400 * work,
-        [pltpu.with_memory_space_constraint(a, pltpu.HBM) for a in operands],
-        [pltpu.VMEM(a.shape, a.dtype) for a in operands]
-        + [pltpu.SemaphoreType.DMA((len(operands),))],
-    )
-    top, bottom = passed_along((top, bottom), "src", 1)
+    hbm = [pltpu.with_memory_space_constraint(a, pltpu.HBM) for a in operands]
+
+    def first_on(core, pieces, cost, given=()):
+        return call(
+            functools.partial(first_front_kernel, core),
+            [VMEM] * len(given) + [HBM] * 8,
+            [(size, rows) for size in pieces] + [(features, edges), (rows, edges), (features, edges)],
+            cost,
+            [*given, *hbm],
+            [pltpu.VMEM(a.shape, a.dtype) for a in operands]
+            + [pltpu.SemaphoreType.DMA((len(operands),))],
+        )
+
+    *across, query, coef, product = first_on(1, cut(features + 24, 2), 400 * work)
+    across = passed_along(tuple(across), "src", 1)
+    *within, query, coef, product = first_on(
+        0, cut(features + 8, 2), 1 * work, (query, coef, product)
+    )
+    within = tuple(core_swapped(part) for part in within)
     dst_next, dst_acc, rel_first, rel_cols, scale, base, spare_acc = call(
         first_back_kernel,
         [VMEM] * 11,
@@ -335,12 +388,12 @@
         ],
     )
     spare_acc_in = swapped(spare_acc, "dst", 0)
-    src_cols, high, low = call(
-        second_gather_kernel,
-        [VMEM] * 4,
-        [(features, edges)] + [jax.ShapeDtypeStruct((features, edges), BF16)] * 2,
+    moved, src_cols, high, low = call(
+        functools.partial(second_gather_kernel, len(across)),
+        [VMEM] * (len(across) + len(within) + 2),
+        [(features + 8, rows), (features, edges)] + [jax.ShapeDtypeStruct((features, edges), BF16)] * 2,
         2 * work,
-        [top, bottom, rel_cols, edge_rows],
+        [*across, *within, rel_cols, edge_rows],
     )
     coef, scaled, rel_both, spare_acc_in = call(
         second_front_kernel,
@@ -354,10 +407,10 @@
     )
     src_out, src_state_out, spare_out, spare_state_out = call(
         second_back_kernel,
-        [VMEM] * 9,
+        [VMEM] * 8,
         [(features, rows), (1, rows), (features, rows), (1, rows)],
         5 * work,
-        [top, bottom, spare_in, spare_acc_in, edge_rows, high, low, coef, scaled],
+        [moved, spare_in, spare_acc_in, edge_rows, high, low, coef, scaled],
     )
     terms = exchanged_terms(rel_both)
     relations_out, rel_state_out = call(

time: 30.7 us -> 31.7 us (1.033)
  starting transfers between devices: 11.3 us -> 14 us
  waiting for transfers between devices: 9.5 us -> 7.6 us
    ppermute x2, waiting for transfers between devices: 4.23 us -> 1.62 us  [passed_along(): lax.ppermute(array, axis, [(i, (i + by) % count) for i in range(count)])]
    ppermute x8 -> x10, starting transfers between devices: 6.11 us -> 7.82 us  [sent(): return lax.ppermute(array, ('src', 'dst'), pairs)]
    ppermute x2, waiting for transfers between devices: 0.01 us -> 1.34 us  [swapped(): lax.ppermute(array, axis, [(i, i ^ 1 << stride) for i in range(lax.axis_s...]
    ppermute x2, starting transfers between devices: 1.64 us -> 2.8 us  [passed_along(): lax.ppermute(array, axis, [(i, (i + by) % count) for i in range(count)])]
    ppermute x8 -> x10, waiting for transfers between devices: 5.27 us -> 4.65 us  [sent(): return lax.ppermute(array, ('src', 'dst'), pairs)]
    pallas_call x7 -> x8, Pallas kernels: 8.33 us -> 8.39 us  [call(): pl.pallas_call(kernel, in_specs=in_specs, out_specs=[VMEM] * len(outs), o...]
  transfers between devices with their start and end apart: 12 -> 14, of which waited for: 7 -> 5; matrix products, arithmetic and copies ran while one was open for 0% -> 0% of each run, Pallas kernels for 21% -> 20%
where the time goes in v3:
time: 31.7 us; the launch traced here: 31.5 us
  starting transfers between devices  14 us (44%)
  Pallas kernels  8.39 us (26%)
  waiting for transfers between devices  7.6 us (24%)
  between operations  0.74 us (2%)
  local copies, waits for them, and re-layouts  0.68 us (2%)
    pallas_call x8, Pallas kernels, call(): pl.pallas_call(kernel, in_specs=in_specs, out_specs=[VMEM] * len(outs), o...  8.39 us
    ppermute x10, starting transfers between devices, sent(): return lax.ppermute(array, ('src', 'dst'), pairs)  7.82 us
    ppermute x10, waiting for transfers between devices, sent(): return lax.ppermute(array, ('src', 'dst'), pairs)  4.65 us
    ppermute x2, starting transfers between devices, swapped(): lax.ppermute(array, axis, [(i, i ^ 1 << stride) for i in range(lax.axis_s...  3.4 us
    ppermute x2, starting transfers between devices, passed_along(): lax.ppermute(array, axis, [(i, (i + by) % count) for i in range(count)])  2.8 us
    ppermute x2, waiting for transfers between devices, passed_along(): lax.ppermute(array, axis, [(i, (i + by) % count) for i in range(count)])  1.62 us
    ppermute x2, waiting for transfers between devices, swapped(): lax.ppermute(array, axis, [(i, i ^ 1 << stride) for i in range(lax.axis_s...  1.34 us
    unnamed x18, local copies, waits for them, and re-layouts  0.68 us
  transfers between devices with their start and end apart: 14, of which 5 were waited for; matrix products, arithmetic and copies ran while one was open for 0% of the time, Pallas kernels for 20%

profile of v3, /device:TPU:0, one launch (start us, length us, event | category | flops | bytes accessed | tf_op | source)
XLA Modules:
  0.0 31.5 jit_solution(5735198604034269497)
XLA Ops:
  0.6 3.1 %collective-permute-start.4 = (f32[400,256]{1,0:T(8,128)}, f32[400,256]{1,0:T(8,128)S(1)}, u32[]{:S(2)}, u32[]{:S(2)}) collective-permute-start(f32[400,256]{1,0:T(8,128)} %param.16), channel_id=1, source_target_pairs={{0,1},{1,0},{2,3},{3,2},{4,5},{5,4},{6,7},{7,6},{8,9},{9,8},{10,11... | collective-permute-start | bytes 1228808 | tf_op jit(solution)/shard_map/ppermute | solution.py:23
  3.7 0.1 shard_map.179
  3.8 2.7 %collective-permute-start = (f32[216,256]{1,0:T(8,128)S(1)}, f32[216,256]{1,0:T(8,128)S(1)}, u32[]{:S(2)}, u32[]{:S(2)}) collective-permute-start(f32[216,256]{1,0:T(8,128)S(1)} %get-tuple-element.39), channel_id=1, source_target_pairs={{0,4},{4,8},{8,12},{12,16},{16,20},{20,24},{24,28},{28,0},{1,5},{5... | collective-permute-start | bytes 663560 | tf_op jit(solution)/shard_map/ppermute | solution.py:28
  6.6 3.3 %shard_map.180 = (f32[208,256]{1,0:T(8,128)S(1)}, f32[200,256]{1,0:T(8,128)S(1)}, f32[400,256]{1,0:T(8,128)S(1)}, f32[256,256]{1,0:T(8,128)S(1)}, f32[400,256]{1,0:T(8,128)S(1)}) custom-call(f32[400,256]{1,0:T(8,128)S(1)} %get-tuple-element.41.refs_0_, f32[256,256]{1,0:T(8,128)S(1)} %get-tuple-element.42.refs_1_, f32[400,256]{1,0:T(8,128)S(1)} %get-tuple-element.43.refs_2_, ...), custom_call_target="tpu_custom_call" | custom-call | flops 52428800 | bytes 1937416 | tf_op jit(solution)/shard_map/pallas_call | solution.py:316
  9.9 0.1 collective-permute-start.2
  10.0 0.5 %collective-permute-start.3 = (f32[200,256]{1,0:T(8,128)S(1)}, f32[200,256]{1,0:T(8,128)S(1)}, u32[]{:S(2)}, u32[]{:S(2)}) collective-permute-start(f32[200,256]{1,0:T(8,128)S(1)} %get-tuple-element.45), channel_id=1, source_target_pairs={{0,4},{1,5},{2,6},{3,7},{4,0},{5,1},{6,2},{7,3},{8,12},{9,13},{10,... | collective-permute-start | bytes 614408 | tf_op jit(solution)/shard_map/ppermute | solution.py:38
  10.5 0.1 copy-done.5
  10.7 0.5 %copy-done.2 = s32[2,2,256]{2,1,0:T(2,128)S(1)} copy-done((s32[2,2,256]{2,1,0:T(2,128)S(1)}, s32[2,2,256]{2,1,0:T(2,128)}, u32[]{:S(2)}) %copy-start.2) | copy-done | bytes 4120
  11.2 1.4 %shard_map.181 = (f32[400,256]{1,0:T(8,128)}, f32[1,256]{1,0:T(1,128)}, f32[16,400]{1,0:T(8,128)S(1)}, f32[400,256]{1,0:T(8,128)S(1)}, f32[256,256]{1,0:T(8,128)...) custom-call(f32[400,256]{1,0:T(8,128)S(1)} %copy-done, f32[1,256]{1,0:T(1,128)S(1)} %bitcast.19, ...), custom_call_target="tpu_custom_call" | custom-call | flops 157286400 | bytes 1528840 | tf_op jit(solution)/shard_map/pallas_call | solution.py:316
  12.6 0.3 %collective-permute-start.5 = (f32[1,256]{1,0:T(1,128)S(1)}, f32[1,256]{1,0:T(1,128)S(1)}, u32[]{:S(2)}, u32[]{:S(2)}) collective-permute-start(f32[1,256]{1,0:T(1,128)S(1)} %get-tuple-element.57), channel_id=1, source_target_pairs={{0,1},{1,0},{2,3},{3,2},{4,5},{5,4},{6,7},{7,6},{8,9},{9,8},{10,11... | collective-permute-start | bytes 3080 | tf_op jit(solution)/shard_map/ppermute | solution.py:23
  12.9 1.6 %collective-permute-done.1.refs_1_ = f32[208,256]{1,0:T(8,128)S(1)} collective-permute-done((f32[208,256]{1,0:T(8,128)S(1)}, f32[208,256]{1,0:T(8,128)S(1)}, u32[]{:S(2)}, u32[]{:S(2)}) %collective-permute-start.1) | collective-permute-done | bytes 213024 | tf_op jit(solution)/shard_map/ppermute | solution.py:28
  14.5 0.3 shard_map.182
  14.8 1.3 %collective-permute-done.5.state = f32[1,256]{1,0:T(1,128)S(1)} collective-permute-done((f32[1,256]{1,0:T(1,128)S(1)}, f32[1,256]{1,0:T(1,128)S(1)}, u32[]{:S(2)}, u32[]{:S(2)}) %collective-permute-start.5) | collective-permute-done | bytes 1056 | tf_op jit(solution)/shard_map/ppermute | solution.py:23
  16.1 1.2 %shard_map.183 = (f32[256,256]{1,0:T(8,128)S(1)}, f32[400,256]{1,0:T(8,128)S(1)}, f32[56,128]{1,0:T(8,128)S(1)}, f32[1,256]{1,0:T(1,128)S(1)}) custom-call(f32[400,256]{1,0:T(8,128)S(1)} %collective-permute-done.4.spare, f32[400,256]{1,0:T(8,128)S(1)} %get-tuple-element.51.src_cols, bf16[400,256]{1,0:T(8,128)(2,1)S(1)} %get-tuple-element.52.high, ...), custom_call_target="tpu_custom_call" | custom-call | flops 524288000 | bytes 2600960 | tf_op jit(solution)/shard_map/pallas_call | solution.py:316
  17.4 1.6 %collective-permute-start.7 = (f32[56,128]{1,0:T(8,128)S(1)}, f32[56,128]{1,0:T(8,128)S(1)}, u32[]{:S(2)}, u32[]{:S(2)}) collective-permute-start(f32[56,128]{1,0:T(8,128)S(1)} %get-tuple-element.67), channel_id=1, source_target_pairs={{0,8},{1,9},{2,10},{3,11},{4,12},{5,13},{6,14},{7,15},{8,0},{9,1},... | collective-permute-start | bytes 86024 | tf_op jit(solution)/shard_map/ppermute | solution.py:38
  19.0 1.6 %collective-permute-start.9 = (f32[56,128]{1,0:T(8,128)S(1)}, f32[56,128]{1,0:T(8,128)S(1)}, u32[]{:S(2)}, u32[]{:S(2)}) collective-permute-start(f32[56,128]{1,0:T(8,128)S(1)} %add.12), channel_id=1, source_target_pairs={{0,16},{1,17},{2,18},{3,19},{4,20},{5,21},{6,22},{7,23},{8,24},{9,... | collective-permute-start | bytes 86024 | tf_op jit(solution)/shard_map/ppermute | solution.py:38
  20.6 1.0 %collective-permute-start.10 = (f32[56,128]{1,0:T(8,128)S(1)}, f32[56,128]{1,0:T(8,128)S(1)}, u32[]{:S(2)}, u32[]{:S(2)}) collective-permute-start(f32[56,128]{1,0:T(8,128)S(1)} %add.12), channel_id=1, source_target_pairs={{0,24},{1,25},{2,26},{3,27},{4,28},{5,29},{6,30},{7,31},{8,16},{9,... | collective-permute-start | bytes 86024 | tf_op jit(solution)/shard_map/ppermute | solution.py:38
  21.6 1.3 %collective-permute-done.9.left = f32[56,128]{1,0:T(8,128)S(1)} collective-permute-done((f32[56,128]{1,0:T(8,128)S(1)}, f32[56,128]{1,0:T(8,128)S(1)}, u32[]{:S(2)}, u32[]{:S(2)}) %collective-permute-start.9) | collective-permute-done | bytes 28704 | tf_op jit(solution)/shard_map/ppermute | solution.py:38
  22.9 2.4 %collective-permute-done.10.right = f32[56,128]{1,0:T(8,128)S(1)} collective-permute-done((f32[56,128]{1,0:T(8,128)S(1)}, f32[56,128]{1,0:T(8,128)S(1)}, u32[]{:S(2)}, u32[]{:S(2)}) %collective-permute-start.10) | collective-permute-done | bytes 28704 | tf_op jit(solution)/shard_map/ppermute | solution.py:38
  25.4 0.5 %collective-permute-start.12 = (f32[56,128]{1,0:T(8,128)S(1)}, f32[56,128]{1,0:T(8,128)S(1)}, u32[]{:S(2)}, u32[]{:S(2)}) collective-permute-start(f32[56,128]{1,0:T(8,128)S(1)} %add_add_fusion.refs_0_), channel_id=1, source_target_pairs={{0,1},{1,0},{2,3},{3,2},{4,7},{5,6},{6,5},{7,4},{8,9},{9,8},{10,11... | collective-permute-start | bytes 86024 | tf_op jit(solution)/shard_map/ppermute | solution.py:38
  25.9 2.6 %collective-permute-start.11 = (f32[56,128]{1,0:T(8,128)S(1)}, f32[56,128]{1,0:T(8,128)S(1)}, u32[]{:S(2)}, u32[]{:S(2)}) collective-permute-start(f32[56,128]{1,0:T(8,128)S(1)} %add_add_fusion.refs_0_), channel_id=1, source_target_pairs={{0,2},{1,3},{2,0},{3,1},{4,6},{5,7},{6,4},{7,5},{8,10},{9,11},{10,... | collective-permute-start | bytes 86024 | tf_op jit(solution)/shard_map/ppermute | solution.py:38
  28.5 0.8 %collective-permute-done.12.refs_2_ = f32[56,128]{1,0:T(8,128)S(1)} collective-permute-done((f32[56,128]{1,0:T(8,128)S(1)}, f32[56,128]{1,0:T(8,128)S(1)}, u32[]{:S(2)}, u32[]{:S(2)}) %collective-permute-start.12) | collective-permute-done | bytes 28704 | tf_op jit(solution)/shard_map/ppermute | solution.py:38
  29.3 1.4 %shard_map.184 = (f32[400,256]{1,0:T(8,128)}, f32[1,256]{1,0:T(1,128)}, f32[400,256]{1,0:T(8,128)}, f32[1,256]{1,0:T(1,128)}) custom-call(f32[408,256]{1,0:T(8,128)S(1)} %get-tuple-element.50.moved, f32[400,256]{1,0:T(8,128)S(1)} %collective-permute-done.4.spare, f32[1,256]{1,0:T(1,128)S(1)} %get-tuple-element.58.spare_state, s32[2,2,256]{2,1,0:T(2,128)S(1)} %copy-done.2, ...), custom_call_target="tpu_custom_call" | custom-call | flops 262144000 | bytes 2323456 | tf_op jit(solution)/shard_map/pallas_call | solution.py:316
  30.8 0.7 %shard_map.186 = (f32[16,400]{1,0:T(8,128)}, f32[16,400]{1,0:T(8,128)}) custom-call(f32[16,400]{1,0:T(8,128)S(1)} %bitcast.14, f32[16,400]{1,0:T(8,128)S(1)} %bitcast.15, f32[56,128]{1,0:T(8,128)S(1)} %add_add_fusion.refs_0_, f32[56,128]{1,0:T(8,128)S(1)} %collective-permute-done.11.refs_1_, f32[56,128]{1,0:T(8,128)S(1)} %collective-permute-done.12.refs_2_, ...), custom_call_target="tpu_custom_call" | custom-call | flops 6400 | bytes 165888 | tf_op jit(solution)/shard_map/pallas_call | solution.py:316
  (32 shorter events, 0.2 us)
Async XLA Ops:
  0.6 15.5 %collective-permute-start.4 = (f32[400,256]{1,0:T(8,128)}, f32[400,256]{1,0:T(8,128)S(1)}, u32[]{:S(2)}, u32[]{:S(2)}) collective-permute-start(f32[400,256]{1,0:T(8,128)} %param.16), channel_id=1, source_target_pairs={{0,1},{1,0},{2,3},{3,2},{4,5},{5,4},{6,7},{7,6},{8,9},{9,8},{10,11... | collective-permute-start | bytes 1228808 | tf_op jit(solution)/shard_map/ppermute | solution.py:23
  3.8 10.7 %collective-permute-start = (f32[216,256]{1,0:T(8,128)S(1)}, f32[216,256]{1,0:T(8,128)S(1)}, u32[]{:S(2)}, u32[]{:S(2)}) collective-permute-start(f32[216,256]{1,0:T(8,128)S(1)} %get-tuple-element.39), channel_id=1, source_target_pairs={{0,4},{4,8},{8,12},{12,16},{16,20},{20,24},{24,28},{28,0},{1,5},{5... | collective-permute-start | bytes 663560 | tf_op jit(solution)/shard_map/ppermute | solution.py:28
  6.5 8.0 %collective-permute-start.1 = (f32[208,256]{1,0:T(8,128)S(1)}, f32[208,256]{1,0:T(8,128)S(1)}, u32[]{:S(2)}, u32[]{:S(2)}) collective-permute-start(f32[208,256]{1,0:T(8,128)S(1)} %get-tuple-element.40), channel_id=1, source_target_pairs={{0,4},{4,8},{8,12},{12,16},{16,20},{20,24},{24,28},{28,0},{1,5},{5... | collective-permute-start | bytes 638984 | tf_op jit(solution)/shard_map/ppermute | solution.py:28
  6.6 3.9 %copy-start = (f32[400,256]{1,0:T(8,128)S(1)}, f32[400,256]{1,0:T(8,128)}, u32[]{:S(2)}) copy-start(f32[400,256]{1,0:T(8,128)} %dst.1) | copy-start | bytes 1228804
  6.6 3.9 %copy-start.1 = (f32[400,16]{0,1:T(8,128)S(1)}, f32[400,16]{0,1:T(8,128)}, u32[]{:S(2)}) copy-start(f32[400,16]{0,1:T(8,128)} %param.18) | copy-start | bytes 76804
  6.6 3.9 %copy-start.7 = (f32[256]{0:T(256)S(1)}, f32[256]{0:T(256)}, u32[]{:S(2)}) copy-start(f32[256]{0:T(256)} %param.15) | copy-start | bytes 3076
  6.6 3.9 %copy-start.8 = (f32[256]{0:T(256)S(1)}, f32[256]{0:T(256)}, u32[]{:S(2)}) copy-start(f32[256]{0:T(256)} %param.17) | copy-start | bytes 3076
  9.9 4.6 %collective-permute-start.2 = (f32[208,256]{1,0:T(8,128)S(1)}, f32[208,256]{1,0:T(8,128)S(1)}, u32[]{:S(2)}, u32[]{:S(2)}) collective-permute-start(f32[208,256]{1,0:T(8,128)S(1)} %get-tuple-element.44), channel_id=1, source_target_pairs={{0,4},{1,5},{2,6},{3,7},{4,0},{5,1},{6,2},{7,3},{8,12},{9,13},{10,... | collective-permute-start | bytes 638984 | tf_op jit(solution)/shard_map/ppermute | solution.py:38
  10.0 0.7 %copy-start.5 = (s32[2,512]{1,0:T(2,128)S(1)}, s32[2,512]{1,0:T(2,128)}, u32[]{:S(2)}) copy-start(s32[2,512]{1,0:T(2,128)} %negs.1) | copy-start | bytes 12292
  10.0 2.6 %collective-permute-start.3 = (f32[200,256]{1,0:T(8,128)S(1)}, f32[200,256]{1,0:T(8,128)S(1)}, u32[]{:S(2)}, u32[]{:S(2)}) collective-permute-start(f32[200,256]{1,0:T(8,128)S(1)} %get-tuple-element.45), channel_id=1, source_target_pairs={{0,4},{1,5},{2,6},{3,7},{4,0},{5,1},{6,2},{7,3},{8,12},{9,13},{10,... | collective-permute-start | bytes 614408 | tf_op jit(solution)/shard_map/ppermute | solution.py:38
  10.5 0.7 %copy-start.2 = (s32[2,2,256]{2,1,0:T(2,128)S(1)}, s32[2,2,256]{2,1,0:T(2,128)}, u32[]{:S(2)}) copy-start(s32[2,2,256]{2,1,0:T(2,128)} %rows.3) | copy-start | bytes 12292
  10.5 0.7 %copy-start.4 = (s32[2,256]{1,0:T(2,128)S(1)}, s32[2,256]{1,0:T(2,128)}, u32[]{:S(2)}) copy-start(s32[2,256]{1,0:T(2,128)} %rels.3) | copy-start | bytes 6148
  10.5 0.7 %copy-start.6 = (s32[2,1]{0,1:T(1,128)S(1)}, s32[2,1]{0,1:T(1,128)}, u32[]{:S(2)}) copy-start(s32[2,1]{0,1:T(1,128)} %param.22) | copy-start | bytes 28
  12.6 3.6 %collective-permute-start.5 = (f32[1,256]{1,0:T(1,128)S(1)}, f32[1,256]{1,0:T(1,128)S(1)}, u32[]{:S(2)}, u32[]{:S(2)}) collective-permute-start(f32[1,256]{1,0:T(1,128)S(1)} %get-tuple-element.57), channel_id=1, source_target_pairs={{0,1},{1,0},{2,3},{3,2},{4,5},{5,4},{6,7},{7,6},{8,9},{9,8},{10,11... | collective-permute-start | bytes 3080 | tf_op jit(solution)/shard_map/ppermute | solution.py:23
  17.4 1.6 %collective-permute-start.6 = (f32[56,128]{1,0:T(8,128)S(1)}, f32[56,128]{1,0:T(8,128)S(1)}, u32[]{:S(2)}, u32[]{:S(2)}) collective-permute-start(f32[56,128]{1,0:T(8,128)S(1)} %get-tuple-element.67), channel_id=1, source_target_pairs={{0,4},{1,5},{2,6},{3,7},{4,0},{5,1},{6,2},{7,3},{8,12},{9,13},{10,... | collective-permute-start | bytes 86024 | tf_op jit(solution)/shard_map/ppermute | solution.py:38
  17.4 4.2 %collective-permute-start.7 = (f32[56,128]{1,0:T(8,128)S(1)}, f32[56,128]{1,0:T(8,128)S(1)}, u32[]{:S(2)}, u32[]{:S(2)}) collective-permute-start(f32[56,128]{1,0:T(8,128)S(1)} %get-tuple-element.67), channel_id=1, source_target_pairs={{0,8},{1,9},{2,10},{3,11},{4,12},{5,13},{6,14},{7,15},{8,0},{9,1},... | collective-permute-start | bytes 86024 | tf_op jit(solution)/shard_map/ppermute | solution.py:38
  19.0 3.9 %collective-permute-start.9 = (f32[56,128]{1,0:T(8,128)S(1)}, f32[56,128]{1,0:T(8,128)S(1)}, u32[]{:S(2)}, u32[]{:S(2)}) collective-permute-start(f32[56,128]{1,0:T(8,128)S(1)} %add.12), channel_id=1, source_target_pairs={{0,16},{1,17},{2,18},{3,19},{4,20},{5,21},{6,22},{7,23},{8,24},{9,... | collective-permute-start | bytes 86024 | tf_op jit(solution)/shard_map/ppermute | solution.py:38
  20.6 4.8 %collective-permute-start.10 = (f32[56,128]{1,0:T(8,128)S(1)}, f32[56,128]{1,0:T(8,128)S(1)}, u32[]{:S(2)}, u32[]{:S(2)}) collective-permute-start(f32[56,128]{1,0:T(8,128)S(1)} %add.12), channel_id=1, source_target_pairs={{0,24},{1,25},{2,26},{3,27},{4,28},{5,29},{6,30},{7,31},{8,16},{9,... | collective-permute-start | bytes 86024 | tf_op jit(solution)/shard_map/ppermute | solution.py:38
  21.6 3.8 %collective-permute-start.8 = (f32[56,128]{1,0:T(8,128)S(1)}, f32[56,128]{1,0:T(8,128)S(1)}, u32[]{:S(2)}, u32[]{:S(2)}) collective-permute-start(f32[56,128]{1,0:T(8,128)S(1)} %collective-permute-done.7), channel_id=1, source_target_pairs={{0,4},{1,5},{2,6},{3,7},{4,0},{5,1},{6,2},{7,3},{8,12},{9,13},{10,... | collective-permute-start | bytes 86024 | tf_op jit(solution)/shard_map/ppermute | solution.py:38
  25.4 3.9 %collective-permute-start.12 = (f32[56,128]{1,0:T(8,128)S(1)}, f32[56,128]{1,0:T(8,128)S(1)}, u32[]{:S(2)}, u32[]{:S(2)}) collective-permute-start(f32[56,128]{1,0:T(8,128)S(1)} %add_add_fusion.refs_0_), channel_id=1, source_target_pairs={{0,1},{1,0},{2,3},{3,2},{4,7},{5,6},{6,5},{7,4},{8,9},{9,8},{10,11... | collective-permute-start | bytes 86024 | tf_op jit(solution)/shard_map/ppermute | solution.py:38
  25.9 4.9 %collective-permute-start.11 = (f32[56,128]{1,0:T(8,128)S(1)}, f32[56,128]{1,0:T(8,128)S(1)}, u32[]{:S(2)}, u32[]{:S(2)}) collective-permute-start(f32[56,128]{1,0:T(8,128)S(1)} %add_add_fusion.refs_0_), channel_id=1, source_target_pairs={{0,2},{1,3},{2,0},{3,1},{4,6},{5,7},{6,4},{7,5},{8,10},{9,11},{10,... | collective-permute-start | bytes 86024 | tf_op jit(solution)/shard_map/ppermute | solution.py:38
  29.3 1.5 %collective-permute-start.13 = (f32[56,128]{1,0:T(8,128)S(1)}, f32[56,128]{1,0:T(8,128)S(1)}, u32[]{:S(2)}, u32[]{:S(2)}) collective-permute-start(f32[56,128]{1,0:T(8,128)S(1)} %collective-permute-done.12.refs_2_), channel_id=1, source_target_pairs={{0,4},{1,5},{2,6},{3,7},{4,0},{5,1},{6,2},{7,3},{8,12},{9,13},{10,... | collective-permute-start | bytes 86024 | tf_op jit(solution)/shard_map/ppermute | solution.py:38
  29.3 1.5 %copy-start.3 = (f32[400,16]{0,1:T(8,128)S(1)}, f32[400,16]{0,1:T(8,128)}, u32[]{:S(2)}) copy-start(f32[400,16]{0,1:T(8,128)} %param.19) | copy-start | bytes 76804

commit v4 on v3

--- a/solution.py
+++ b/solution.py
@@ -51,7 +51,7 @@
     return steps
 
 
-def exchanged_terms(array):
+def exchanged_terms(array, beside):
     steps = [(0, r, u) for r, u in digits(lax.axis_size("src") // 2, 2)]
     steps += [(1, r, u) for r, u in digits(lax.axis_size("dst"), 1)]
     terms = None
@@ -66,9 +66,11 @@
             if radix == 4:
                 two = sent(array, (flip(2), flip(2)))
                 three = sent(array, (flip(3), flip(3)))
-                (late,) = call(add_kernel, [VMEM] * 2, [array.shape], 10**9, [two, three])
+                turn = beside(one)
+                (late,) = call(add_kernel, [VMEM] * 3, [array.shape], 10**9, [two, three, turn])
                 terms = ((array, one + core_swapped(one)), (late,))
             else:
+                beside(one)
                 terms = ((array,), (one + core_swapped(one),))
             continue
         array = tree_sum([tree_sum(pair) for pair in terms])
@@ -242,18 +244,23 @@
     product_out[...] = query_grad * src_cols
 
 
-def first_back_kernel(
-    dst, dst_state, query, coef, product, rel, rows, rels, counts, negs,
-    spare_state, table_out, state_out, rel_first_out, rel_cols_out, scale_out, base_out, spare_out,
+def between_kernel(
+    product, rel, rows, rels, counts, negs, spare_state,
+    rel_first_out, rel_cols_out, scale_out, base_out, spare_out,
 ):
+    rel_first_out[...] = dot_right(
+        hot_relations(0, rels, rel.shape[0]), halves(product[...]), NT
+    )
+    rel_cols_out[...] = dot_left(halves(rel[...]), hot_relations(1, rels, rel.shape[0]), TN)
+    columns = scale_out.shape[0]
+    scale_out[...], base_out[...] = coefficient_parts(1, columns, rows, counts, negs)
+    spare_out[...] = spare_state[...]
+
+
+def first_back_kernel(dst, dst_state, query, coef, turn, table_out, state_out, turn_out):
     grad = dot_split(halves(query[...]), halves(coef[...]), NT)
     table_out[...], state_out[...] = row_step(dst[...], dst_state[...], grad)
-    rel_first_out[...] = dot_right(
-        hot_relations(0, rels, rel.shape[0]), halves(product[...]), NT
-    )
-    rel_cols_out[...] = dot_left(halves(rel[...]), hot_relations(1, rels, rel.shape[0]), TN)
-    scale_out[...], base_out[...] = coefficient_parts(1, dst.shape[1], rows, counts, negs)
-    spare_out[...] = spare_state[...]
+    turn_out[...] = jnp.zeros_like(turn_out)
 
 
 def second_gather_kernel(count, *refs):
@@ -299,7 +306,7 @@
     spare_out[...], spare_acc[...] = row_step(spare[...], spare_state[...], spare_grad)
 
 
-def add_kernel(left, right, out):
+def add_kernel(left, right, turn, out):
     out[...] = left[...] + right[...]
 
 
@@ -370,22 +377,16 @@
 
     *across, query, coef, product = first_on(1, cut(features + 24, 2), 400 * work)
     across = passed_along(tuple(across), "src", 1)
-    *within, query, coef, product = first_on(
+    *within, query, coef_first, product = first_on(
         0, cut(features + 8, 2), 1 * work, (query, coef, product)
     )
     within = tuple(core_swapped(part) for part in within)
-    dst_next, dst_acc, rel_first, rel_cols, scale, base, spare_acc = call(
-        first_back_kernel,
-        [VMEM] * 11,
-        [
-            (features, rows), (1, rows), (rels, features), (features, edges), (rows, edges),
-            (rows, edges), (1, rows),
-        ],
-        3 * work,
-        [
-            dst_table, dst_state.reshape(1, rows), query, coef, product,
-            rel, edge_rows, edge_rel, live, negatives, spare_state.reshape(1, rows),
-        ],
+    rel_first, rel_cols, scale, base, spare_acc = call(
+        between_kernel,
+        [VMEM] * 7,
+        [(rels, features), (features, edges), (rows, edges), (rows, edges), (1, rows)],
+        work,
+        [product, rel, edge_rows, edge_rel, live, negatives, spare_state.reshape(1, rows)],
     )
     spare_acc_in = swapped(spare_acc, "dst", 0)
     moved, src_cols, high, low = call(
@@ -412,7 +413,22 @@
         5 * work,
         [moved, spare_in, spare_acc_in, edge_rows, high, low, coef, scaled],
     )
-    terms = exchanged_terms(rel_both)
+    dst_results = []
+
+    def first_back(one):
+        dst_results.extend(
+            call(
+                first_back_kernel,
+                [VMEM] * 5,
+                [(features, rows), (1, rows), (8, 128)],
+                3 * work,
+                [dst_table, dst_state.reshape(1, rows), query, coef_first, one],
+            )
+        )
+        return dst_results.pop()
+
+    terms = exchanged_terms(rel_both, first_back)
+    dst_next, dst_acc = dst_results
     relations_out, rel_state_out = call(
         relation_kernel,
         [VMEM] * (2 + len(terms)),

time: 31.7 us -> 30.8 us (0.972)
  waiting for transfers between devices: 7.6 us -> 5.79 us
  local copies, waits for them, and re-layouts: 0.68 us -> 1.37 us
    ppermute x10, waiting for transfers between devices: 4.65 us -> 2.85 us  [sent(): return lax.ppermute(array, ('src', 'dst'), pairs)]
    ppermute x2, waiting for transfers between devices: 1.34 us -> 0.45 us  [swapped(): lax.ppermute(array, axis, [(i, i ^ 1 << stride) for i in range(lax.axis_s...]
    ppermute x2, waiting for transfers between devices: 1.62 us -> 2.49 us  [passed_along(): lax.ppermute(array, axis, [(i, (i + by) % count) for i in range(count)])]
    unnamed x18, local copies, waits for them, and re-layouts: 0.68 us -> 1.37 us
    pallas_call x8 -> x9, Pallas kernels: 8.39 us -> 8.65 us  [call(): pl.pallas_call(kernel, in_specs=in_specs, out_specs=[VMEM] * len(outs), o...]
  transfers between devices with their start and end apart: 14 -> 14, of which waited for: 5 -> 5; matrix products, arithmetic and copies ran while one was open for 0% -> 0% of each run, Pallas kernels for 20% -> 22%
where the time goes in v4:
time: 30.8 us; the launch traced here: 30.6 us
  starting transfers between devices  14 us (45%)
  Pallas kernels  8.65 us (28%)
  waiting for transfers between devices  5.79 us (19%)
  local copies, waits for them, and re-layouts  1.37 us (4%)
  between operations  0.74 us (2%)
    pallas_call x9, Pallas kernels, call(): pl.pallas_call(kernel, in_specs=in_specs, out_specs=[VMEM] * len(outs), o...  8.65 us
    ppermute x10, starting transfers between devices, sent(): return lax.ppermute(array, ('src', 'dst'), pairs)  7.83 us
    ppermute x2, starting transfers between devices, swapped(): lax.ppermute(array, axis, [(i, i ^ 1 << stride) for i in range(lax.axis_s...  3.4 us
    ppermute x10, waiting for transfers between devices, sent(): return lax.ppermute(array, ('src', 'dst'), pairs)  2.85 us
    ppermute x2, starting transfers between devices, passed_along(): lax.ppermute(array, axis, [(i, (i + by) % count) for i in range(count)])  2.8 us
    ppermute x2, waiting for transfers between devices, passed_along(): lax.ppermute(array, axis, [(i, (i + by) % count) for i in range(count)])  2.49 us
    unnamed x18, local copies, waits for them, and re-layouts  1.37 us
  transfers between devices with their start and end apart: 14, of which 5 were waited for; matrix products, arithmetic and copies ran while one was open for 0% of the time, Pallas kernels for 22%

profile of v4, /device:TPU:0, one launch (start us, length us, event | category | flops | bytes accessed | tf_op | source)
XLA Modules:
  0.0 30.6 jit_solution(18211479309389343176)
XLA Ops:
  0.6 3.1 %collective-permute-start.4 = (f32[400,256]{1,0:T(8,128)}, f32[400,256]{1,0:T(8,128)S(1)}, u32[]{:S(2)}, u32[]{:S(2)}) collective-permute-start(f32[400,256]{1,0:T(8,128)} %param.16), channel_id=1, source_target_pairs={{0,1},{1,0},{2,3},{3,2},{4,5},{5,4},{6,7},{7,6},{8,9},{9,8},{10,11... | collective-permute-start | bytes 1228808 | tf_op jit(solution)/shard_map/ppermute | solution.py:23
  3.8 2.7 %collective-permute-start = (f32[216,256]{1,0:T(8,128)S(1)}, f32[216,256]{1,0:T(8,128)S(1)}, u32[]{:S(2)}, u32[]{:S(2)}) collective-permute-start(f32[216,256]{1,0:T(8,128)S(1)} %get-tuple-element.40), channel_id=1, source_target_pairs={{0,4},{4,8},{8,12},{12,16},{16,20},{20,24},{24,28},{28,0},{1,5},{5... | collective-permute-start | bytes 663560 | tf_op jit(solution)/shard_map/ppermute | solution.py:28
  6.6 3.2 %shard_map.180 = (f32[208,256]{1,0:T(8,128)S(1)}, f32[200,256]{1,0:T(8,128)S(1)}, f32[400,256]{1,0:T(8,128)S(1)}, f32[256,256]{1,0:T(8,128)S(1)}, f32[400,256]{1,0:T(8,128)S(1)}) custom-call(f32[400,256]{1,0:T(8,128)S(1)} %get-tuple-element.42.refs_0_, f32[256,256]{1,0:T(8,128)S(1)} %get-tuple-element.43.refs_1_, f32[400,256]{1,0:T(8,128)S(1)} %get-tuple-element.44.refs_2_, ...), custom_call_target="tpu_custom_call" | custom-call | flops 52428800 | bytes 1937416 | tf_op jit(solution)/shard_map/pallas_call | solution.py:323
  10.0 0.5 %collective-permute-start.3 = (f32[200,256]{1,0:T(8,128)S(1)}, f32[200,256]{1,0:T(8,128)S(1)}, u32[]{:S(2)}, u32[]{:S(2)}) collective-permute-start(f32[200,256]{1,0:T(8,128)S(1)} %get-tuple-element.46), channel_id=1, source_target_pairs={{0,4},{1,5},{2,6},{3,7},{4,0},{5,1},{6,2},{7,3},{8,12},{9,13},{10,... | collective-permute-start | bytes 614408 | tf_op jit(solution)/shard_map/ppermute | solution.py:38
  10.5 0.1 copy-done.2
  10.6 0.5 %copy-done.6 = s32[2,1]{0,1:T(1,128)S(1)} copy-done((s32[2,1]{0,1:T(1,128)S(1)}, s32[2,1]{0,1:T(1,128)}, u32[]{:S(2)}) %copy-start.6) | copy-done | bytes 32
  11.1 0.4 %shard_map.181 = (f32[16,400]{1,0:T(8,128)S(1)}, f32[400,256]{1,0:T(8,128)S(1)}, f32[256,256]{1,0:T(8,128)S(1)}, f32[256,256]{1,0:T(8,128)S(1)}, f32[1,256]{1,0:T(1,128)S(1)}) custom-call(f32[400,256]{1,0:T(8,128)S(1)} %get-tuple-element.47.product, f32[16,400]{1,0:T(8,128)S(1)} %bitcast.13, s32[2,2,256]{2,1,0:T(2,128)S(1)} %copy-done.2, ...), custom_call_target="tpu_custom_call" | custom-call | flops 52428800 | bytes 446472 | tf_op jit(solution)/shard_map/pallas_call | solution.py:323
  11.6 0.1 collective-permute-done.3.refs_3_
  11.7 0.3 %collective-permute-start.5 = (f32[1,256]{1,0:T(1,128)S(1)}, f32[1,256]{1,0:T(1,128)S(1)}, u32[]{:S(2)}, u32[]{:S(2)}) collective-permute-start(f32[1,256]{1,0:T(1,128)S(1)} %get-tuple-element.56), channel_id=1, source_target_pairs={{0,1},{1,0},{2,3},{3,2},{4,5},{5,4},{6,7},{7,6},{8,9},{9,8},{10,11... | collective-permute-start | bytes 3080 | tf_op jit(solution)/shard_map/ppermute | solution.py:23
  12.0 2.5 %collective-permute-done.1.refs_1_ = f32[208,256]{1,0:T(8,128)S(1)} collective-permute-done((f32[208,256]{1,0:T(8,128)S(1)}, f32[208,256]{1,0:T(8,128)S(1)}, u32[]{:S(2)}, u32[]{:S(2)}) %collective-permute-start.1) | collective-permute-done | bytes 213024 | tf_op jit(solution)/shard_map/ppermute | solution.py:28
  14.5 0.3 shard_map.182
  14.8 0.5 %collective-permute-done.5.state = f32[1,256]{1,0:T(1,128)S(1)} collective-permute-done((f32[1,256]{1,0:T(1,128)S(1)}, f32[1,256]{1,0:T(1,128)S(1)}, u32[]{:S(2)}, u32[]{:S(2)}) %collective-permute-start.5) | collective-permute-done | bytes 1056 | tf_op jit(solution)/shard_map/ppermute | solution.py:23
  15.3 1.2 %shard_map.183 = (f32[256,256]{1,0:T(8,128)S(1)}, f32[400,256]{1,0:T(8,128)S(1)}, f32[56,128]{1,0:T(8,128)S(1)}, f32[1,256]{1,0:T(1,128)S(1)}) custom-call(f32[400,256]{1,0:T(8,128)S(1)} %collective-permute-done.4.spare, f32[400,256]{1,0:T(8,128)S(1)} %get-tuple-element.50.src_cols, bf16[400,256]{1,0:T(8,128)(2,1)S(1)} %get-tuple-element.51.high, ...), custom_call_target="tpu_custom_call" | custom-call | flops 524288000 | bytes 2600960 | tf_op jit(solution)/shard_map/pallas_call | solution.py:323
  16.5 1.6 %collective-permute-start.6 = (f32[56,128]{1,0:T(8,128)S(1)}, f32[56,128]{1,0:T(8,128)S(1)}, u32[]{:S(2)}, u32[]{:S(2)}) collective-permute-start(f32[56,128]{1,0:T(8,128)S(1)} %get-tuple-element.64), channel_id=1, source_target_pairs={{0,8},{1,9},{2,10},{3,11},{4,12},{5,13},{6,14},{7,15},{8,0},{9,1},... | collective-permute-start | bytes 86024 | tf_op jit(solution)/shard_map/ppermute | solution.py:38
  18.1 1.6 %collective-permute-start.9 = (f32[56,128]{1,0:T(8,128)S(1)}, f32[56,128]{1,0:T(8,128)S(1)}, u32[]{:S(2)}, u32[]{:S(2)}) collective-permute-start(f32[56,128]{1,0:T(8,128)S(1)} %add.12), channel_id=1, source_target_pairs={{0,16},{1,17},{2,18},{3,19},{4,20},{5,21},{6,22},{7,23},{8,24},{9,... | collective-permute-start | bytes 86024 | tf_op jit(solution)/shard_map/ppermute | solution.py:38
  19.7 1.0 %collective-permute-start.10 = (f32[56,128]{1,0:T(8,128)S(1)}, f32[56,128]{1,0:T(8,128)S(1)}, u32[]{:S(2)}, u32[]{:S(2)}) collective-permute-start(f32[56,128]{1,0:T(8,128)S(1)} %add.12), channel_id=1, source_target_pairs={{0,24},{1,25},{2,26},{3,27},{4,28},{5,29},{6,30},{7,31},{8,16},{9,... | collective-permute-start | bytes 86024 | tf_op jit(solution)/shard_map/ppermute | solution.py:38
  20.7 0.7 %copy-done.8 = f32[256]{0:T(256)S(1)} copy-done((f32[256]{0:T(256)S(1)}, f32[256]{0:T(256)}, u32[]{:S(2)}) %copy-start.8) | copy-done | bytes 1048
  21.4 1.2 %shard_map.185 = (f32[400,256]{1,0:T(8,128)}, f32[1,256]{1,0:T(1,128)}, f32[8,128]{1,0:T(8,128)S(1)}) custom-call(f32[400,256]{1,0:T(8,128)S(1)} %copy-done, f32[1,256]{1,0:T(1,128)S(1)} %bitcast.20, f32[400,256]{1,0:T(8,128)S(1)} %get-tuple-element.62.query, f32[256,256]{1,0:T(8,128)S(1)} %get-tuple-element.63.coef, f32[56,128]{1,0:T(8,128)S(1)} %collective-permute-done.6.turn), custom_call_target="tpu_custom_call" | custom-call | flops 157286400 | bytes 1111040 | tf_op jit(solution)/shard_map/pallas_call | solution.py:323
  22.6 1.8 %collective-permute-done.10.right = f32[56,128]{1,0:T(8,128)S(1)} collective-permute-done((f32[56,128]{1,0:T(8,128)S(1)}, f32[56,128]{1,0:T(8,128)S(1)}, u32[]{:S(2)}, u32[]{:S(2)}) %collective-permute-start.10) | collective-permute-done | bytes 28704 | tf_op jit(solution)/shard_map/ppermute | solution.py:38
  24.5 0.5 %collective-permute-start.12 = (f32[56,128]{1,0:T(8,128)S(1)}, f32[56,128]{1,0:T(8,128)S(1)}, u32[]{:S(2)}, u32[]{:S(2)}) collective-permute-start(f32[56,128]{1,0:T(8,128)S(1)} %add_add_fusion.refs_0_), channel_id=1, source_target_pairs={{0,1},{1,0},{2,3},{3,2},{4,7},{5,6},{6,5},{7,4},{8,9},{9,8},{10,11... | collective-permute-start | bytes 86024 | tf_op jit(solution)/shard_map/ppermute | solution.py:38
  25.0 2.6 %collective-permute-start.11 = (f32[56,128]{1,0:T(8,128)S(1)}, f32[56,128]{1,0:T(8,128)S(1)}, u32[]{:S(2)}, u32[]{:S(2)}) collective-permute-start(f32[56,128]{1,0:T(8,128)S(1)} %add_add_fusion.refs_0_), channel_id=1, source_target_pairs={{0,2},{1,3},{2,0},{3,1},{4,6},{5,7},{6,4},{7,5},{8,10},{9,11},{10,... | collective-permute-start | bytes 86024 | tf_op jit(solution)/shard_map/ppermute | solution.py:38
  27.6 0.8 %collective-permute-done.12.refs_2_ = f32[56,128]{1,0:T(8,128)S(1)} collective-permute-done((f32[56,128]{1,0:T(8,128)S(1)}, f32[56,128]{1,0:T(8,128)S(1)}, u32[]{:S(2)}, u32[]{:S(2)}) %collective-permute-start.12) | collective-permute-done | bytes 28704 | tf_op jit(solution)/shard_map/ppermute | solution.py:38
  28.4 1.4 %shard_map.184 = (f32[400,256]{1,0:T(8,128)}, f32[1,256]{1,0:T(1,128)}, f32[400,256]{1,0:T(8,128)}, f32[1,256]{1,0:T(1,128)}) custom-call(f32[408,256]{1,0:T(8,128)S(1)} %get-tuple-element.49.moved, f32[400,256]{1,0:T(8,128)S(1)} %collective-permute-done.4.spare, f32[1,256]{1,0:T(1,128)S(1)} %get-tuple-element.57.spare_state, s32[2,2,256]{2,1,0:T(2,128)S(1)} %copy-done.2, ...), custom_call_target="tpu_custom_call" | custom-call | flops 262144000 | bytes 2323456 | tf_op jit(solution)/shard_map/pallas_call | solution.py:323
  29.9 0.7 %shard_map.187 = (f32[16,400]{1,0:T(8,128)}, f32[16,400]{1,0:T(8,128)}) custom-call(f32[16,400]{1,0:T(8,128)S(1)} %bitcast.14, f32[16,400]{1,0:T(8,128)S(1)} %bitcast.15, f32[56,128]{1,0:T(8,128)S(1)} %add_add_fusion.refs_0_, f32[56,128]{1,0:T(8,128)S(1)} %collective-permute-done.11.refs_1_, f32[56,128]{1,0:T(8,128)S(1)} %collective-permute-done.12.refs_2_, ...), custom_call_target="tpu_custom_call" | custom-call | flops 6400 | bytes 165888 | tf_op jit(solution)/shard_map/pallas_call | solution.py:323
  (33 shorter events, 0.5 us)
Async XLA Ops:
  0.6 14.6 %collective-permute-start.4 = (f32[400,256]{1,0:T(8,128)}, f32[400,256]{1,0:T(8,128)S(1)}, u32[]{:S(2)}, u32[]{:S(2)}) collective-permute-start(f32[400,256]{1,0:T(8,128)} %param.16), channel_id=1, source_target_pairs={{0,1},{1,0},{2,3},{3,2},{4,5},{5,4},{6,7},{7,6},{8,9},{9,8},{10,11... | collective-permute-start | bytes 1228808 | tf_op jit(solution)/shard_map/ppermute | solution.py:23
  3.8 10.7 %collective-permute-start = (f32[216,256]{1,0:T(8,128)S(1)}, f32[216,256]{1,0:T(8,128)S(1)}, u32[]{:S(2)}, u32[]{:S(2)}) collective-permute-start(f32[216,256]{1,0:T(8,128)S(1)} %get-tuple-element.40), channel_id=1, source_target_pairs={{0,4},{4,8},{8,12},{12,16},{16,20},{20,24},{24,28},{28,0},{1,5},{5... | collective-permute-start | bytes 663560 | tf_op jit(solution)/shard_map/ppermute | solution.py:28
  6.5 8.0 %collective-permute-start.1 = (f32[208,256]{1,0:T(8,128)S(1)}, f32[208,256]{1,0:T(8,128)S(1)}, u32[]{:S(2)}, u32[]{:S(2)}) collective-permute-start(f32[208,256]{1,0:T(8,128)S(1)} %get-tuple-element.41), channel_id=1, source_target_pairs={{0,4},{4,8},{8,12},{12,16},{16,20},{20,24},{24,28},{28,0},{1,5},{5... | collective-permute-start | bytes 638984 | tf_op jit(solution)/shard_map/ppermute | solution.py:28
  6.6 3.9 %copy-start.1 = (f32[400,16]{0,1:T(8,128)S(1)}, f32[400,16]{0,1:T(8,128)}, u32[]{:S(2)}) copy-start(f32[400,16]{0,1:T(8,128)} %param.18) | copy-start | bytes 76804
  6.6 3.9 %copy-start.5 = (s32[2,512]{1,0:T(2,128)S(1)}, s32[2,512]{1,0:T(2,128)}, u32[]{:S(2)}) copy-start(s32[2,512]{1,0:T(2,128)} %negs.1) | copy-start | bytes 12292
  9.9 0.7 %copy-start.2 = (s32[2,2,256]{2,1,0:T(2,128)S(1)}, s32[2,2,256]{2,1,0:T(2,128)}, u32[]{:S(2)}) copy-start(s32[2,2,256]{2,1,0:T(2,128)} %rows.3) | copy-start | bytes 12292
  9.9 4.6 %collective-permute-start.2 = (f32[208,256]{1,0:T(8,128)S(1)}, f32[208,256]{1,0:T(8,128)S(1)}, u32[]{:S(2)}, u32[]{:S(2)}) collective-permute-start(f32[208,256]{1,0:T(8,128)S(1)} %get-tuple-element.45), channel_id=1, source_target_pairs={{0,4},{1,5},{2,6},{3,7},{4,0},{5,1},{6,2},{7,3},{8,12},{9,13},{10,... | collective-permute-start | bytes 638984 | tf_op jit(solution)/shard_map/ppermute | solution.py:38
  9.9 0.7 %copy-start.4 = (s32[2,256]{1,0:T(2,128)S(1)}, s32[2,256]{1,0:T(2,128)}, u32[]{:S(2)}) copy-start(s32[2,256]{1,0:T(2,128)} %rels.3) | copy-start | bytes 6148
  10.0 1.7 %collective-permute-start.3 = (f32[200,256]{1,0:T(8,128)S(1)}, f32[200,256]{1,0:T(8,128)S(1)}, u32[]{:S(2)}, u32[]{:S(2)}) collective-permute-start(f32[200,256]{1,0:T(8,128)S(1)} %get-tuple-element.46), channel_id=1, source_target_pairs={{0,4},{1,5},{2,6},{3,7},{4,0},{5,1},{6,2},{7,3},{8,12},{9,13},{10,... | collective-permute-start | bytes 614408 | tf_op jit(solution)/shard_map/ppermute | solution.py:38
  10.4 0.7 %copy-start.6 = (s32[2,1]{0,1:T(1,128)S(1)}, s32[2,1]{0,1:T(1,128)}, u32[]{:S(2)}) copy-start(s32[2,1]{0,1:T(1,128)} %param.22) | copy-start | bytes 28
  10.5 0.7 %copy-start.7 = (f32[256]{0:T(256)S(1)}, f32[256]{0:T(256)}, u32[]{:S(2)}) copy-start(f32[256]{0:T(256)} %param.17) | copy-start | bytes 3076
  11.7 3.6 %collective-permute-start.5 = (f32[1,256]{1,0:T(1,128)S(1)}, f32[1,256]{1,0:T(1,128)S(1)}, u32[]{:S(2)}, u32[]{:S(2)}) collective-permute-start(f32[1,256]{1,0:T(1,128)S(1)} %get-tuple-element.56), channel_id=1, source_target_pairs={{0,1},{1,0},{2,3},{3,2},{4,5},{5,4},{6,7},{7,6},{8,9},{9,8},{10,11... | collective-permute-start | bytes 3080 | tf_op jit(solution)/shard_map/ppermute | solution.py:23
  15.3 5.4 %copy-start = (f32[400,256]{1,0:T(8,128)S(1)}, f32[400,256]{1,0:T(8,128)}, u32[]{:S(2)}) copy-start(f32[400,256]{1,0:T(8,128)} %dst.1) | copy-start | bytes 1228804
  16.5 1.6 %collective-permute-start.7 = (f32[56,128]{1,0:T(8,128)S(1)}, f32[56,128]{1,0:T(8,128)S(1)}, u32[]{:S(2)}, u32[]{:S(2)}) collective-permute-start(f32[56,128]{1,0:T(8,128)S(1)} %get-tuple-element.64), channel_id=1, source_target_pairs={{0,4},{1,5},{2,6},{3,7},{4,0},{5,1},{6,2},{7,3},{8,12},{9,13},{10,... | collective-permute-start | bytes 86024 | tf_op jit(solution)/shard_map/ppermute | solution.py:38
  16.5 4.2 %collective-permute-start.6 = (f32[56,128]{1,0:T(8,128)S(1)}, f32[56,128]{1,0:T(8,128)S(1)}, u32[]{:S(2)}, u32[]{:S(2)}) collective-permute-start(f32[56,128]{1,0:T(8,128)S(1)} %get-tuple-element.64), channel_id=1, source_target_pairs={{0,8},{1,9},{2,10},{3,11},{4,12},{5,13},{6,14},{7,15},{8,0},{9,1},... | collective-permute-start | bytes 86024 | tf_op jit(solution)/shard_map/ppermute | solution.py:38
  18.1 4.5 %collective-permute-start.9 = (f32[56,128]{1,0:T(8,128)S(1)}, f32[56,128]{1,0:T(8,128)S(1)}, u32[]{:S(2)}, u32[]{:S(2)}) collective-permute-start(f32[56,128]{1,0:T(8,128)S(1)} %add.12), channel_id=1, source_target_pairs={{0,16},{1,17},{2,18},{3,19},{4,20},{5,21},{6,22},{7,23},{8,24},{9,... | collective-permute-start | bytes 86024 | tf_op jit(solution)/shard_map/ppermute | solution.py:38
  19.7 4.8 %collective-permute-start.10 = (f32[56,128]{1,0:T(8,128)S(1)}, f32[56,128]{1,0:T(8,128)S(1)}, u32[]{:S(2)}, u32[]{:S(2)}) collective-permute-start(f32[56,128]{1,0:T(8,128)S(1)} %add.12), channel_id=1, source_target_pairs={{0,24},{1,25},{2,26},{3,27},{4,28},{5,29},{6,30},{7,31},{8,16},{9,... | collective-permute-start | bytes 86024 | tf_op jit(solution)/shard_map/ppermute | solution.py:38
  20.7 3.8 %collective-permute-start.8 = (f32[56,128]{1,0:T(8,128)S(1)}, f32[56,128]{1,0:T(8,128)S(1)}, u32[]{:S(2)}, u32[]{:S(2)}) collective-permute-start(f32[56,128]{1,0:T(8,128)S(1)} %collective-permute-done.6.turn), channel_id=1, source_target_pairs={{0,4},{1,5},{2,6},{3,7},{4,0},{5,1},{6,2},{7,3},{8,12},{9,13},{10,... | collective-permute-start | bytes 86024 | tf_op jit(solution)/shard_map/ppermute | solution.py:38
  20.7 0.7 %copy-start.8 = (f32[256]{0:T(256)S(1)}, f32[256]{0:T(256)}, u32[]{:S(2)}) copy-start(f32[256]{0:T(256)} %param.15) | copy-start | bytes 3076
  24.5 3.9 %collective-permute-start.12 = (f32[56,128]{1,0:T(8,128)S(1)}, f32[56,128]{1,0:T(8,128)S(1)}, u32[]{:S(2)}, u32[]{:S(2)}) collective-permute-start(f32[56,128]{1,0:T(8,128)S(1)} %add_add_fusion.refs_0_), channel_id=1, source_target_pairs={{0,1},{1,0},{2,3},{3,2},{4,7},{5,6},{6,5},{7,4},{8,9},{9,8},{10,11... | collective-permute-start | bytes 86024 | tf_op jit(solution)/shard_map/ppermute | solution.py:38
  25.0 4.9 %collective-permute-start.11 = (f32[56,128]{1,0:T(8,128)S(1)}, f32[56,128]{1,0:T(8,128)S(1)}, u32[]{:S(2)}, u32[]{:S(2)}) collective-permute-start(f32[56,128]{1,0:T(8,128)S(1)} %add_add_fusion.refs_0_), channel_id=1, source_target_pairs={{0,2},{1,3},{2,0},{3,1},{4,6},{5,7},{6,4},{7,5},{8,10},{9,11},{10,... | collective-permute-start | bytes 86024 | tf_op jit(solution)/shard_map/ppermute | solution.py:38
  28.4 1.5 %collective-permute-start.13 = (f32[56,128]{1,0:T(8,128)S(1)}, f32[56,128]{1,0:T(8,128)S(1)}, u32[]{:S(2)}, u32[]{:S(2)}) collective-permute-start(f32[56,128]{1,0:T(8,128)S(1)} %collective-permute-done.12.refs_2_), channel_id=1, source_target_pairs={{0,4},{1,5},{2,6},{3,7},{4,0},{5,1},{6,2},{7,3},{8,12},{9,13},{10,... | collective-permute-start | bytes 86024 | tf_op jit(solution)/shard_map/ppermute | solution.py:38
  28.4 1.5 %copy-start.3 = (f32[400,16]{0,1:T(8,128)S(1)}, f32[400,16]{0,1:T(8,128)}, u32[]{:S(2)}) copy-start(f32[400,16]{0,1:T(8,128)} %param.19) | copy-start | bytes 76804

commit v5 on v2

--- a/solution.py
+++ b/solution.py
@@ -122,16 +122,27 @@
     return lax.dot_general(a, b, dims, preferred_element_type=F32)
 
 
+def stacked(parts, dims, side):
+    return jnp.concatenate(parts, axis=dims[0][side][0])
+
+
 def dot_split(a, b, dims):
-    return dot(a[0], b[0], dims) + dot(a[0], b[1], dims) + dot(a[1], b[0], dims)
+    if a[0].shape[dims[0][0][0]] % 128:
+        return dot(a[0], b[0], dims) + dot(a[0], b[1], dims) + dot(a[1], b[0], dims)
+    left = stacked((a[0], a[0], a[1]), dims, 0)
+    return dot(left, stacked((b[0], b[1], b[0]), dims, 1), dims)
 
 
 def dot_left(a, b, dims):
-    return dot(a[0], b, dims) + dot(a[1], b, dims)
+    if a[0].shape[dims[0][0][0]] % 128:
+        return dot(a[0], b, dims) + dot(a[1], b, dims)
+    return dot(stacked(a, dims, 0), stacked((b, b), dims, 1), dims)
 
 
 def dot_right(a, b, dims):
-    return dot(a, b[0], dims) + dot(a, b[1], dims)
+    if b[0].shape[dims[0][1][0]] % 128:
+        return dot(a, b[0], dims) + dot(a, b[1], dims)
+    return dot(stacked((a, a), dims, 0), stacked(b, dims, 1), dims)
 
 
 def onehot(index, length):
@@ -174,29 +185,31 @@
     top_out, bottom_out, query_out, coef_out, product_out,
     src, src_state, dst, rel, rows, rels, counts, negs, sems,
 ):
-    pairs = [
-        (rows_hbm, rows), (rels_hbm, rels), (rel_hbm, rel), (counts_hbm, counts),
-        (negs_hbm, negs), (dst_hbm, dst), (src_hbm, src), (state_hbm, src_state),
+    features, columns = src.shape
+    small = [
+        (rows_hbm, rows), (rels_hbm, rels), (rel_hbm, rel), (counts_hbm, counts), (negs_hbm, negs),
     ]
+    slabs = [(dst_hbm, dst), (src_hbm, src)]
+    pairs = small + slabs + [(state_hbm, src_state)]
     copies = [pltpu.make_async_copy(a, b, sems.at[i]) for i, (a, b) in enumerate(pairs)]
-    for copy in copies:
+    for copy in copies[len(small) :] + copies[: len(small)]:
         copy.start()
-    for copy in copies[:5]:
+    for_dst, for_src, for_state = copies[len(small) :]
+    for copy in copies[: len(small)]:
         copy.wait()
-    features, columns = src.shape
     src_hot = as_bf16(onehot(rows[0, 0:1, :], columns))
     rel_cols = dot_left(halves(rel[...]), hot_relations(0, rels, rel.shape[0]), TN)
     scale, base = coefficient_parts(0, columns, rows, counts, negs)
-    copies[5].wait()
+    for_dst.wait()
     table_dst = halves(dst[...])
     table_rows = halves(dst[...].T)
-    copies[6].wait()
+    for_src.wait()
     src_cols = dot_left(halves(src[...]), src_hot, NN)
     query = src_cols * rel_cols
     coef = coefficients(halves(query), table_rows, scale, base)
     query_grad = dot_split(table_dst, halves(coef), NN)
     src_grad = dot_left(halves(query_grad * rel_cols), src_hot, NT)
-    copies[7].wait()
+    for_state.wait()
     table, state = row_step(src[...], src_state[...], src_grad)
     top, rest = top_out.shape[0], features - top_out.shape[0]
     top_out[...] = table[0:top, :]

time: 30.7 us -> 30.9 us (level)
  no operation moved by 1% of the time
where the time goes in v5:
time: 30.9 us; the launch traced here: 30.8 us
  starting transfers between devices  11.4 us (37%)
  waiting for transfers between devices  9.37 us (30%)
  Pallas kernels  8.55 us (28%)
  between operations  0.76 us (2%)
  local copies, waits for them, and re-layouts  0.69 us (2%)
    pallas_call x7, Pallas kernels, call(): pl.pallas_call(kernel, in_specs=in_specs, out_specs=[VMEM] * len(outs), o...  8.55 us
    ppermute x8, starting transfers between devices, sent(): return lax.ppermute(array, ('src', 'dst'), pairs)  6.21 us
    ppermute x8, waiting for transfers between devices, sent(): return lax.ppermute(array, ('src', 'dst'), pairs)  5.14 us
    ppermute x2, waiting for transfers between devices, passed_along(): lax.ppermute(array, axis, [(i, (i + by) % count) for i in range(count)])  4.23 us
    ppermute x2, starting transfers between devices, swapped(): lax.ppermute(array, axis, [(i, i ^ 1 << stride) for i in range(lax.axis_s...  3.54 us
    ppermute x2, starting transfers between devices, passed_along(): lax.ppermute(array, axis, [(i, (i + by) % count) for i in range(count)])  1.64 us
    unnamed x18, local copies, waits for them, and re-layouts  0.69 us
  transfers between devices with their start and end apart: 12, of which 7 were waited for; matrix products, arithmetic and copies ran while one was open for 0% of the time, Pallas kernels for 21%

profile of v5, /device:TPU:0, one launch (start us, length us, event | category | flops | bytes accessed | tf_op | source)
XLA Modules:
  0.0 30.8 jit_solution(13530656010505058108)
XLA Ops:
  0.6 3.1 %collective-permute-start.2 = (f32[400,256]{1,0:T(8,128)}, f32[400,256]{1,0:T(8,128)S(1)}, u32[]{:S(2)}, u32[]{:S(2)}) collective-permute-start(f32[400,256]{1,0:T(8,128)} %param.16), channel_id=1, source_target_pairs={{0,1},{1,0},{2,3},{3,2},{4,5},{5,4},{6,7},{7,6},{8,9},{9,8},{10,11... | collective-permute-start | bytes 1228808 | tf_op jit(solution)/shard_map/ppermute | solution.py:21
  3.7 3.5 %shard_map.179 = (f32[200,256]{1,0:T(8,128)S(1)}, f32[208,256]{1,0:T(8,128)S(1)}, f32[400,256]{1,0:T(8,128)S(1)}, f32[256,256]{1,0:T(8,128)S(1)}, f32[400,256]{1,0:T(8,128)S(1)}) custom-call(f32[400,256]{1,0:T(8,128)} %src_hbm.1, f32[1,256]{1,0:T(1,128)} %bitcast.21, f32[400,256]{1,0:T(8,128)} %dst.1, f32[16,400]{1,0:T(8,128)} %bitcast.11, ...), custom_call_target="tpu_custom_call" | custom-call | flops 20971520000 | bytes 856072 | tf_op jit(solution)/shard_map/pallas_call | solution.py:286
  7.2 0.1 collective-permute-start.1
  7.3 1.6 %collective-permute-start = (f32[200,256]{1,0:T(8,128)S(1)}, f32[200,256]{1,0:T(8,128)S(1)}, u32[]{:S(2)}, u32[]{:S(2)}) collective-permute-start(f32[200,256]{1,0:T(8,128)S(1)} %get-tuple-element.33), channel_id=1, source_target_pairs={{0,4},{4,8},{8,12},{12,16},{16,20},{20,24},{24,28},{28,0},{1,5},{5... | collective-permute-start | bytes 614408 | tf_op jit(solution)/shard_map/ppermute | solution.py:26
  9.0 0.6 %copy-done.2 = s32[2,2,256]{2,1,0:T(2,128)S(1)} copy-done((s32[2,2,256]{2,1,0:T(2,128)S(1)}, s32[2,2,256]{2,1,0:T(2,128)}, u32[]{:S(2)}) %copy-start.2) | copy-done | bytes 4120
  9.6 1.4 %shard_map.180 = (f32[400,256]{1,0:T(8,128)}, f32[1,256]{1,0:T(1,128)}, f32[16,400]{1,0:T(8,128)S(1)}, f32[400,256]{1,0:T(8,128)S(1)}, f32[256,256]{1,0:T(8,128)...) custom-call(f32[400,256]{1,0:T(8,128)S(1)} %copy-done, f32[1,256]{1,0:T(1,128)S(1)} %bitcast.15, ...), custom_call_target="tpu_custom_call" | custom-call | flops 157286400 | bytes 1528840 | tf_op jit(solution)/shard_map/pallas_call | solution.py:286
  11.0 0.4 %collective-permute-start.3 = (f32[1,256]{1,0:T(1,128)S(1)}, f32[1,256]{1,0:T(1,128)S(1)}, u32[]{:S(2)}, u32[]{:S(2)}) collective-permute-start(f32[1,256]{1,0:T(1,128)S(1)} %get-tuple-element.45), channel_id=1, source_target_pairs={{0,1},{1,0},{2,3},{3,2},{4,5},{5,4},{6,7},{7,6},{8,9},{9,8},{10,11... | collective-permute-start | bytes 3080 | tf_op jit(solution)/shard_map/ppermute | solution.py:21
  11.4 4.2 %collective-permute-done.top = f32[200,256]{1,0:T(8,128)S(1)} collective-permute-done((f32[200,256]{1,0:T(8,128)S(1)}, f32[200,256]{1,0:T(8,128)S(1)}, u32[]{:S(2)}, u32[]{:S(2)}) %collective-permute-start) | collective-permute-done | bytes 204832 | tf_op jit(solution)/shard_map/ppermute | solution.py:26
  15.7 0.3 shard_map.181
  16.0 1.2 %shard_map.182 = (f32[256,256]{1,0:T(8,128)S(1)}, f32[400,256]{1,0:T(8,128)S(1)}, f32[56,128]{1,0:T(8,128)S(1)}, f32[1,256]{1,0:T(1,128)S(1)}) custom-call(f32[400,256]{1,0:T(8,128)S(1)} %collective-permute-done.2.spare, f32[400,256]{1,0:T(8,128)S(1)} %get-tuple-element.39.src_cols, bf16[400,256]{1,0:T(8,128)(2,1)S(1)} %get-tuple-element.40.high, ...), custom_call_target="tpu_custom_call" | custom-call | flops 524288000 | bytes 2600960 | tf_op jit(solution)/shard_map/pallas_call | solution.py:286
  17.2 0.0 collective-permute-start.4
  17.3 0.7 %collective-permute-start.5 = (f32[56,128]{1,0:T(8,128)S(1)}, f32[56,128]{1,0:T(8,128)S(1)}, u32[]{:S(2)}, u32[]{:S(2)}) collective-permute-start(f32[56,128]{1,0:T(8,128)S(1)} %get-tuple-element.55), channel_id=1, source_target_pairs={{0,8},{1,9},{2,10},{3,11},{4,12},{5,13},{6,14},{7,15},{8,0},{9,1},... | collective-permute-start | bytes 86024 | tf_op jit(solution)/shard_map/ppermute | solution.py:36
  17.9 0.5 %collective-permute-done.4 = f32[56,128]{1,0:T(8,128)S(1)} collective-permute-done((f32[56,128]{1,0:T(8,128)S(1)}, f32[56,128]{1,0:T(8,128)S(1)}, u32[]{:S(2)}, u32[]{:S(2)}) %collective-permute-start.4) | collective-permute-done | bytes 28704 | tf_op jit(solution)/shard_map/ppermute | solution.py:36
  18.5 1.9 %collective-permute-start.8 = (f32[56,128]{1,0:T(8,128)S(1)}, f32[56,128]{1,0:T(8,128)S(1)}, u32[]{:S(2)}, u32[]{:S(2)}) collective-permute-start(f32[56,128]{1,0:T(8,128)S(1)} %add.12), channel_id=1, source_target_pairs={{0,24},{1,25},{2,26},{3,27},{4,28},{5,29},{6,30},{7,31},{8,16},{9,... | collective-permute-start | bytes 86024 | tf_op jit(solution)/shard_map/ppermute | solution.py:36
  20.4 0.5 %collective-permute-start.7 = (f32[56,128]{1,0:T(8,128)S(1)}, f32[56,128]{1,0:T(8,128)S(1)}, u32[]{:S(2)}, u32[]{:S(2)}) collective-permute-start(f32[56,128]{1,0:T(8,128)S(1)} %add.12), channel_id=1, source_target_pairs={{0,16},{1,17},{2,18},{3,19},{4,20},{5,21},{6,22},{7,23},{8,24},{9,... | collective-permute-start | bytes 86024 | tf_op jit(solution)/shard_map/ppermute | solution.py:36
  20.9 0.3 collective-permute-done.5
  21.2 2.1 %collective-permute-done.8.right = f32[56,128]{1,0:T(8,128)S(1)} collective-permute-done((f32[56,128]{1,0:T(8,128)S(1)}, f32[56,128]{1,0:T(8,128)S(1)}, u32[]{:S(2)}, u32[]{:S(2)}) %collective-permute-start.8) | collective-permute-done | bytes 28704 | tf_op jit(solution)/shard_map/ppermute | solution.py:36
  23.3 0.9 %collective-permute-done.7.left = f32[56,128]{1,0:T(8,128)S(1)} collective-permute-done((f32[56,128]{1,0:T(8,128)S(1)}, f32[56,128]{1,0:T(8,128)S(1)}, u32[]{:S(2)}, u32[]{:S(2)}) %collective-permute-start.7) | collective-permute-done | bytes 28704 | tf_op jit(solution)/shard_map/ppermute | solution.py:36
  24.3 0.5 %collective-permute-start.10 = (f32[56,128]{1,0:T(8,128)S(1)}, f32[56,128]{1,0:T(8,128)S(1)}, u32[]{:S(2)}, u32[]{:S(2)}) collective-permute-start(f32[56,128]{1,0:T(8,128)S(1)} %add_add_fusion.refs_0_), channel_id=1, source_target_pairs={{0,1},{1,0},{2,3},{3,2},{4,7},{5,6},{6,5},{7,4},{8,9},{9,8},{10,11... | collective-permute-start | bytes 86024 | tf_op jit(solution)/shard_map/ppermute | solution.py:36
  24.8 2.6 %collective-permute-start.9 = (f32[56,128]{1,0:T(8,128)S(1)}, f32[56,128]{1,0:T(8,128)S(1)}, u32[]{:S(2)}, u32[]{:S(2)}) collective-permute-start(f32[56,128]{1,0:T(8,128)S(1)} %add_add_fusion.refs_0_), channel_id=1, source_target_pairs={{0,2},{1,3},{2,0},{3,1},{4,6},{5,7},{6,4},{7,5},{8,10},{9,11},{10,... | collective-permute-start | bytes 86024 | tf_op jit(solution)/shard_map/ppermute | solution.py:36
  27.4 1.1 %collective-permute-done.10.refs_2_ = f32[56,128]{1,0:T(8,128)S(1)} collective-permute-done((f32[56,128]{1,0:T(8,128)S(1)}, f32[56,128]{1,0:T(8,128)S(1)}, u32[]{:S(2)}, u32[]{:S(2)}) %collective-permute-start.10) | collective-permute-done | bytes 28704 | tf_op jit(solution)/shard_map/ppermute | solution.py:36
  28.5 1.4 %shard_map.183 = (f32[400,256]{1,0:T(8,128)}, f32[1,256]{1,0:T(1,128)}, f32[400,256]{1,0:T(8,128)}, f32[1,256]{1,0:T(1,128)}) custom-call(f32[200,256]{1,0:T(8,128)S(1)} %collective-permute-done.top, f32[208,256]{1,0:T(8,128)S(1)} %collective-permute-done.1.bottom, f32[400,256]{1,0:T(8,128)S(1)} %collective-permute-done.2.spare, ...), custom_call_target="tpu_custom_call" | custom-call | flops 262144000 | bytes 2323456 | tf_op jit(solution)/shard_map/pallas_call | solution.py:286
  29.9 0.2 collective-permute-done.9.refs_1_
  30.1 0.7 %shard_map.185 = (f32[16,400]{1,0:T(8,128)}, f32[16,400]{1,0:T(8,128)}) custom-call(f32[16,400]{1,0:T(8,128)S(1)} %bitcast.13, f32[16,400]{1,0:T(8,128)S(1)} %bitcast.14, f32[56,128]{1,0:T(8,128)S(1)} %add_add_fusion.refs_0_, f32[56,128]{1,0:T(8,128)S(1)} %collective-permute-done.9.refs_1_, f32[56,128]{1,0:T(8,128)S(1)} %collective-permute-done.10.refs_2_, ...), custom_call_target="tpu_custom_call" | custom-call | flops 6400 | bytes 165888 | tf_op jit(solution)/shard_map/pallas_call | solution.py:286
  (27 shorter events, 0.1 us)
Async XLA Ops:
  0.6 15.3 %collective-permute-start.2 = (f32[400,256]{1,0:T(8,128)}, f32[400,256]{1,0:T(8,128)S(1)}, u32[]{:S(2)}, u32[]{:S(2)}) collective-permute-start(f32[400,256]{1,0:T(8,128)} %param.16), channel_id=1, source_target_pairs={{0,1},{1,0},{2,3},{3,2},{4,5},{5,4},{6,7},{7,6},{8,9},{9,8},{10,11... | collective-permute-start | bytes 1228808 | tf_op jit(solution)/shard_map/ppermute | solution.py:21
  3.7 5.2 %copy-start = (f32[400,256]{1,0:T(8,128)S(1)}, f32[400,256]{1,0:T(8,128)}, u32[]{:S(2)}) copy-start(f32[400,256]{1,0:T(8,128)} %dst.1) | copy-start | bytes 1228804
  3.7 5.2 %copy-start.1 = (f32[400,16]{0,1:T(8,128)S(1)}, f32[400,16]{0,1:T(8,128)}, u32[]{:S(2)}) copy-start(f32[400,16]{0,1:T(8,128)} %param.18) | copy-start | bytes 76804
  3.7 5.2 %copy-start.7 = (f32[256]{0:T(256)S(1)}, f32[256]{0:T(256)}, u32[]{:S(2)}) copy-start(f32[256]{0:T(256)} %param.17) | copy-start | bytes 3076
  3.7 5.2 %copy-start.8 = (s32[2,1]{0,1:T(1,128)S(1)}, s32[2,1]{0,1:T(1,128)}, u32[]{:S(2)}) copy-start(s32[2,1]{0,1:T(1,128)} %param.22) | copy-start | bytes 28
  7.2 8.4 %collective-permute-start.1 = (f32[208,256]{1,0:T(8,128)S(1)}, f32[208,256]{1,0:T(8,128)S(1)}, u32[]{:S(2)}, u32[]{:S(2)}) collective-permute-start(f32[208,256]{1,0:T(8,128)S(1)} %get-tuple-element.34), channel_id=1, source_target_pairs={{0,4},{4,8},{8,12},{12,16},{16,20},{20,24},{24,28},{28,0},{1,5},{5... | collective-permute-start | bytes 638984 | tf_op jit(solution)/shard_map/ppermute | solution.py:26
  7.3 1.6 %copy-start.5 = (s32[2,512]{1,0:T(2,128)S(1)}, s32[2,512]{1,0:T(2,128)}, u32[]{:S(2)}) copy-start(s32[2,512]{1,0:T(2,128)} %negs.1) | copy-start | bytes 12292
  7.3 8.3 %collective-permute-start = (f32[200,256]{1,0:T(8,128)S(1)}, f32[200,256]{1,0:T(8,128)S(1)}, u32[]{:S(2)}, u32[]{:S(2)}) collective-permute-start(f32[200,256]{1,0:T(8,128)S(1)} %get-tuple-element.33), channel_id=1, source_target_pairs={{0,4},{4,8},{8,12},{12,16},{16,20},{20,24},{24,28},{28,0},{1,5},{5... | collective-permute-start | bytes 614408 | tf_op jit(solution)/shard_map/ppermute | solution.py:26
  8.9 0.7 %copy-start.2 = (s32[2,2,256]{2,1,0:T(2,128)S(1)}, s32[2,2,256]{2,1,0:T(2,128)}, u32[]{:S(2)}) copy-start(s32[2,2,256]{2,1,0:T(2,128)} %rows.5) | copy-start | bytes 12292
  8.9 0.7 %copy-start.4 = (s32[2,256]{1,0:T(2,128)S(1)}, s32[2,256]{1,0:T(2,128)}, u32[]{:S(2)}) copy-start(s32[2,256]{1,0:T(2,128)} %rels.3) | copy-start | bytes 6148
  8.9 0.7 %copy-start.6 = (f32[256]{0:T(256)S(1)}, f32[256]{0:T(256)}, u32[]{:S(2)}) copy-start(f32[256]{0:T(256)} %param.15) | copy-start | bytes 3076
  11.0 5.0 %collective-permute-start.3 = (f32[1,256]{1,0:T(1,128)S(1)}, f32[1,256]{1,0:T(1,128)S(1)}, u32[]{:S(2)}, u32[]{:S(2)}) collective-permute-start(f32[1,256]{1,0:T(1,128)S(1)} %get-tuple-element.45), channel_id=1, source_target_pairs={{0,1},{1,0},{2,3},{3,2},{4,5},{5,4},{6,7},{7,6},{8,9},{9,8},{10,11... | collective-permute-start | bytes 3080 | tf_op jit(solution)/shard_map/ppermute | solution.py:21
  17.2 1.2 %collective-permute-start.4 = (f32[56,128]{1,0:T(8,128)S(1)}, f32[56,128]{1,0:T(8,128)S(1)}, u32[]{:S(2)}, u32[]{:S(2)}) collective-permute-start(f32[56,128]{1,0:T(8,128)S(1)} %get-tuple-element.55), channel_id=1, source_target_pairs={{0,4},{1,5},{2,6},{3,7},{4,0},{5,1},{6,2},{7,3},{8,12},{9,13},{10,... | collective-permute-start | bytes 86024 | tf_op jit(solution)/shard_map/ppermute | solution.py:36
  17.3 3.9 %collective-permute-start.5 = (f32[56,128]{1,0:T(8,128)S(1)}, f32[56,128]{1,0:T(8,128)S(1)}, u32[]{:S(2)}, u32[]{:S(2)}) collective-permute-start(f32[56,128]{1,0:T(8,128)S(1)} %get-tuple-element.55), channel_id=1, source_target_pairs={{0,8},{1,9},{2,10},{3,11},{4,12},{5,13},{6,14},{7,15},{8,0},{9,1},... | collective-permute-start | bytes 86024 | tf_op jit(solution)/shard_map/ppermute | solution.py:36
  18.5 4.9 %collective-permute-start.8 = (f32[56,128]{1,0:T(8,128)S(1)}, f32[56,128]{1,0:T(8,128)S(1)}, u32[]{:S(2)}, u32[]{:S(2)}) collective-permute-start(f32[56,128]{1,0:T(8,128)S(1)} %add.12), channel_id=1, source_target_pairs={{0,24},{1,25},{2,26},{3,27},{4,28},{5,29},{6,30},{7,31},{8,16},{9,... | collective-permute-start | bytes 86024 | tf_op jit(solution)/shard_map/ppermute | solution.py:36
  20.4 3.9 %collective-permute-start.7 = (f32[56,128]{1,0:T(8,128)S(1)}, f32[56,128]{1,0:T(8,128)S(1)}, u32[]{:S(2)}, u32[]{:S(2)}) collective-permute-start(f32[56,128]{1,0:T(8,128)S(1)} %add.12), channel_id=1, source_target_pairs={{0,16},{1,17},{2,18},{3,19},{4,20},{5,21},{6,22},{7,23},{8,24},{9,... | collective-permute-start | bytes 86024 | tf_op jit(solution)/shard_map/ppermute | solution.py:36
  21.2 3.1 %collective-permute-start.6 = (f32[56,128]{1,0:T(8,128)S(1)}, f32[56,128]{1,0:T(8,128)S(1)}, u32[]{:S(2)}, u32[]{:S(2)}) collective-permute-start(f32[56,128]{1,0:T(8,128)S(1)} %collective-permute-done.5), channel_id=1, source_target_pairs={{0,4},{1,5},{2,6},{3,7},{4,0},{5,1},{6,2},{7,3},{8,12},{9,13},{10,... | collective-permute-start | bytes 86024 | tf_op jit(solution)/shard_map/ppermute | solution.py:36
  24.3 4.2 %collective-permute-start.10 = (f32[56,128]{1,0:T(8,128)S(1)}, f32[56,128]{1,0:T(8,128)S(1)}, u32[]{:S(2)}, u32[]{:S(2)}) collective-permute-start(f32[56,128]{1,0:T(8,128)S(1)} %add_add_fusion.refs_0_), channel_id=1, source_target_pairs={{0,1},{1,0},{2,3},{3,2},{4,7},{5,6},{6,5},{7,4},{8,9},{9,8},{10,11... | collective-permute-start | bytes 86024 | tf_op jit(solution)/shard_map/ppermute | solution.py:36
  24.8 5.3 %collective-permute-start.9 = (f32[56,128]{1,0:T(8,128)S(1)}, f32[56,128]{1,0:T(8,128)S(1)}, u32[]{:S(2)}, u32[]{:S(2)}) collective-permute-start(f32[56,128]{1,0:T(8,128)S(1)} %add_add_fusion.refs_0_), channel_id=1, source_target_pairs={{0,2},{1,3},{2,0},{3,1},{4,6},{5,7},{6,4},{7,5},{8,10},{9,11},{10,... | collective-permute-start | bytes 86024 | tf_op jit(solution)/shard_map/ppermute | solution.py:36
  28.5 1.6 %collective-permute-start.11 = (f32[56,128]{1,0:T(8,128)S(1)}, f32[56,128]{1,0:T(8,128)S(1)}, u32[]{:S(2)}, u32[]{:S(2)}) collective-permute-start(f32[56,128]{1,0:T(8,128)S(1)} %collective-permute-done.10.refs_2_), channel_id=1, source_target_pairs={{0,4},{1,5},{2,6},{3,7},{4,0},{5,1},{6,2},{7,3},{8,12},{9,13},{10,... | collective-permute-start | bytes 86024 | tf_op jit(solution)/shard_map/ppermute | solution.py:36
  28.5 1.6 %copy-start.3 = (f32[400,16]{0,1:T(8,128)S(1)}, f32[400,16]{0,1:T(8,128)}, u32[]{:S(2)}) copy-start(f32[400,16]{0,1:T(8,128)} %param.19) | copy-start | bytes 76804

commit v6 on v5

--- a/solution.py
+++ b/solution.py
@@ -192,20 +192,20 @@
     slabs = [(dst_hbm, dst), (src_hbm, src)]
     pairs = small + slabs + [(state_hbm, src_state)]
     copies = [pltpu.make_async_copy(a, b, sems.at[i]) for i, (a, b) in enumerate(pairs)]
-    for copy in copies[len(small) :] + copies[: len(small)]:
+    for copy in copies:
         copy.start()
     for_dst, for_src, for_state = copies[len(small) :]
     for copy in copies[: len(small)]:
         copy.wait()
     src_hot = as_bf16(onehot(rows[0, 0:1, :], columns))
     rel_cols = dot_left(halves(rel[...]), hot_relations(0, rels, rel.shape[0]), TN)
-    scale, base = coefficient_parts(0, columns, rows, counts, negs)
     for_dst.wait()
+    for_src.wait()
     table_dst = halves(dst[...])
     table_rows = halves(dst[...].T)
-    for_src.wait()
     src_cols = dot_left(halves(src[...]), src_hot, NN)
     query = src_cols * rel_cols
+    scale, base = coefficient_parts(0, columns, rows, counts, negs)
     coef = coefficients(halves(query), table_rows, scale, base)
     query_grad = dot_split(table_dst, halves(coef), NN)
     src_grad = dot_left(halves(query_grad * rel_cols), src_hot, NT)

time: 30.9 us -> 30.4 us (0.984)
  Pallas kernels: 8.55 us -> 8.01 us
    pallas_call x7, Pallas kernels: 8.55 us -> 8.01 us  [call(): pl.pallas_call(kernel, in_specs=in_specs, out_specs=[VMEM] * len(outs), o...]
  transfers between devices with their start and end apart: 12 -> 12, of which waited for: 7 -> 7; matrix products, arithmetic and copies ran while one was open for 0% -> 0% of each run, Pallas kernels for 21% -> 20%
where the time goes in v6:
time: 30.4 us; the launch traced here: 30.2 us
  starting transfers between devices  11.4 us (38%)
  waiting for transfers between devices  9.38 us (31%)
  Pallas kernels  8.01 us (26%)
  between operations  0.76 us (2%)
  local copies, waits for them, and re-layouts  0.69 us (2%)
    pallas_call x7, Pallas kernels, call(): pl.pallas_call(kernel, in_specs=in_specs, out_specs=[VMEM] * len(outs), o...  8.01 us
    ppermute x8, starting transfers between devices, sent(): return lax.ppermute(array, ('src', 'dst'), pairs)  6.2 us
    ppermute x8, waiting for transfers between devices, sent(): return lax.ppermute(array, ('src', 'dst'), pairs)  5.15 us
    ppermute x2, waiting for transfers between devices, passed_along(): lax.ppermute(array, axis, [(i, (i + by) % count) for i in range(count)])  4.22 us
    ppermute x2, starting transfers between devices, swapped(): lax.ppermute(array, axis, [(i, i ^ 1 << stride) for i in range(lax.axis_s...  3.54 us
    ppermute x2, starting transfers between devices, passed_along(): lax.ppermute(array, axis, [(i, (i + by) % count) for i in range(count)])  1.64 us
    unnamed x18, local copies, waits for them, and re-layouts  0.69 us
  transfers between devices with their start and end apart: 12, of which 7 were waited for; matrix products, arithmetic and copies ran while one was open for 0% of the time, Pallas kernels for 20%

profile of v6, /device:TPU:0, one launch (start us, length us, event | category | flops | bytes accessed | tf_op | source)
XLA Modules:
  0.0 30.2 jit_solution(10645566757766273194)
XLA Ops:
  0.6 3.1 %collective-permute-start.2 = (f32[400,256]{1,0:T(8,128)}, f32[400,256]{1,0:T(8,128)S(1)}, u32[]{:S(2)}, u32[]{:S(2)}) collective-permute-start(f32[400,256]{1,0:T(8,128)} %param.16), channel_id=1, source_target_pairs={{0,1},{1,0},{2,3},{3,2},{4,5},{5,4},{6,7},{7,6},{8,9},{9,8},{10,11... | collective-permute-start | bytes 1228808 | tf_op jit(solution)/shard_map/ppermute | solution.py:21
  3.7 3.0 %shard_map.179 = (f32[200,256]{1,0:T(8,128)S(1)}, f32[208,256]{1,0:T(8,128)S(1)}, f32[400,256]{1,0:T(8,128)S(1)}, f32[256,256]{1,0:T(8,128)S(1)}, f32[400,256]{1,0:T(8,128)S(1)}) custom-call(f32[400,256]{1,0:T(8,128)} %src_hbm.1, f32[1,256]{1,0:T(1,128)} %bitcast.21, f32[400,256]{1,0:T(8,128)} %dst.1, f32[16,400]{1,0:T(8,128)} %bitcast.11, ...), custom_call_target="tpu_custom_call" | custom-call | flops 20971520000 | bytes 856072 | tf_op jit(solution)/shard_map/pallas_call | solution.py:286
  6.7 0.1 collective-permute-start.1
  6.8 1.6 %collective-permute-start = (f32[200,256]{1,0:T(8,128)S(1)}, f32[200,256]{1,0:T(8,128)S(1)}, u32[]{:S(2)}, u32[]{:S(2)}) collective-permute-start(f32[200,256]{1,0:T(8,128)S(1)} %get-tuple-element.33), channel_id=1, source_target_pairs={{0,4},{4,8},{8,12},{12,16},{16,20},{20,24},{24,28},{28,0},{1,5},{5... | collective-permute-start | bytes 614408 | tf_op jit(solution)/shard_map/ppermute | solution.py:26
  8.4 0.6 %copy-done.2 = s32[2,2,256]{2,1,0:T(2,128)S(1)} copy-done((s32[2,2,256]{2,1,0:T(2,128)S(1)}, s32[2,2,256]{2,1,0:T(2,128)}, u32[]{:S(2)}) %copy-start.2) | copy-done | bytes 4120
  9.1 1.4 %shard_map.180 = (f32[400,256]{1,0:T(8,128)}, f32[1,256]{1,0:T(1,128)}, f32[16,400]{1,0:T(8,128)S(1)}, f32[400,256]{1,0:T(8,128)S(1)}, f32[256,256]{1,0:T(8,128)...) custom-call(f32[400,256]{1,0:T(8,128)S(1)} %copy-done, f32[1,256]{1,0:T(1,128)S(1)} %bitcast.15, ...), custom_call_target="tpu_custom_call" | custom-call | flops 157286400 | bytes 1528840 | tf_op jit(solution)/shard_map/pallas_call | solution.py:286
  10.4 0.4 %collective-permute-start.3 = (f32[1,256]{1,0:T(1,128)S(1)}, f32[1,256]{1,0:T(1,128)S(1)}, u32[]{:S(2)}, u32[]{:S(2)}) collective-permute-start(f32[1,256]{1,0:T(1,128)S(1)} %get-tuple-element.45), channel_id=1, source_target_pairs={{0,1},{1,0},{2,3},{3,2},{4,5},{5,4},{6,7},{7,6},{8,9},{9,8},{10,11... | collective-permute-start | bytes 3080 | tf_op jit(solution)/shard_map/ppermute | solution.py:21
  10.9 4.2 %collective-permute-done.top = f32[200,256]{1,0:T(8,128)S(1)} collective-permute-done((f32[200,256]{1,0:T(8,128)S(1)}, f32[200,256]{1,0:T(8,128)S(1)}, u32[]{:S(2)}, u32[]{:S(2)}) %collective-permute-start) | collective-permute-done | bytes 204832 | tf_op jit(solution)/shard_map/ppermute | solution.py:26
  15.1 0.3 shard_map.181
  15.5 1.2 %shard_map.182 = (f32[256,256]{1,0:T(8,128)S(1)}, f32[400,256]{1,0:T(8,128)S(1)}, f32[56,128]{1,0:T(8,128)S(1)}, f32[1,256]{1,0:T(1,128)S(1)}) custom-call(f32[400,256]{1,0:T(8,128)S(1)} %collective-permute-done.2.spare, f32[400,256]{1,0:T(8,128)S(1)} %get-tuple-element.39.src_cols, bf16[400,256]{1,0:T(8,128)(2,1)S(1)} %get-tuple-element.40.high, ...), custom_call_target="tpu_custom_call" | custom-call | flops 524288000 | bytes 2600960 | tf_op jit(solution)/shard_map/pallas_call | solution.py:286
  16.7 0.0 collective-permute-start.4
  16.7 0.7 %collective-permute-start.5 = (f32[56,128]{1,0:T(8,128)S(1)}, f32[56,128]{1,0:T(8,128)S(1)}, u32[]{:S(2)}, u32[]{:S(2)}) collective-permute-start(f32[56,128]{1,0:T(8,128)S(1)} %get-tuple-element.55), channel_id=1, source_target_pairs={{0,8},{1,9},{2,10},{3,11},{4,12},{5,13},{6,14},{7,15},{8,0},{9,1},... | collective-permute-start | bytes 86024 | tf_op jit(solution)/shard_map/ppermute | solution.py:36
  17.4 0.5 %collective-permute-done.4 = f32[56,128]{1,0:T(8,128)S(1)} collective-permute-done((f32[56,128]{1,0:T(8,128)S(1)}, f32[56,128]{1,0:T(8,128)S(1)}, u32[]{:S(2)}, u32[]{:S(2)}) %collective-permute-start.4) | collective-permute-done | bytes 28704 | tf_op jit(solution)/shard_map/ppermute | solution.py:36
  17.9 1.9 %collective-permute-start.8 = (f32[56,128]{1,0:T(8,128)S(1)}, f32[56,128]{1,0:T(8,128)S(1)}, u32[]{:S(2)}, u32[]{:S(2)}) collective-permute-start(f32[56,128]{1,0:T(8,128)S(1)} %add.12), channel_id=1, source_target_pairs={{0,24},{1,25},{2,26},{3,27},{4,28},{5,29},{6,30},{7,31},{8,16},{9,... | collective-permute-start | bytes 86024 | tf_op jit(solution)/shard_map/ppermute | solution.py:36
  19.8 0.5 %collective-permute-start.7 = (f32[56,128]{1,0:T(8,128)S(1)}, f32[56,128]{1,0:T(8,128)S(1)}, u32[]{:S(2)}, u32[]{:S(2)}) collective-permute-start(f32[56,128]{1,0:T(8,128)S(1)} %add.12), channel_id=1, source_target_pairs={{0,16},{1,17},{2,18},{3,19},{4,20},{5,21},{6,22},{7,23},{8,24},{9,... | collective-permute-start | bytes 86024 | tf_op jit(solution)/shard_map/ppermute | solution.py:36
  20.4 0.3 %collective-permute-done.5 = f32[56,128]{1,0:T(8,128)S(1)} collective-permute-done((f32[56,128]{1,0:T(8,128)S(1)}, f32[56,128]{1,0:T(8,128)S(1)}, u32[]{:S(2)}, u32[]{:S(2)}) %collective-permute-start.5) | collective-permute-done | bytes 28704 | tf_op jit(solution)/shard_map/ppermute | solution.py:36
  20.7 2.1 %collective-permute-done.8.right = f32[56,128]{1,0:T(8,128)S(1)} collective-permute-done((f32[56,128]{1,0:T(8,128)S(1)}, f32[56,128]{1,0:T(8,128)S(1)}, u32[]{:S(2)}, u32[]{:S(2)}) %collective-permute-start.8) | collective-permute-done | bytes 28704 | tf_op jit(solution)/shard_map/ppermute | solution.py:36
  22.8 0.9 %collective-permute-done.7.left = f32[56,128]{1,0:T(8,128)S(1)} collective-permute-done((f32[56,128]{1,0:T(8,128)S(1)}, f32[56,128]{1,0:T(8,128)S(1)}, u32[]{:S(2)}, u32[]{:S(2)}) %collective-permute-start.7) | collective-permute-done | bytes 28704 | tf_op jit(solution)/shard_map/ppermute | solution.py:36
  23.7 0.5 %collective-permute-start.10 = (f32[56,128]{1,0:T(8,128)S(1)}, f32[56,128]{1,0:T(8,128)S(1)}, u32[]{:S(2)}, u32[]{:S(2)}) collective-permute-start(f32[56,128]{1,0:T(8,128)S(1)} %add_add_fusion.refs_0_), channel_id=1, source_target_pairs={{0,1},{1,0},{2,3},{3,2},{4,7},{5,6},{6,5},{7,4},{8,9},{9,8},{10,11... | collective-permute-start | bytes 86024 | tf_op jit(solution)/shard_map/ppermute | solution.py:36
  24.3 2.6 %collective-permute-start.9 = (f32[56,128]{1,0:T(8,128)S(1)}, f32[56,128]{1,0:T(8,128)S(1)}, u32[]{:S(2)}, u32[]{:S(2)}) collective-permute-start(f32[56,128]{1,0:T(8,128)S(1)} %add_add_fusion.refs_0_), channel_id=1, source_target_pairs={{0,2},{1,3},{2,0},{3,1},{4,6},{5,7},{6,4},{7,5},{8,10},{9,11},{10,... | collective-permute-start | bytes 86024 | tf_op jit(solution)/shard_map/ppermute | solution.py:36
  26.8 1.1 %collective-permute-done.10.refs_2_ = f32[56,128]{1,0:T(8,128)S(1)} collective-permute-done((f32[56,128]{1,0:T(8,128)S(1)}, f32[56,128]{1,0:T(8,128)S(1)}, u32[]{:S(2)}, u32[]{:S(2)}) %collective-permute-start.10) | collective-permute-done | bytes 28704 | tf_op jit(solution)/shard_map/ppermute | solution.py:36
  27.9 1.4 %shard_map.183 = (f32[400,256]{1,0:T(8,128)}, f32[1,256]{1,0:T(1,128)}, f32[400,256]{1,0:T(8,128)}, f32[1,256]{1,0:T(1,128)}) custom-call(f32[200,256]{1,0:T(8,128)S(1)} %collective-permute-done.top, f32[208,256]{1,0:T(8,128)S(1)} %collective-permute-done.1.bottom, f32[400,256]{1,0:T(8,128)S(1)} %collective-permute-done.2.spare, ...), custom_call_target="tpu_custom_call" | custom-call | flops 262144000 | bytes 2323456 | tf_op jit(solution)/shard_map/pallas_call | solution.py:286
  29.3 0.2 collective-permute-done.9.refs_1_
  29.5 0.7 %shard_map.185 = (f32[16,400]{1,0:T(8,128)}, f32[16,400]{1,0:T(8,128)}) custom-call(f32[16,400]{1,0:T(8,128)S(1)} %bitcast.13, f32[16,400]{1,0:T(8,128)S(1)} %bitcast.14, f32[56,128]{1,0:T(8,128)S(1)} %add_add_fusion.refs_0_, f32[56,128]{1,0:T(8,128)S(1)} %collective-permute-done.9.refs_1_, f32[56,128]{1,0:T(8,128)S(1)} %collective-permute-done.10.refs_2_, ...), custom_call_target="tpu_custom_call" | custom-call | flops 6400 | bytes 165888 | tf_op jit(solution)/shard_map/pallas_call | solution.py:286
  (27 shorter events, 0.1 us)
Async XLA Ops:
  0.6 14.8 %collective-permute-start.2 = (f32[400,256]{1,0:T(8,128)}, f32[400,256]{1,0:T(8,128)S(1)}, u32[]{:S(2)}, u32[]{:S(2)}) collective-permute-start(f32[400,256]{1,0:T(8,128)} %param.16), channel_id=1, source_target_pairs={{0,1},{1,0},{2,3},{3,2},{4,5},{5,4},{6,7},{7,6},{8,9},{9,8},{10,11... | collective-permute-start | bytes 1228808 | tf_op jit(solution)/shard_map/ppermute | solution.py:21
  3.7 4.6 %copy-start = (f32[400,256]{1,0:T(8,128)S(1)}, f32[400,256]{1,0:T(8,128)}, u32[]{:S(2)}) copy-start(f32[400,256]{1,0:T(8,128)} %dst.1) | copy-start | bytes 1228804
  3.7 4.7 %copy-start.1 = (f32[400,16]{0,1:T(8,128)S(1)}, f32[400,16]{0,1:T(8,128)}, u32[]{:S(2)}) copy-start(f32[400,16]{0,1:T(8,128)} %param.18) | copy-start | bytes 76804
  3.7 4.7 %copy-start.7 = (f32[256]{0:T(256)S(1)}, f32[256]{0:T(256)}, u32[]{:S(2)}) copy-start(f32[256]{0:T(256)} %param.17) | copy-start | bytes 3076
  3.7 4.7 %copy-start.8 = (s32[2,1]{0,1:T(1,128)S(1)}, s32[2,1]{0,1:T(1,128)}, u32[]{:S(2)}) copy-start(s32[2,1]{0,1:T(1,128)} %param.22) | copy-start | bytes 28
  6.7 8.4 %collective-permute-start.1 = (f32[208,256]{1,0:T(8,128)S(1)}, f32[208,256]{1,0:T(8,128)S(1)}, u32[]{:S(2)}, u32[]{:S(2)}) collective-permute-start(f32[208,256]{1,0:T(8,128)S(1)} %get-tuple-element.34), channel_id=1, source_target_pairs={{0,4},{4,8},{8,12},{12,16},{16,20},{20,24},{24,28},{28,0},{1,5},{5... | collective-permute-start | bytes 638984 | tf_op jit(solution)/shard_map/ppermute | solution.py:26
  6.8 1.6 %copy-start.5 = (s32[2,512]{1,0:T(2,128)S(1)}, s32[2,512]{1,0:T(2,128)}, u32[]{:S(2)}) copy-start(s32[2,512]{1,0:T(2,128)} %negs.1) | copy-start | bytes 12292
  6.8 8.3 %collective-permute-start = (f32[200,256]{1,0:T(8,128)S(1)}, f32[200,256]{1,0:T(8,128)S(1)}, u32[]{:S(2)}, u32[]{:S(2)}) collective-permute-start(f32[200,256]{1,0:T(8,128)S(1)} %get-tuple-element.33), channel_id=1, source_target_pairs={{0,4},{4,8},{8,12},{12,16},{16,20},{20,24},{24,28},{28,0},{1,5},{5... | collective-permute-start | bytes 614408 | tf_op jit(solution)/shard_map/ppermute | solution.py:26
  8.4 0.7 %copy-start.2 = (s32[2,2,256]{2,1,0:T(2,128)S(1)}, s32[2,2,256]{2,1,0:T(2,128)}, u32[]{:S(2)}) copy-start(s32[2,2,256]{2,1,0:T(2,128)} %rows.5) | copy-start | bytes 12292
  8.4 0.7 %copy-start.4 = (s32[2,256]{1,0:T(2,128)S(1)}, s32[2,256]{1,0:T(2,128)}, u32[]{:S(2)}) copy-start(s32[2,256]{1,0:T(2,128)} %rels.3) | copy-start | bytes 6148
  8.4 0.7 %copy-start.6 = (f32[256]{0:T(256)S(1)}, f32[256]{0:T(256)}, u32[]{:S(2)}) copy-start(f32[256]{0:T(256)} %param.15) | copy-start | bytes 3076
  10.4 5.0 %collective-permute-start.3 = (f32[1,256]{1,0:T(1,128)S(1)}, f32[1,256]{1,0:T(1,128)S(1)}, u32[]{:S(2)}, u32[]{:S(2)}) collective-permute-start(f32[1,256]{1,0:T(1,128)S(1)} %get-tuple-element.45), channel_id=1, source_target_pairs={{0,1},{1,0},{2,3},{3,2},{4,5},{5,4},{6,7},{7,6},{8,9},{9,8},{10,11... | collective-permute-start | bytes 3080 | tf_op jit(solution)/shard_map/ppermute | solution.py:21
  16.7 1.2 %collective-permute-start.4 = (f32[56,128]{1,0:T(8,128)S(1)}, f32[56,128]{1,0:T(8,128)S(1)}, u32[]{:S(2)}, u32[]{:S(2)}) collective-permute-start(f32[56,128]{1,0:T(8,128)S(1)} %get-tuple-element.55), channel_id=1, source_target_pairs={{0,4},{1,5},{2,6},{3,7},{4,0},{5,1},{6,2},{7,3},{8,12},{9,13},{10,... | collective-permute-start | bytes 86024 | tf_op jit(solution)/shard_map/ppermute | solution.py:36
  16.7 3.9 %collective-permute-start.5 = (f32[56,128]{1,0:T(8,128)S(1)}, f32[56,128]{1,0:T(8,128)S(1)}, u32[]{:S(2)}, u32[]{:S(2)}) collective-permute-start(f32[56,128]{1,0:T(8,128)S(1)} %get-tuple-element.55), channel_id=1, source_target_pairs={{0,8},{1,9},{2,10},{3,11},{4,12},{5,13},{6,14},{7,15},{8,0},{9,1},... | collective-permute-start | bytes 86024 | tf_op jit(solution)/shard_map/ppermute | solution.py:36
  17.9 4.9 %collective-permute-start.8 = (f32[56,128]{1,0:T(8,128)S(1)}, f32[56,128]{1,0:T(8,128)S(1)}, u32[]{:S(2)}, u32[]{:S(2)}) collective-permute-start(f32[56,128]{1,0:T(8,128)S(1)} %add.12), channel_id=1, source_target_pairs={{0,24},{1,25},{2,26},{3,27},{4,28},{5,29},{6,30},{7,31},{8,16},{9,... | collective-permute-start | bytes 86024 | tf_op jit(solution)/shard_map/ppermute | solution.py:36
  19.8 3.9 %collective-permute-start.7 = (f32[56,128]{1,0:T(8,128)S(1)}, f32[56,128]{1,0:T(8,128)S(1)}, u32[]{:S(2)}, u32[]{:S(2)}) collective-permute-start(f32[56,128]{1,0:T(8,128)S(1)} %add.12), channel_id=1, source_target_pairs={{0,16},{1,17},{2,18},{3,19},{4,20},{5,21},{6,22},{7,23},{8,24},{9,... | collective-permute-start | bytes 86024 | tf_op jit(solution)/shard_map/ppermute | solution.py:36
  20.7 3.1 %collective-permute-start.6 = (f32[56,128]{1,0:T(8,128)S(1)}, f32[56,128]{1,0:T(8,128)S(1)}, u32[]{:S(2)}, u32[]{:S(2)}) collective-permute-start(f32[56,128]{1,0:T(8,128)S(1)} %collective-permute-done.5), channel_id=1, source_target_pairs={{0,4},{1,5},{2,6},{3,7},{4,0},{5,1},{6,2},{7,3},{8,12},{9,13},{10,... | collective-permute-start | bytes 86024 | tf_op jit(solution)/shard_map/ppermute | solution.py:36
  23.7 4.2 %collective-permute-start.10 = (f32[56,128]{1,0:T(8,128)S(1)}, f32[56,128]{1,0:T(8,128)S(1)}, u32[]{:S(2)}, u32[]{:S(2)}) collective-permute-start(f32[56,128]{1,0:T(8,128)S(1)} %add_add_fusion.refs_0_), channel_id=1, source_target_pairs={{0,1},{1,0},{2,3},{3,2},{4,7},{5,6},{6,5},{7,4},{8,9},{9,8},{10,11... | collective-permute-start | bytes 86024 | tf_op jit(solution)/shard_map/ppermute | solution.py:36
  24.3 5.3 %collective-permute-start.9 = (f32[56,128]{1,0:T(8,128)S(1)}, f32[56,128]{1,0:T(8,128)S(1)}, u32[]{:S(2)}, u32[]{:S(2)}) collective-permute-start(f32[56,128]{1,0:T(8,128)S(1)} %add_add_fusion.refs_0_), channel_id=1, source_target_pairs={{0,2},{1,3},{2,0},{3,1},{4,6},{5,7},{6,4},{7,5},{8,10},{9,11},{10,... | collective-permute-start | bytes 86024 | tf_op jit(solution)/shard_map/ppermute | solution.py:36
  27.9 1.6 %collective-permute-start.11 = (f32[56,128]{1,0:T(8,128)S(1)}, f32[56,128]{1,0:T(8,128)S(1)}, u32[]{:S(2)}, u32[]{:S(2)}) collective-permute-start(f32[56,128]{1,0:T(8,128)S(1)} %collective-permute-done.10.refs_2_), channel_id=1, source_target_pairs={{0,4},{1,5},{2,6},{3,7},{4,0},{5,1},{6,2},{7,3},{8,12},{9,13},{10,... | collective-permute-start | bytes 86024 | tf_op jit(solution)/shard_map/ppermute | solution.py:36
  27.9 1.6 %copy-start.3 = (f32[400,16]{0,1:T(8,128)S(1)}, f32[400,16]{0,1:T(8,128)}, u32[]{:S(2)}) copy-start(f32[400,16]{0,1:T(8,128)} %param.19) | copy-start | bytes 76804

commit v7 on v6

--- a/solution.py
+++ b/solution.py
@@ -62,10 +62,8 @@
             one = sent(array, (flip(1), flip(1)))
             array = array + core_swapped(array)
             if radix == 4:
-                two = sent(array, (flip(2), flip(2)))
-                three = sent(array, (flip(3), flip(3)))
-                (late,) = call(add_kernel, [VMEM] * 2, [array.shape], 10**9, [two, three])
-                terms = ((array, one + core_swapped(one)), (late,))
+                rest = sent(array, (flip(2), flip(3)))
+                terms = ((array, one + core_swapped(one)), (rest, core_swapped(rest)))
             else:
                 terms = ((array,), (one + core_swapped(one),))
             continue
@@ -269,10 +267,6 @@
     spare_out[...], spare_acc[...] = row_step(spare[...], spare_state[...], spare_grad)
 
 
-def add_kernel(left, right, out):
-    out[...] = left[...] + right[...]
-
-
 def relation_kernel(rel, rel_state, *refs):
     terms, (rel_out, state_out) = refs[:-2], refs[-2:]
     total = unpack(tree_sum([term[...] for term in terms]), *rel.shape)

time: 30.4 us -> 30.4 us (level)
    pallas_call x7 -> x6, Pallas kernels: 8.01 us -> 8.01 us  [call(): pl.pallas_call(kernel, in_specs=in_specs, out_specs=[VMEM] * len(outs), o...]
  transfers between devices with their start and end apart: 12 -> 12, of which waited for: 7 -> 6; matrix products, arithmetic and copies ran while one was open for 0% -> 0% of each run, Pallas kernels for 20% -> 20%
where the time goes in v7:
time: 30.4 us; the launch traced here: 30.3 us
  starting transfers between devices  11.3 us (37%)
  waiting for transfers between devices  9.47 us (31%)
  Pallas kernels  8.01 us (26%)
  between operations  0.76 us (2%)
  local copies, waits for them, and re-layouts  0.69 us (2%)
    pallas_call x6, Pallas kernels, call(): pl.pallas_call(kernel, in_specs=in_specs, out_specs=[VMEM] * len(outs), o...  8.01 us
    ppermute x8, starting transfers between devices, sent(): return lax.ppermute(array, ('src', 'dst'), pairs)  6.14 us
    ppermute x8, waiting for transfers between devices, sent(): return lax.ppermute(array, ('src', 'dst'), pairs)  5.24 us
    ppermute x2, waiting for transfers between devices, passed_along(): lax.ppermute(array, axis, [(i, (i + by) % count) for i in range(count)])  4.22 us
    ppermute x2, starting transfers between devices, swapped(): lax.ppermute(array, axis, [(i, i ^ 1 << stride) for i in range(lax.axis_s...  3.54 us
    ppermute x2, starting transfers between devices, passed_along(): lax.ppermute(array, axis, [(i, (i + by) % count) for i in range(count)])  1.64 us
    unnamed x18, local copies, waits for them, and re-layouts  0.69 us
  transfers between devices with their start and end apart: 12, of which 6 were waited for; matrix products, arithmetic and copies ran while one was open for 0% of the time, Pallas kernels for 20%

profile of v7, /device:TPU:0, one launch (start us, length us, event | category | flops | bytes accessed | tf_op | source)
XLA Modules:
  0.0 30.3 jit_solution(1829650442717707471)
XLA Ops:
  0.6 3.1 %collective-permute-start.2 = (f32[400,256]{1,0:T(8,128)}, f32[400,256]{1,0:T(8,128)S(1)}, u32[]{:S(2)}, u32[]{:S(2)}) collective-permute-start(f32[400,256]{1,0:T(8,128)} %param.16), channel_id=1, source_target_pairs={{0,1},{1,0},{2,3},{3,2},{4,5},{5,4},{6,7},{7,6},{8,9},{9,8},{10,11... | collective-permute-start | bytes 1228808 | tf_op jit(solution)/shard_map/ppermute | solution.py:21
  3.7 3.0 %shard_map.179 = (f32[200,256]{1,0:T(8,128)S(1)}, f32[208,256]{1,0:T(8,128)S(1)}, f32[400,256]{1,0:T(8,128)S(1)}, f32[256,256]{1,0:T(8,128)S(1)}, f32[400,256]{1,0:T(8,128)S(1)}) custom-call(f32[400,256]{1,0:T(8,128)} %src_hbm.1, f32[1,256]{1,0:T(1,128)} %bitcast.21, f32[400,256]{1,0:T(8,128)} %dst.1, f32[16,400]{1,0:T(8,128)} %bitcast.11, ...), custom_call_target="tpu_custom_call" | custom-call | flops 20971520000 | bytes 856072 | tf_op jit(solution)/shard_map/pallas_call | solution.py:280
  6.7 0.1 collective-permute-start.1
  6.8 1.6 %collective-permute-start = (f32[200,256]{1,0:T(8,128)S(1)}, f32[200,256]{1,0:T(8,128)S(1)}, u32[]{:S(2)}, u32[]{:S(2)}) collective-permute-start(f32[200,256]{1,0:T(8,128)S(1)} %get-tuple-element.33), channel_id=1, source_target_pairs={{0,4},{4,8},{8,12},{12,16},{16,20},{20,24},{24,28},{28,0},{1,5},{5... | collective-permute-start | bytes 614408 | tf_op jit(solution)/shard_map/ppermute | solution.py:26
  8.4 0.6 %copy-done.2 = s32[2,2,256]{2,1,0:T(2,128)S(1)} copy-done((s32[2,2,256]{2,1,0:T(2,128)S(1)}, s32[2,2,256]{2,1,0:T(2,128)}, u32[]{:S(2)}) %copy-start.2) | copy-done | bytes 4120
  9.1 0.0 copy-done.6
  9.1 1.4 %shard_map.180 = (f32[400,256]{1,0:T(8,128)}, f32[1,256]{1,0:T(1,128)}, f32[16,400]{1,0:T(8,128)S(1)}, f32[400,256]{1,0:T(8,128)S(1)}, f32[256,256]{1,0:T(8,128)...) custom-call(f32[400,256]{1,0:T(8,128)S(1)} %copy-done, f32[1,256]{1,0:T(1,128)S(1)} %bitcast.15, ...), custom_call_target="tpu_custom_call" | custom-call | flops 157286400 | bytes 1528840 | tf_op jit(solution)/shard_map/pallas_call | solution.py:280
  10.4 0.4 %collective-permute-start.3 = (f32[1,256]{1,0:T(1,128)S(1)}, f32[1,256]{1,0:T(1,128)S(1)}, u32[]{:S(2)}, u32[]{:S(2)}) collective-permute-start(f32[1,256]{1,0:T(1,128)S(1)} %get-tuple-element.45), channel_id=1, source_target_pairs={{0,1},{1,0},{2,3},{3,2},{4,5},{5,4},{6,7},{7,6},{8,9},{9,8},{10,11... | collective-permute-start | bytes 3080 | tf_op jit(solution)/shard_map/ppermute | solution.py:21
  10.9 4.2 %collective-permute-done.top = f32[200,256]{1,0:T(8,128)S(1)} collective-permute-done((f32[200,256]{1,0:T(8,128)S(1)}, f32[200,256]{1,0:T(8,128)S(1)}, u32[]{:S(2)}, u32[]{:S(2)}) %collective-permute-start) | collective-permute-done | bytes 204832 | tf_op jit(solution)/shard_map/ppermute | solution.py:26
  15.1 0.3 shard_map.181
  15.5 1.2 %shard_map.182 = (f32[256,256]{1,0:T(8,128)S(1)}, f32[400,256]{1,0:T(8,128)S(1)}, f32[56,128]{1,0:T(8,128)S(1)}, f32[1,256]{1,0:T(1,128)S(1)}) custom-call(f32[400,256]{1,0:T(8,128)S(1)} %collective-permute-done.2.spare, f32[400,256]{1,0:T(8,128)S(1)} %get-tuple-element.39.src_cols, bf16[400,256]{1,0:T(8,128)(2,1)S(1)} %get-tuple-element.40.high, ...), custom_call_target="tpu_custom_call" | custom-call | flops 524288000 | bytes 2600960 | tf_op jit(solution)/shard_map/pallas_call | solution.py:280
  16.7 0.0 collective-permute-start.4
  16.7 0.7 %collective-permute-start.5 = (f32[56,128]{1,0:T(8,128)S(1)}, f32[56,128]{1,0:T(8,128)S(1)}, u32[]{:S(2)}, u32[]{:S(2)}) collective-permute-start(f32[56,128]{1,0:T(8,128)S(1)} %get-tuple-element.55), channel_id=1, source_target_pairs={{0,8},{1,9},{2,10},{3,11},{4,12},{5,13},{6,14},{7,15},{8,0},{9,1},... | collective-permute-start | bytes 86024 | tf_op jit(solution)/shard_map/ppermute | solution.py:36
  17.4 0.5 %collective-permute-done.4 = f32[56,128]{1,0:T(8,128)S(1)} collective-permute-done((f32[56,128]{1,0:T(8,128)S(1)}, f32[56,128]{1,0:T(8,128)S(1)}, u32[]{:S(2)}, u32[]{:S(2)}) %collective-permute-start.4) | collective-permute-done | bytes 28704 | tf_op jit(solution)/shard_map/ppermute | solution.py:36
  17.9 1.5 %collective-permute-start.7 = (f32[56,128]{1,0:T(8,128)S(1)}, f32[56,128]{1,0:T(8,128)S(1)}, u32[]{:S(2)}, u32[]{:S(2)}) collective-permute-start(f32[56,128]{1,0:T(8,128)S(1)} %add.15), channel_id=1, source_target_pairs={{0,16},{1,17},{2,18},{3,19},{4,28},{5,29},{6,30},{7,31},{8,24},{9,... | collective-permute-start | bytes 86024 | tf_op jit(solution)/shard_map/ppermute | solution.py:36
  19.4 1.2 %collective-permute-done.5 = f32[56,128]{1,0:T(8,128)S(1)} collective-permute-done((f32[56,128]{1,0:T(8,128)S(1)}, f32[56,128]{1,0:T(8,128)S(1)}, u32[]{:S(2)}, u32[]{:S(2)}) %collective-permute-start.5) | collective-permute-done | bytes 28704 | tf_op jit(solution)/shard_map/ppermute | solution.py:36
  20.7 1.4 %collective-permute-done.7 = f32[56,128]{1,0:T(8,128)S(1)} collective-permute-done((f32[56,128]{1,0:T(8,128)S(1)}, f32[56,128]{1,0:T(8,128)S(1)}, u32[]{:S(2)}, u32[]{:S(2)}) %collective-permute-start.7) | collective-permute-done | bytes 28704 | tf_op jit(solution)/shard_map/ppermute | solution.py:36
  22.1 1.2 %collective-permute-done.8 = f32[56,128]{1,0:T(8,128)S(1)} collective-permute-done((f32[56,128]{1,0:T(8,128)S(1)}, f32[56,128]{1,0:T(8,128)S(1)}, u32[]{:S(2)}, u32[]{:S(2)}) %collective-permute-start.8) | collective-permute-done | bytes 28704 | tf_op jit(solution)/shard_map/ppermute | solution.py:36
  23.3 0.1 collective-permute-start.10
  23.5 3.0 %collective-permute-start.9 = (f32[56,128]{1,0:T(8,128)S(1)}, f32[56,128]{1,0:T(8,128)S(1)}, u32[]{:S(2)}, u32[]{:S(2)}) collective-permute-start(f32[56,128]{1,0:T(8,128)S(1)} %add_add_fusion.refs_0_), channel_id=1, source_target_pairs={{0,2},{1,3},{2,0},{3,1},{4,6},{5,7},{6,4},{7,5},{8,10},{9,11},{10,... | collective-permute-start | bytes 86024 | tf_op jit(solution)/shard_map/ppermute | solution.py:36
  26.4 0.8 %collective-permute-done.10.refs_2_ = f32[56,128]{1,0:T(8,128)S(1)} collective-permute-done((f32[56,128]{1,0:T(8,128)S(1)}, f32[56,128]{1,0:T(8,128)S(1)}, u32[]{:S(2)}, u32[]{:S(2)}) %collective-permute-start.10) | collective-permute-done | bytes 28704 | tf_op jit(solution)/shard_map/ppermute | solution.py:36
  27.3 0.8 %collective-permute-start.11 = (f32[56,128]{1,0:T(8,128)S(1)}, f32[56,128]{1,0:T(8,128)S(1)}, u32[]{:S(2)}, u32[]{:S(2)}) collective-permute-start(f32[56,128]{1,0:T(8,128)S(1)} %collective-permute-done.10.refs_2_), channel_id=1, source_target_pairs={{0,4},{1,5},{2,6},{3,7},{4,0},{5,1},{6,2},{7,3},{8,12},{9,13},{10,... | collective-permute-start | bytes 86024 | tf_op jit(solution)/shard_map/ppermute | solution.py:36
  28.1 1.4 %shard_map.183 = (f32[400,256]{1,0:T(8,128)}, f32[1,256]{1,0:T(1,128)}, f32[400,256]{1,0:T(8,128)}, f32[1,256]{1,0:T(1,128)}) custom-call(f32[200,256]{1,0:T(8,128)S(1)} %collective-permute-done.top, f32[208,256]{1,0:T(8,128)S(1)} %collective-permute-done.1.bottom, f32[400,256]{1,0:T(8,128)S(1)} %collective-permute-done.2.spare, ...), custom_call_target="tpu_custom_call" | custom-call | flops 262144000 | bytes 2323456 | tf_op jit(solution)/shard_map/pallas_call | solution.py:280
  29.5 0.7 %shard_map.184 = (f32[16,400]{1,0:T(8,128)}, f32[16,400]{1,0:T(8,128)}) custom-call(f32[16,400]{1,0:T(8,128)S(1)} %bitcast.13, f32[16,400]{1,0:T(8,128)S(1)} %bitcast.14, f32[56,128]{1,0:T(8,128)S(1)} %add_add_fusion.refs_0_, f32[56,128]{1,0:T(8,128)S(1)} %collective-permute-done.9.refs_1_, f32[56,128]{1,0:T(8,128)S(1)} %collective-permute-done.10.refs_2_, ...), custom_call_target="tpu_custom_call" | custom-call | flops 6400 | bytes 165888 | tf_op jit(solution)/shard_map/pallas_call | solution.py:280
  (26 shorter events, 0.1 us)
Async XLA Ops:
  0.6 14.8 %collective-permute-start.2 = (f32[400,256]{1,0:T(8,128)}, f32[400,256]{1,0:T(8,128)S(1)}, u32[]{:S(2)}, u32[]{:S(2)}) collective-permute-start(f32[400,256]{1,0:T(8,128)} %param.16), channel_id=1, source_target_pairs={{0,1},{1,0},{2,3},{3,2},{4,5},{5,4},{6,7},{7,6},{8,9},{9,8},{10,11... | collective-permute-start | bytes 1228808 | tf_op jit(solution)/shard_map/ppermute | solution.py:21
  3.7 4.6 %copy-start = (f32[400,256]{1,0:T(8,128)S(1)}, f32[400,256]{1,0:T(8,128)}, u32[]{:S(2)}) copy-start(f32[400,256]{1,0:T(8,128)} %dst.1) | copy-start | bytes 1228804
  3.7 4.7 %copy-start.1 = (f32[400,16]{0,1:T(8,128)S(1)}, f32[400,16]{0,1:T(8,128)}, u32[]{:S(2)}) copy-start(f32[400,16]{0,1:T(8,128)} %param.18) | copy-start | bytes 76804
  3.7 4.7 %copy-start.7 = (f32[256]{0:T(256)S(1)}, f32[256]{0:T(256)}, u32[]{:S(2)}) copy-start(f32[256]{0:T(256)} %param.17) | copy-start | bytes 3076
  3.7 4.7 %copy-start.8 = (s32[2,1]{0,1:T(1,128)S(1)}, s32[2,1]{0,1:T(1,128)}, u32[]{:S(2)}) copy-start(s32[2,1]{0,1:T(1,128)} %param.22) | copy-start | bytes 28
  6.7 8.4 %collective-permute-start.1 = (f32[208,256]{1,0:T(8,128)S(1)}, f32[208,256]{1,0:T(8,128)S(1)}, u32[]{:S(2)}, u32[]{:S(2)}) collective-permute-start(f32[208,256]{1,0:T(8,128)S(1)} %get-tuple-element.34), channel_id=1, source_target_pairs={{0,4},{4,8},{8,12},{12,16},{16,20},{20,24},{24,28},{28,0},{1,5},{5... | collective-permute-start | bytes 638984 | tf_op jit(solution)/shard_map/ppermute | solution.py:26
  6.8 1.6 %copy-start.5 = (s32[2,512]{1,0:T(2,128)S(1)}, s32[2,512]{1,0:T(2,128)}, u32[]{:S(2)}) copy-start(s32[2,512]{1,0:T(2,128)} %negs.1) | copy-start | bytes 12292
  6.8 8.3 %collective-permute-start = (f32[200,256]{1,0:T(8,128)S(1)}, f32[200,256]{1,0:T(8,128)S(1)}, u32[]{:S(2)}, u32[]{:S(2)}) collective-permute-start(f32[200,256]{1,0:T(8,128)S(1)} %get-tuple-element.33), channel_id=1, source_target_pairs={{0,4},{4,8},{8,12},{12,16},{16,20},{20,24},{24,28},{28,0},{1,5},{5... | collective-permute-start | bytes 614408 | tf_op jit(solution)/shard_map/ppermute | solution.py:26
  8.4 0.7 %copy-start.2 = (s32[2,2,256]{2,1,0:T(2,128)S(1)}, s32[2,2,256]{2,1,0:T(2,128)}, u32[]{:S(2)}) copy-start(s32[2,2,256]{2,1,0:T(2,128)} %rows.5) | copy-start | bytes 12292
  8.4 0.7 %copy-start.4 = (s32[2,256]{1,0:T(2,128)S(1)}, s32[2,256]{1,0:T(2,128)}, u32[]{:S(2)}) copy-start(s32[2,256]{1,0:T(2,128)} %rels.3) | copy-start | bytes 6148
  8.4 0.7 %copy-start.6 = (f32[256]{0:T(256)S(1)}, f32[256]{0:T(256)}, u32[]{:S(2)}) copy-start(f32[256]{0:T(256)} %param.15) | copy-start | bytes 3076
  10.4 5.0 %collective-permute-start.3 = (f32[1,256]{1,0:T(1,128)S(1)}, f32[1,256]{1,0:T(1,128)S(1)}, u32[]{:S(2)}, u32[]{:S(2)}) collective-permute-start(f32[1,256]{1,0:T(1,128)S(1)} %get-tuple-element.45), channel_id=1, source_target_pairs={{0,1},{1,0},{2,3},{3,2},{4,5},{5,4},{6,7},{7,6},{8,9},{9,8},{10,11... | collective-permute-start | bytes 3080 | tf_op jit(solution)/shard_map/ppermute | solution.py:21
  16.7 1.2 %collective-permute-start.4 = (f32[56,128]{1,0:T(8,128)S(1)}, f32[56,128]{1,0:T(8,128)S(1)}, u32[]{:S(2)}, u32[]{:S(2)}) collective-permute-start(f32[56,128]{1,0:T(8,128)S(1)} %get-tuple-element.55), channel_id=1, source_target_pairs={{0,4},{1,5},{2,6},{3,7},{4,0},{5,1},{6,2},{7,3},{8,12},{9,13},{10,... | collective-permute-start | bytes 86024 | tf_op jit(solution)/shard_map/ppermute | solution.py:36
  16.7 3.9 %collective-permute-start.5 = (f32[56,128]{1,0:T(8,128)S(1)}, f32[56,128]{1,0:T(8,128)S(1)}, u32[]{:S(2)}, u32[]{:S(2)}) collective-permute-start(f32[56,128]{1,0:T(8,128)S(1)} %get-tuple-element.55), channel_id=1, source_target_pairs={{0,8},{1,9},{2,10},{3,11},{4,12},{5,13},{6,14},{7,15},{8,0},{9,1},... | collective-permute-start | bytes 86024 | tf_op jit(solution)/shard_map/ppermute | solution.py:36
  17.9 4.2 %collective-permute-start.7 = (f32[56,128]{1,0:T(8,128)S(1)}, f32[56,128]{1,0:T(8,128)S(1)}, u32[]{:S(2)}, u32[]{:S(2)}) collective-permute-start(f32[56,128]{1,0:T(8,128)S(1)} %add.15), channel_id=1, source_target_pairs={{0,16},{1,17},{2,18},{3,19},{4,28},{5,29},{6,30},{7,31},{8,24},{9,... | collective-permute-start | bytes 86024 | tf_op jit(solution)/shard_map/ppermute | solution.py:36
  20.7 1.5 %collective-permute-start.6 = (f32[56,128]{1,0:T(8,128)S(1)}, f32[56,128]{1,0:T(8,128)S(1)}, u32[]{:S(2)}, u32[]{:S(2)}) collective-permute-start(f32[56,128]{1,0:T(8,128)S(1)} %collective-permute-done.5), channel_id=1, source_target_pairs={{0,4},{1,5},{2,6},{3,7},{4,0},{5,1},{6,2},{7,3},{8,12},{9,13},{10,... | collective-permute-start | bytes 86024 | tf_op jit(solution)/shard_map/ppermute | solution.py:36
  22.1 1.2 %collective-permute-start.8 = (f32[56,128]{1,0:T(8,128)S(1)}, f32[56,128]{1,0:T(8,128)S(1)}, u32[]{:S(2)}, u32[]{:S(2)}) collective-permute-start(f32[56,128]{1,0:T(8,128)S(1)} %collective-permute-done.7), channel_id=1, source_target_pairs={{0,4},{1,5},{2,6},{3,7},{4,0},{5,1},{6,2},{7,3},{8,12},{9,13},{10,... | collective-permute-start | bytes 86024 | tf_op jit(solution)/shard_map/ppermute | solution.py:36
  23.3 3.9 %collective-permute-start.10 = (f32[56,128]{1,0:T(8,128)S(1)}, f32[56,128]{1,0:T(8,128)S(1)}, u32[]{:S(2)}, u32[]{:S(2)}) collective-permute-start(f32[56,128]{1,0:T(8,128)S(1)} %add_add_fusion.refs_0_), channel_id=1, source_target_pairs={{0,1},{1,0},{2,3},{3,2},{4,7},{5,6},{6,5},{7,4},{8,9},{9,8},{10,11... | collective-permute-start | bytes 86024 | tf_op jit(solution)/shard_map/ppermute | solution.py:36
  23.5 6.1 %collective-permute-start.9 = (f32[56,128]{1,0:T(8,128)S(1)}, f32[56,128]{1,0:T(8,128)S(1)}, u32[]{:S(2)}, u32[]{:S(2)}) collective-permute-start(f32[56,128]{1,0:T(8,128)S(1)} %add_add_fusion.refs_0_), channel_id=1, source_target_pairs={{0,2},{1,3},{2,0},{3,1},{4,6},{5,7},{6,4},{7,5},{8,10},{9,11},{10,... | collective-permute-start | bytes 86024 | tf_op jit(solution)/shard_map/ppermute | solution.py:36
  27.3 2.3 %collective-permute-start.11 = (f32[56,128]{1,0:T(8,128)S(1)}, f32[56,128]{1,0:T(8,128)S(1)}, u32[]{:S(2)}, u32[]{:S(2)}) collective-permute-start(f32[56,128]{1,0:T(8,128)S(1)} %collective-permute-done.10.refs_2_), channel_id=1, source_target_pairs={{0,4},{1,5},{2,6},{3,7},{4,0},{5,1},{6,2},{7,3},{8,12},{9,13},{10,... | collective-permute-start | bytes 86024 | tf_op jit(solution)/shard_map/ppermute | solution.py:36
  28.1 1.4 %copy-start.3 = (f32[400,16]{0,1:T(8,128)S(1)}, f32[400,16]{0,1:T(8,128)}, u32[]{:S(2)}) copy-start(f32[400,16]{0,1:T(8,128)} %param.19) | copy-start | bytes 76804

commit v8 on v6

--- a/solution.py
+++ b/solution.py
@@ -173,7 +173,7 @@
 
 def row_step(table, state, gradient):
     new_state = state + jnp.sum(gradient * gradient, axis=0, keepdims=True) * (1.0 / table.shape[0])
-    return table - gradient * (ROW_RATE / jnp.sqrt(new_state)), new_state
+    return table - gradient * (ROW_RATE * lax.rsqrt(new_state)), new_state
 
 
 def hot_relations(round_id, edge_rel, rels):
@@ -189,18 +189,20 @@
     small = [
         (rows_hbm, rows), (rels_hbm, rels), (rel_hbm, rel), (counts_hbm, counts), (negs_hbm, negs),
     ]
-    slabs = [(dst_hbm, dst), (src_hbm, src)]
+    half = features // 32 * 16
+    halves_of = [pl.ds(0, half), pl.ds(half, features - half)]
+    slabs = [(whole.at[c], part.at[c]) for whole, part in ((dst_hbm, dst), (src_hbm, src)) for c in halves_of]
     pairs = small + slabs + [(state_hbm, src_state)]
     copies = [pltpu.make_async_copy(a, b, sems.at[i]) for i, (a, b) in enumerate(pairs)]
     for copy in copies:
         copy.start()
-    for_dst, for_src, for_state = copies[len(small) :]
+    *for_slabs, for_state = copies[len(small) :]
     for copy in copies[: len(small)]:
         copy.wait()
     src_hot = as_bf16(onehot(rows[0, 0:1, :], columns))
     rel_cols = dot_left(halves(rel[...]), hot_relations(0, rels, rel.shape[0]), TN)
-    for_dst.wait()
-    for_src.wait()
+    for copy in for_slabs:
+        copy.wait()
     table_dst = halves(dst[...])
     table_rows = halves(dst[...].T)
     src_cols = dot_left(halves(src[...]), src_hot, NN)
@@ -331,7 +333,7 @@
         400 * work,
         [pltpu.with_memory_space_constraint(a, pltpu.HBM) for a in operands],
         [pltpu.VMEM(a.shape, a.dtype) for a in operands]
-        + [pltpu.SemaphoreType.DMA((len(operands),))],
+        + [pltpu.SemaphoreType.DMA((len(operands) + 2,))],
     )
     top, bottom = passed_along((top, bottom), "src", 1)
     dst_next, dst_acc, rel_first, rel_cols, scale, base, spare_acc = call(

time: 30.4 us -> 30.5 us (level)
  no operation moved by 1% of the time
where the time goes in v8:
time: 30.5 us; the launch traced here: 30.3 us
  starting transfers between devices  11.4 us (37%)
  waiting for transfers between devices  9.37 us (31%)
  Pallas kernels  8.12 us (27%)
  between operations  0.76 us (2%)
  local copies, waits for them, and re-layouts  0.69 us (2%)
    pallas_call x7, Pallas kernels, call(): pl.pallas_call(kernel, in_specs=in_specs, out_specs=[VMEM] * len(outs), o...  8.12 us
    ppermute x8, starting transfers between devices, sent(): return lax.ppermute(array, ('src', 'dst'), pairs)  6.21 us
    ppermute x8, waiting for transfers between devices, sent(): return lax.ppermute(array, ('src', 'dst'), pairs)  5.13 us
    ppermute x2, waiting for transfers between devices, passed_along(): lax.ppermute(array, axis, [(i, (i + by) % count) for i in range(count)])  4.23 us
    ppermute x2, starting transfers between devices, swapped(): lax.ppermute(array, axis, [(i, i ^ 1 << stride) for i in range(lax.axis_s...  3.54 us
    ppermute x2, starting transfers between devices, passed_along(): lax.ppermute(array, axis, [(i, (i + by) % count) for i in range(count)])  1.64 us
    unnamed x18, local copies, waits for them, and re-layouts  0.69 us
  transfers between devices with their start and end apart: 12, of which 7 were waited for; matrix products, arithmetic and copies ran while one was open for 0% of the time, Pallas kernels for 20%

profile of v8, /device:TPU:0, one launch (start us, length us, event | category | flops | bytes accessed | tf_op | source)
XLA Modules:
  0.0 30.3 jit_solution(14263525472179729526)
XLA Ops:
  0.6 3.1 %collective-permute-start.2 = (f32[400,256]{1,0:T(8,128)}, f32[400,256]{1,0:T(8,128)S(1)}, u32[]{:S(2)}, u32[]{:S(2)}) collective-permute-start(f32[400,256]{1,0:T(8,128)} %param.16), channel_id=1, source_target_pairs={{0,1},{1,0},{2,3},{3,2},{4,5},{5,4},{6,7},{7,6},{8,9},{9,8},{10,11... | collective-permute-start | bytes 1228808 | tf_op jit(solution)/shard_map/ppermute | solution.py:21
  3.7 3.1 %shard_map.179 = (f32[200,256]{1,0:T(8,128)S(1)}, f32[208,256]{1,0:T(8,128)S(1)}, f32[400,256]{1,0:T(8,128)S(1)}, f32[256,256]{1,0:T(8,128)S(1)}, f32[400,256]{1,0:T(8,128)S(1)}) custom-call(f32[400,256]{1,0:T(8,128)} %src_hbm.1, f32[1,256]{1,0:T(1,128)} %bitcast.21, f32[400,256]{1,0:T(8,128)} %dst.1, f32[16,400]{1,0:T(8,128)} %bitcast.11, ...), custom_call_target="tpu_custom_call" | custom-call | flops 20971520000 | bytes 856072 | tf_op jit(solution)/shard_map/pallas_call | solution.py:288
  6.8 0.1 collective-permute-start.1
  6.9 1.6 %collective-permute-start = (f32[200,256]{1,0:T(8,128)S(1)}, f32[200,256]{1,0:T(8,128)S(1)}, u32[]{:S(2)}, u32[]{:S(2)}) collective-permute-start(f32[200,256]{1,0:T(8,128)S(1)} %get-tuple-element.33), channel_id=1, source_target_pairs={{0,4},{4,8},{8,12},{12,16},{16,20},{20,24},{24,28},{28,0},{1,5},{5... | collective-permute-start | bytes 614408 | tf_op jit(solution)/shard_map/ppermute | solution.py:26
  8.5 0.6 %copy-done.2 = s32[2,2,256]{2,1,0:T(2,128)S(1)} copy-done((s32[2,2,256]{2,1,0:T(2,128)S(1)}, s32[2,2,256]{2,1,0:T(2,128)}, u32[]{:S(2)}) %copy-start.2) | copy-done | bytes 4120
  9.2 1.4 %shard_map.180 = (f32[400,256]{1,0:T(8,128)}, f32[1,256]{1,0:T(1,128)}, f32[16,400]{1,0:T(8,128)S(1)}, f32[400,256]{1,0:T(8,128)S(1)}, f32[256,256]{1,0:T(8,128)...) custom-call(f32[400,256]{1,0:T(8,128)S(1)} %copy-done, f32[1,256]{1,0:T(1,128)S(1)} %bitcast.15, ...), custom_call_target="tpu_custom_call" | custom-call | flops 157286400 | bytes 1528840 | tf_op jit(solution)/shard_map/pallas_call | solution.py:288
  10.5 0.5 %collective-permute-start.3 = (f32[1,256]{1,0:T(1,128)S(1)}, f32[1,256]{1,0:T(1,128)S(1)}, u32[]{:S(2)}, u32[]{:S(2)}) collective-permute-start(f32[1,256]{1,0:T(1,128)S(1)} %get-tuple-element.45), channel_id=1, source_target_pairs={{0,1},{1,0},{2,3},{3,2},{4,5},{5,4},{6,7},{7,6},{8,9},{9,8},{10,11... | collective-permute-start | bytes 3080 | tf_op jit(solution)/shard_map/ppermute | solution.py:21
  11.0 4.2 %collective-permute-done.top = f32[200,256]{1,0:T(8,128)S(1)} collective-permute-done((f32[200,256]{1,0:T(8,128)S(1)}, f32[200,256]{1,0:T(8,128)S(1)}, u32[]{:S(2)}, u32[]{:S(2)}) %collective-permute-start) | collective-permute-done | bytes 204832 | tf_op jit(solution)/shard_map/ppermute | solution.py:26
  15.2 0.3 shard_map.181
  15.6 1.2 %shard_map.182 = (f32[256,256]{1,0:T(8,128)S(1)}, f32[400,256]{1,0:T(8,128)S(1)}, f32[56,128]{1,0:T(8,128)S(1)}, f32[1,256]{1,0:T(1,128)S(1)}) custom-call(f32[400,256]{1,0:T(8,128)S(1)} %collective-permute-done.2.spare, f32[400,256]{1,0:T(8,128)S(1)} %get-tuple-element.39.src_cols, bf16[400,256]{1,0:T(8,128)(2,1)S(1)} %get-tuple-element.40.high, ...), custom_call_target="tpu_custom_call" | custom-call | flops 524288000 | bytes 2600960 | tf_op jit(solution)/shard_map/pallas_call | solution.py:288
  16.8 0.0 collective-permute-start.4
  16.8 0.7 %collective-permute-start.5 = (f32[56,128]{1,0:T(8,128)S(1)}, f32[56,128]{1,0:T(8,128)S(1)}, u32[]{:S(2)}, u32[]{:S(2)}) collective-permute-start(f32[56,128]{1,0:T(8,128)S(1)} %get-tuple-element.55), channel_id=1, source_target_pairs={{0,8},{1,9},{2,10},{3,11},{4,12},{5,13},{6,14},{7,15},{8,0},{9,1},... | collective-permute-start | bytes 86024 | tf_op jit(solution)/shard_map/ppermute | solution.py:36
  17.5 0.5 %collective-permute-done.4 = f32[56,128]{1,0:T(8,128)S(1)} collective-permute-done((f32[56,128]{1,0:T(8,128)S(1)}, f32[56,128]{1,0:T(8,128)S(1)}, u32[]{:S(2)}, u32[]{:S(2)}) %collective-permute-start.4) | collective-permute-done | bytes 28704 | tf_op jit(solution)/shard_map/ppermute | solution.py:36
  18.0 1.9 %collective-permute-start.8 = (f32[56,128]{1,0:T(8,128)S(1)}, f32[56,128]{1,0:T(8,128)S(1)}, u32[]{:S(2)}, u32[]{:S(2)}) collective-permute-start(f32[56,128]{1,0:T(8,128)S(1)} %add.12), channel_id=1, source_target_pairs={{0,24},{1,25},{2,26},{3,27},{4,28},{5,29},{6,30},{7,31},{8,16},{9,... | collective-permute-start | bytes 86024 | tf_op jit(solution)/shard_map/ppermute | solution.py:36
  19.9 0.5 %collective-permute-start.7 = (f32[56,128]{1,0:T(8,128)S(1)}, f32[56,128]{1,0:T(8,128)S(1)}, u32[]{:S(2)}, u32[]{:S(2)}) collective-permute-start(f32[56,128]{1,0:T(8,128)S(1)} %add.12), channel_id=1, source_target_pairs={{0,16},{1,17},{2,18},{3,19},{4,20},{5,21},{6,22},{7,23},{8,24},{9,... | collective-permute-start | bytes 86024 | tf_op jit(solution)/shard_map/ppermute | solution.py:36
  20.5 0.3 %collective-permute-done.5 = f32[56,128]{1,0:T(8,128)S(1)} collective-permute-done((f32[56,128]{1,0:T(8,128)S(1)}, f32[56,128]{1,0:T(8,128)S(1)}, u32[]{:S(2)}, u32[]{:S(2)}) %collective-permute-start.5) | collective-permute-done | bytes 28704 | tf_op jit(solution)/shard_map/ppermute | solution.py:36
  20.8 2.1 %collective-permute-done.8.right = f32[56,128]{1,0:T(8,128)S(1)} collective-permute-done((f32[56,128]{1,0:T(8,128)S(1)}, f32[56,128]{1,0:T(8,128)S(1)}, u32[]{:S(2)}, u32[]{:S(2)}) %collective-permute-start.8) | collective-permute-done | bytes 28704 | tf_op jit(solution)/shard_map/ppermute | solution.py:36
  22.9 0.9 %collective-permute-done.7.left = f32[56,128]{1,0:T(8,128)S(1)} collective-permute-done((f32[56,128]{1,0:T(8,128)S(1)}, f32[56,128]{1,0:T(8,128)S(1)}, u32[]{:S(2)}, u32[]{:S(2)}) %collective-permute-start.7) | collective-permute-done | bytes 28704 | tf_op jit(solution)/shard_map/ppermute | solution.py:36
  23.8 0.5 %collective-permute-start.10 = (f32[56,128]{1,0:T(8,128)S(1)}, f32[56,128]{1,0:T(8,128)S(1)}, u32[]{:S(2)}, u32[]{:S(2)}) collective-permute-start(f32[56,128]{1,0:T(8,128)S(1)} %add_add_fusion.refs_0_), channel_id=1, source_target_pairs={{0,1},{1,0},{2,3},{3,2},{4,7},{5,6},{6,5},{7,4},{8,9},{9,8},{10,11... | collective-permute-start | bytes 86024 | tf_op jit(solution)/shard_map/ppermute | solution.py:36
  24.4 2.6 %collective-permute-start.9 = (f32[56,128]{1,0:T(8,128)S(1)}, f32[56,128]{1,0:T(8,128)S(1)}, u32[]{:S(2)}, u32[]{:S(2)}) collective-permute-start(f32[56,128]{1,0:T(8,128)S(1)} %add_add_fusion.refs_0_), channel_id=1, source_target_pairs={{0,2},{1,3},{2,0},{3,1},{4,6},{5,7},{6,4},{7,5},{8,10},{9,11},{10,... | collective-permute-start | bytes 86024 | tf_op jit(solution)/shard_map/ppermute | solution.py:36
  27.0 1.1 %collective-permute-done.10.refs_2_ = f32[56,128]{1,0:T(8,128)S(1)} collective-permute-done((f32[56,128]{1,0:T(8,128)S(1)}, f32[56,128]{1,0:T(8,128)S(1)}, u32[]{:S(2)}, u32[]{:S(2)}) %collective-permute-start.10) | collective-permute-done | bytes 28704 | tf_op jit(solution)/shard_map/ppermute | solution.py:36
  28.0 1.4 %shard_map.183 = (f32[400,256]{1,0:T(8,128)}, f32[1,256]{1,0:T(1,128)}, f32[400,256]{1,0:T(8,128)}, f32[1,256]{1,0:T(1,128)}) custom-call(f32[200,256]{1,0:T(8,128)S(1)} %collective-permute-done.top, f32[208,256]{1,0:T(8,128)S(1)} %collective-permute-done.1.bottom, f32[400,256]{1,0:T(8,128)S(1)} %collective-permute-done.2.spare, ...), custom_call_target="tpu_custom_call" | custom-call | flops 262144000 | bytes 2323456 | tf_op jit(solution)/shard_map/pallas_call | solution.py:288
  29.5 0.2 collective-permute-done.9.refs_1_
  29.6 0.7 %shard_map.185 = (f32[16,400]{1,0:T(8,128)}, f32[16,400]{1,0:T(8,128)}) custom-call(f32[16,400]{1,0:T(8,128)S(1)} %bitcast.13, f32[16,400]{1,0:T(8,128)S(1)} %bitcast.14, f32[56,128]{1,0:T(8,128)S(1)} %add_add_fusion.refs_0_, f32[56,128]{1,0:T(8,128)S(1)} %collective-permute-done.9.refs_1_, f32[56,128]{1,0:T(8,128)S(1)} %collective-permute-done.10.refs_2_, ...), custom_call_target="tpu_custom_call" | custom-call | flops 6400 | bytes 165888 | tf_op jit(solution)/shard_map/pallas_call | solution.py:288
  (27 shorter events, 0.1 us)
Async XLA Ops:
  0.6 14.9 %collective-permute-start.2 = (f32[400,256]{1,0:T(8,128)}, f32[400,256]{1,0:T(8,128)S(1)}, u32[]{:S(2)}, u32[]{:S(2)}) collective-permute-start(f32[400,256]{1,0:T(8,128)} %param.16), channel_id=1, source_target_pairs={{0,1},{1,0},{2,3},{3,2},{4,5},{5,4},{6,7},{7,6},{8,9},{9,8},{10,11... | collective-permute-start | bytes 1228808 | tf_op jit(solution)/shard_map/ppermute | solution.py:21
  3.7 4.8 %copy-start = (f32[400,256]{1,0:T(8,128)S(1)}, f32[400,256]{1,0:T(8,128)}, u32[]{:S(2)}) copy-start(f32[400,256]{1,0:T(8,128)} %dst.1) | copy-start | bytes 1228804
  3.7 4.8 %copy-start.1 = (f32[400,16]{0,1:T(8,128)S(1)}, f32[400,16]{0,1:T(8,128)}, u32[]{:S(2)}) copy-start(f32[400,16]{0,1:T(8,128)} %param.18) | copy-start | bytes 76804
  3.7 4.8 %copy-start.7 = (f32[256]{0:T(256)S(1)}, f32[256]{0:T(256)}, u32[]{:S(2)}) copy-start(f32[256]{0:T(256)} %param.17) | copy-start | bytes 3076
  3.7 4.8 %copy-start.8 = (s32[2,1]{0,1:T(1,128)S(1)}, s32[2,1]{0,1:T(1,128)}, u32[]{:S(2)}) copy-start(s32[2,1]{0,1:T(1,128)} %param.22) | copy-start | bytes 28
  6.8 8.4 %collective-permute-start.1 = (f32[208,256]{1,0:T(8,128)S(1)}, f32[208,256]{1,0:T(8,128)S(1)}, u32[]{:S(2)}, u32[]{:S(2)}) collective-permute-start(f32[208,256]{1,0:T(8,128)S(1)} %get-tuple-element.34), channel_id=1, source_target_pairs={{0,4},{4,8},{8,12},{12,16},{16,20},{20,24},{24,28},{28,0},{1,5},{5... | collective-permute-start | bytes 638984 | tf_op jit(solution)/shard_map/ppermute | solution.py:26
  6.9 1.6 %copy-start.5 = (s32[2,512]{1,0:T(2,128)S(1)}, s32[2,512]{1,0:T(2,128)}, u32[]{:S(2)}) copy-start(s32[2,512]{1,0:T(2,128)} %negs.1) | copy-start | bytes 12292
  6.9 8.3 %collective-permute-start = (f32[200,256]{1,0:T(8,128)S(1)}, f32[200,256]{1,0:T(8,128)S(1)}, u32[]{:S(2)}, u32[]{:S(2)}) collective-permute-start(f32[200,256]{1,0:T(8,128)S(1)} %get-tuple-element.33), channel_id=1, source_target_pairs={{0,4},{4,8},{8,12},{12,16},{16,20},{20,24},{24,28},{28,0},{1,5},{5... | collective-permute-start | bytes 614408 | tf_op jit(solution)/shard_map/ppermute | solution.py:26
  8.5 0.7 %copy-start.2 = (s32[2,2,256]{2,1,0:T(2,128)S(1)}, s32[2,2,256]{2,1,0:T(2,128)}, u32[]{:S(2)}) copy-start(s32[2,2,256]{2,1,0:T(2,128)} %rows.5) | copy-start | bytes 12292
  8.5 0.7 %copy-start.4 = (s32[2,256]{1,0:T(2,128)S(1)}, s32[2,256]{1,0:T(2,128)}, u32[]{:S(2)}) copy-start(s32[2,256]{1,0:T(2,128)} %rels.3) | copy-start | bytes 6148
  8.5 0.7 %copy-start.6 = (f32[256]{0:T(256)S(1)}, f32[256]{0:T(256)}, u32[]{:S(2)}) copy-start(f32[256]{0:T(256)} %param.15) | copy-start | bytes 3076
  10.5 5.0 %collective-permute-start.3 = (f32[1,256]{1,0:T(1,128)S(1)}, f32[1,256]{1,0:T(1,128)S(1)}, u32[]{:S(2)}, u32[]{:S(2)}) collective-permute-start(f32[1,256]{1,0:T(1,128)S(1)} %get-tuple-element.45), channel_id=1, source_target_pairs={{0,1},{1,0},{2,3},{3,2},{4,5},{5,4},{6,7},{7,6},{8,9},{9,8},{10,11... | collective-permute-start | bytes 3080 | tf_op jit(solution)/shard_map/ppermute | solution.py:21
  16.8 1.2 %collective-permute-start.4 = (f32[56,128]{1,0:T(8,128)S(1)}, f32[56,128]{1,0:T(8,128)S(1)}, u32[]{:S(2)}, u32[]{:S(2)}) collective-permute-start(f32[56,128]{1,0:T(8,128)S(1)} %get-tuple-element.55), channel_id=1, source_target_pairs={{0,4},{1,5},{2,6},{3,7},{4,0},{5,1},{6,2},{7,3},{8,12},{9,13},{10,... | collective-permute-start | bytes 86024 | tf_op jit(solution)/shard_map/ppermute | solution.py:36
  16.8 3.9 %collective-permute-start.5 = (f32[56,128]{1,0:T(8,128)S(1)}, f32[56,128]{1,0:T(8,128)S(1)}, u32[]{:S(2)}, u32[]{:S(2)}) collective-permute-start(f32[56,128]{1,0:T(8,128)S(1)} %get-tuple-element.55), channel_id=1, source_target_pairs={{0,8},{1,9},{2,10},{3,11},{4,12},{5,13},{6,14},{7,15},{8,0},{9,1},... | collective-permute-start | bytes 86024 | tf_op jit(solution)/shard_map/ppermute | solution.py:36
  18.0 4.9 %collective-permute-start.8 = (f32[56,128]{1,0:T(8,128)S(1)}, f32[56,128]{1,0:T(8,128)S(1)}, u32[]{:S(2)}, u32[]{:S(2)}) collective-permute-start(f32[56,128]{1,0:T(8,128)S(1)} %add.12), channel_id=1, source_target_pairs={{0,24},{1,25},{2,26},{3,27},{4,28},{5,29},{6,30},{7,31},{8,16},{9,... | collective-permute-start | bytes 86024 | tf_op jit(solution)/shard_map/ppermute | solution.py:36
  19.9 3.9 %collective-permute-start.7 = (f32[56,128]{1,0:T(8,128)S(1)}, f32[56,128]{1,0:T(8,128)S(1)}, u32[]{:S(2)}, u32[]{:S(2)}) collective-permute-start(f32[56,128]{1,0:T(8,128)S(1)} %add.12), channel_id=1, source_target_pairs={{0,16},{1,17},{2,18},{3,19},{4,20},{5,21},{6,22},{7,23},{8,24},{9,... | collective-permute-start | bytes 86024 | tf_op jit(solution)/shard_map/ppermute | solution.py:36
  20.8 3.1 %collective-permute-start.6 = (f32[56,128]{1,0:T(8,128)S(1)}, f32[56,128]{1,0:T(8,128)S(1)}, u32[]{:S(2)}, u32[]{:S(2)}) collective-permute-start(f32[56,128]{1,0:T(8,128)S(1)} %collective-permute-done.5), channel_id=1, source_target_pairs={{0,4},{1,5},{2,6},{3,7},{4,0},{5,1},{6,2},{7,3},{8,12},{9,13},{10,... | collective-permute-start | bytes 86024 | tf_op jit(solution)/shard_map/ppermute | solution.py:36
  23.8 4.2 %collective-permute-start.10 = (f32[56,128]{1,0:T(8,128)S(1)}, f32[56,128]{1,0:T(8,128)S(1)}, u32[]{:S(2)}, u32[]{:S(2)}) collective-permute-start(f32[56,128]{1,0:T(8,128)S(1)} %add_add_fusion.refs_0_), channel_id=1, source_target_pairs={{0,1},{1,0},{2,3},{3,2},{4,7},{5,6},{6,5},{7,4},{8,9},{9,8},{10,11... | collective-permute-start | bytes 86024 | tf_op jit(solution)/shard_map/ppermute | solution.py:36
  24.4 5.3 %collective-permute-start.9 = (f32[56,128]{1,0:T(8,128)S(1)}, f32[56,128]{1,0:T(8,128)S(1)}, u32[]{:S(2)}, u32[]{:S(2)}) collective-permute-start(f32[56,128]{1,0:T(8,128)S(1)} %add_add_fusion.refs_0_), channel_id=1, source_target_pairs={{0,2},{1,3},{2,0},{3,1},{4,6},{5,7},{6,4},{7,5},{8,10},{9,11},{10,... | collective-permute-start | bytes 86024 | tf_op jit(solution)/shard_map/ppermute | solution.py:36
  28.0 1.6 %collective-permute-start.11 = (f32[56,128]{1,0:T(8,128)S(1)}, f32[56,128]{1,0:T(8,128)S(1)}, u32[]{:S(2)}, u32[]{:S(2)}) collective-permute-start(f32[56,128]{1,0:T(8,128)S(1)} %collective-permute-done.10.refs_2_), channel_id=1, source_target_pairs={{0,4},{1,5},{2,6},{3,7},{4,0},{5,1},{6,2},{7,3},{8,12},{9,13},{10,... | collective-permute-start | bytes 86024 | tf_op jit(solution)/shard_map/ppermute | solution.py:36
  28.0 1.6 %copy-start.3 = (f32[400,16]{0,1:T(8,128)S(1)}, f32[400,16]{0,1:T(8,128)}, u32[]{:S(2)}) copy-start(f32[400,16]{0,1:T(8,128)} %param.19) | copy-start | bytes 76804

commit v9 on v3

--- a/solution.py
+++ b/solution.py
@@ -51,7 +51,7 @@
     return steps
 
 
-def exchanged_terms(array):
+def exchanged_terms(array, of_chip):
     steps = [(0, r, u) for r, u in digits(lax.axis_size("src") // 2, 2)]
     steps += [(1, r, u) for r, u in digits(lax.axis_size("dst"), 1)]
     terms = None
@@ -62,7 +62,7 @@
 
         if terms is None:
             one = sent(array, (flip(1), flip(1)))
-            array = array + core_swapped(array)
+            array = of_chip(array, core_swapped(array))
             if radix == 4:
                 two = sent(array, (flip(2), flip(2)))
                 three = sent(array, (flip(3), flip(3)))
@@ -220,13 +220,13 @@
         copy.wait()
     src_hot = as_bf16(onehot(rows[0, 0:1, :], columns))
     rel_cols = dot_left(halves(rel[...]), hot_relations(0, rels, rel.shape[0]), TN)
-    scale, base = coefficient_parts(0, columns, rows, counts, negs)
     for_dst.wait()
+    for_src.wait()
     table_dst = halves(dst[...])
     table_rows = halves(dst[...].T)
-    for_src.wait()
     src_cols = dot_left(halves(src[...]), src_hot, NN)
     query = src_cols * rel_cols
+    scale, base = coefficient_parts(0, columns, rows, counts, negs)
     coef = coefficients(halves(query), table_rows, scale, base)
     query_grad = dot_split(table_dst, halves(coef), NN)
     src_grad = dot_left(halves(query_grad * rel_cols), src_hot, NT)
@@ -242,9 +242,9 @@
     product_out[...] = query_grad * src_cols
 
 
-def first_back_kernel(
-    dst, dst_state, query, coef, product, rel, rows, rels, counts, negs,
-    spare_state, table_out, state_out, rel_first_out, rel_cols_out, scale_out, base_out, spare_out,
+def between_kernel(
+    dst, dst_state, query, coef, product, rel, rows, rels, counts, negs, spare_state,
+    table_out, state_out, rel_first_out, rel_cols_out, scale_out, base_out, spare_out,
 ):
     grad = dot_split(halves(query[...]), halves(coef[...]), NT)
     table_out[...], state_out[...] = row_step(dst[...], dst_state[...], grad)
@@ -252,8 +252,9 @@
         hot_relations(0, rels, rel.shape[0]), halves(product[...]), NT
     )
     rel_cols_out[...] = dot_left(halves(rel[...]), hot_relations(1, rels, rel.shape[0]), TN)
-    scale_out[...], base_out[...] = coefficient_parts(1, dst.shape[1], rows, counts, negs)
-    spare_out[...] = spare_state[...]
+    columns = scale_out.shape[0]
+    scale_out[...], base_out[...] = coefficient_parts(1, columns, rows, counts, negs)
+    spare_out[...] = jnp.broadcast_to(spare_state[...], spare_out.shape)
 
 
 def second_gather_kernel(count, *refs):
@@ -273,14 +274,13 @@
 
 
 def second_front_kernel(
-    spare, src_cols, high, low, rel_cols, scale, base, rels, rel_first, state,
-    coef_out, scaled_out, rel_out, state_out,
+    spare, src_cols, high, low, rel_cols, scale, base, rels, rel_first,
+    coef_out, scaled_out, rel_out,
 ):
     rel_hot = hot_relations(1, rels, rel_first.shape[0])
     coef = coefficients((high[...], low[...]), halves(spare[...].T), scale[...], base[...])
     query_grad = dot_split(halves(spare[...]), halves(coef), NN)
     pack(rel_out, rel_first[...] + dot_right(rel_hot, halves(query_grad * src_cols[...]), NT))
-    state_out[...] = state[...]
     coef_out[...] = coef
     scaled_out[...] = query_grad * rel_cols[...]
 
@@ -297,6 +297,11 @@
     )
     spare_grad = dot_split((high[...], low[...]), halves(coef[...]), NT)
     spare_out[...], spare_acc[...] = row_step(spare[...], spare_state[...], spare_grad)
+
+
+def chip_kernel(own, other, state, out, state_out):
+    out[...] = own[...] + other[...]
+    state_out[...] = state[0:1, :]
 
 
 def add_kernel(left, right, out):
@@ -370,20 +375,17 @@
 
     *across, query, coef, product = first_on(1, cut(features + 24, 2), 400 * work)
     across = passed_along(tuple(across), "src", 1)
-    *within, query, coef, product = first_on(
+    *within, query, coef_first, product = first_on(
         0, cut(features + 8, 2), 1 * work, (query, coef, product)
     )
     within = tuple(core_swapped(part) for part in within)
     dst_next, dst_acc, rel_first, rel_cols, scale, base, spare_acc = call(
-        first_back_kernel,
+        between_kernel,
         [VMEM] * 11,
+        [(features, rows), (1, rows), (rels, features), (features, edges), (rows, edges), (rows, edges), (40, rows)],
+        work,
         [
-            (features, rows), (1, rows), (rels, features), (features, edges), (rows, edges),
-            (rows, edges), (1, rows),
-        ],
-        3 * work,
-        [
-            dst_table, dst_state.reshape(1, rows), query, coef, product,
+            dst_table, dst_state.reshape(1, rows), query, coef_first, product,
             rel, edge_rows, edge_rel, live, negatives, spare_state.reshape(1, rows),
         ],
     )
@@ -395,24 +397,33 @@
         2 * work,
         [*across, *within, rel_cols, edge_rows],
     )
-    coef, scaled, rel_both, spare_acc_in = call(
+    coef, scaled, rel_both = call(
         second_front_kernel,
-        [VMEM] * 10,
-        [(rows, edges), (features, edges), packed_shape(rels, features), (1, rows)],
+        [VMEM] * 9,
+        [(rows, edges), (features, edges), packed_shape(rels, features)],
         10 * work,
         [
             spare_in, src_cols, high, low, rel_cols, scale, base, edge_rel, rel_first,
-            spare_acc_in,
         ],
     )
+    arrived_state = []
+
+    def of_chip(own, other):
+        total, state = call(
+            chip_kernel, [VMEM] * 3, [own.shape, (1, rows)], 0, [own, other, spare_acc_in]
+        )
+        arrived_state.append(state)
+        return total
+
+    terms = exchanged_terms(rel_both, of_chip)
+    (arrived,) = arrived_state
     src_out, src_state_out, spare_out, spare_state_out = call(
         second_back_kernel,
         [VMEM] * 8,
         [(features, rows), (1, rows), (features, rows), (1, rows)],
         5 * work,
-        [moved, spare_in, spare_acc_in, edge_rows, high, low, coef, scaled],
-    )
-    terms = exchanged_terms(rel_both)
+        [moved, spare_in, arrived, edge_rows, high, low, coef, scaled],
+    )
     relations_out, rel_state_out = call(
         relation_kernel,
         [VMEM] * (2 + len(terms)),

time: 31.7 us -> 30.3 us (0.956)
  waiting for transfers between devices: 7.6 us -> 6.84 us
  Pallas kernels: 8.39 us -> 8.06 us
    ppermute x2, waiting for transfers between devices: 1.34 us -> 0.01 us  [swapped(): lax.ppermute(array, axis, [(i, i ^ 1 << stride) for i in range(lax.axis_s...]
    pallas_call x8 -> x9, Pallas kernels: 8.39 us -> 8.06 us  [call(): pl.pallas_call(kernel, in_specs=in_specs, out_specs=[VMEM] * len(outs), o...]
    ppermute x2, waiting for transfers between devices: 1.62 us -> 1.94 us  [passed_along(): lax.ppermute(array, axis, [(i, (i + by) % count) for i in range(count)])]
  transfers between devices with their start and end apart: 14 -> 14, of which waited for: 5 -> 6; matrix products, arithmetic and copies ran while one was open for 0% -> 0% of each run, Pallas kernels for 20% -> 24%
where the time goes in v9:
time: 30.3 us; the launch traced here: 30.1 us
  starting transfers between devices  13.8 us (46%)
  Pallas kernels  8.06 us (27%)
  waiting for transfers between devices  6.84 us (23%)
  between operations  0.75 us (2%)
  local copies, waits for them, and re-layouts  0.68 us (2%)
    pallas_call x9, Pallas kernels, call(): pl.pallas_call(kernel, in_specs=in_specs, out_specs=[VMEM] * len(outs), o...  8.06 us
    ppermute x10, starting transfers between devices, sent(): return lax.ppermute(array, ('src', 'dst'), pairs)  7.84 us
    ppermute x10, waiting for transfers between devices, sent(): return lax.ppermute(array, ('src', 'dst'), pairs)  4.89 us
    ppermute x2, starting transfers between devices, swapped(): lax.ppermute(array, axis, [(i, i ^ 1 << stride) for i in range(lax.axis_s...  3.4 us
    ppermute x2, starting transfers between devices, passed_along(): lax.ppermute(array, axis, [(i, (i + by) % count) for i in range(count)])  2.52 us
    ppermute x2, waiting for transfers between devices, passed_along(): lax.ppermute(array, axis, [(i, (i + by) % count) for i in range(count)])  1.94 us
    unnamed x18, local copies, waits for them, and re-layouts  0.68 us
  transfers between devices with their start and end apart: 14, of which 6 were waited for; matrix products, arithmetic and copies ran while one was open for 0% of the time, Pallas kernels for 24%

profile of v9, /device:TPU:0, one launch (start us, length us, event | category | flops | bytes accessed | tf_op | source)
XLA Modules:
  0.0 30.1 jit_solution(15186523854083659629)
XLA Ops:
  0.6 3.1 %collective-permute-start.4 = (f32[400,256]{1,0:T(8,128)}, f32[400,256]{1,0:T(8,128)S(1)}, u32[]{:S(2)}, u32[]{:S(2)}) collective-permute-start(f32[400,256]{1,0:T(8,128)} %param.16), channel_id=1, source_target_pairs={{0,1},{1,0},{2,3},{3,2},{4,5},{5,4},{6,7},{7,6},{8,9},{9,8},{10,11... | collective-permute-start | bytes 1228808 | tf_op jit(solution)/shard_map/ppermute | solution.py:23
  3.7 0.1 shard_map.179
  3.8 2.5 %collective-permute-start = (f32[216,256]{1,0:T(8,128)S(1)}, f32[216,256]{1,0:T(8,128)S(1)}, u32[]{:S(2)}, u32[]{:S(2)}) collective-permute-start(f32[216,256]{1,0:T(8,128)S(1)} %get-tuple-element.40), channel_id=1, source_target_pairs={{0,4},{4,8},{8,12},{12,16},{16,20},{20,24},{24,28},{28,0},{1,5},{5... | collective-permute-start | bytes 663560 | tf_op jit(solution)/shard_map/ppermute | solution.py:28
  6.3 3.0 %shard_map.180 = (f32[208,256]{1,0:T(8,128)S(1)}, f32[200,256]{1,0:T(8,128)S(1)}, f32[400,256]{1,0:T(8,128)S(1)}, f32[256,256]{1,0:T(8,128)S(1)}, f32[400,256]{1,0:T(8,128)S(1)}) custom-call(f32[400,256]{1,0:T(8,128)S(1)} %get-tuple-element.42.refs_0_, f32[256,256]{1,0:T(8,128)S(1)} %get-tuple-element.43.refs_1_, f32[400,256]{1,0:T(8,128)S(1)} %get-tuple-element.44.refs_2_, ...), custom_call_target="tpu_custom_call" | custom-call | flops 52428800 | bytes 1937416 | tf_op jit(solution)/shard_map/pallas_call | solution.py:321
  9.4 0.5 %collective-permute-start.3 = (f32[200,256]{1,0:T(8,128)S(1)}, f32[200,256]{1,0:T(8,128)S(1)}, u32[]{:S(2)}, u32[]{:S(2)}) collective-permute-start(f32[200,256]{1,0:T(8,128)S(1)} %get-tuple-element.46), channel_id=1, source_target_pairs={{0,4},{1,5},{2,6},{3,7},{4,0},{5,1},{6,2},{7,3},{8,12},{9,13},{10,... | collective-permute-start | bytes 614408 | tf_op jit(solution)/shard_map/ppermute | solution.py:38
  9.9 0.1 copy-done.5
  10.1 0.5 %copy-done.2 = s32[2,2,256]{2,1,0:T(2,128)S(1)} copy-done((s32[2,2,256]{2,1,0:T(2,128)S(1)}, s32[2,2,256]{2,1,0:T(2,128)}, u32[]{:S(2)}) %copy-start.2) | copy-done | bytes 4120
  10.6 1.4 %shard_map.181 = (f32[400,256]{1,0:T(8,128)}, f32[1,256]{1,0:T(1,128)}, f32[16,400]{1,0:T(8,128)S(1)}, f32[400,256]{1,0:T(8,128)S(1)}, f32[256,256]{1,0:T(8,128)...) custom-call(f32[400,256]{1,0:T(8,128)S(1)} %copy-done, f32[1,256]{1,0:T(1,128)S(1)} %bitcast.19, ...), custom_call_target="tpu_custom_call" | custom-call | flops 52428800 | bytes 1528840 | tf_op jit(solution)/shard_map/pallas_call | solution.py:321
  12.0 0.3 %collective-permute-start.6 = (f32[40,256]{1,0:T(8,128)S(1)}, f32[40,256]{1,0:T(8,128)S(1)}, u32[]{:S(2)}, u32[]{:S(2)}) collective-permute-start(f32[40,256]{1,0:T(8,128)S(1)} %get-tuple-element.59), channel_id=1, source_target_pairs={{0,1},{1,0},{2,3},{3,2},{4,5},{5,4},{6,7},{7,6},{8,9},{9,8},{10,11... | collective-permute-start | bytes 122888 | tf_op jit(solution)/shard_map/ppermute | solution.py:23
  12.3 1.9 %collective-permute-done.1.refs_1_ = f32[208,256]{1,0:T(8,128)S(1)} collective-permute-done((f32[208,256]{1,0:T(8,128)S(1)}, f32[208,256]{1,0:T(8,128)S(1)}, u32[]{:S(2)}, u32[]{:S(2)}) %collective-permute-start.1) | collective-permute-done | bytes 213024 | tf_op jit(solution)/shard_map/ppermute | solution.py:28
  14.2 0.3 shard_map.182
  14.5 1.2 %shard_map.183 = (f32[256,256]{1,0:T(8,128)S(1)}, f32[400,256]{1,0:T(8,128)S(1)}, f32[56,128]{1,0:T(8,128)S(1)}) custom-call(f32[400,256]{1,0:T(8,128)S(1)} %collective-permute-done.4.spare, f32[400,256]{1,0:T(8,128)S(1)} %get-tuple-element.52.src_cols, bf16[400,256]{1,0:T(8,128)(2,1)S(1)} %get-tuple-element.53.high, ...), custom_call_target="tpu_custom_call" | custom-call | flops 524288000 | bytes 2599936 | tf_op jit(solution)/shard_map/pallas_call | solution.py:321
  15.8 0.6 %collective-permute-start.7 = (f32[56,128]{1,0:T(8,128)S(1)}, f32[56,128]{1,0:T(8,128)S(1)}, u32[]{:S(2)}, u32[]{:S(2)}) collective-permute-start(f32[56,128]{1,0:T(8,128)S(1)} %get-tuple-element.58.own), channel_id=1, source_target_pairs={{0,8},{1,9},{2,10},{3,11},{4,12},{5,13},{6,14},{7,15},{8,0},{9,1},... | collective-permute-start | bytes 86024 | tf_op jit(solution)/shard_map/ppermute | solution.py:38
  16.4 0.6 %collective-permute-done.5.other = f32[56,128]{1,0:T(8,128)S(1)} collective-permute-done((f32[56,128]{1,0:T(8,128)S(1)}, f32[56,128]{1,0:T(8,128)S(1)}, u32[]{:S(2)}, u32[]{:S(2)}) %collective-permute-start.5) | collective-permute-done | bytes 28704 | tf_op jit(solution)/shard_map/ppermute | solution.py:38
  17.0 1.0 %collective-permute-start.9 = (f32[56,128]{1,0:T(8,128)S(1)}, f32[56,128]{1,0:T(8,128)S(1)}, u32[]{:S(2)}, u32[]{:S(2)}) collective-permute-start(f32[56,128]{1,0:T(8,128)S(1)} %get-tuple-element.69), channel_id=1, source_target_pairs={{0,16},{1,17},{2,18},{3,19},{4,20},{5,21},{6,22},{7,23},{8,24},{9,... | collective-permute-start | bytes 86024 | tf_op jit(solution)/shard_map/ppermute | solution.py:38
  18.0 1.4 %collective-permute-start.10 = (f32[56,128]{1,0:T(8,128)S(1)}, f32[56,128]{1,0:T(8,128)S(1)}, u32[]{:S(2)}, u32[]{:S(2)}) collective-permute-start(f32[56,128]{1,0:T(8,128)S(1)} %get-tuple-element.69), channel_id=1, source_target_pairs={{0,24},{1,25},{2,26},{3,27},{4,28},{5,29},{6,30},{7,31},{8,16},{9,... | collective-permute-start | bytes 86024 | tf_op jit(solution)/shard_map/ppermute | solution.py:38
  19.4 0.3 collective-permute-done.7
  19.7 1.1 %collective-permute-done.9.left = f32[56,128]{1,0:T(8,128)S(1)} collective-permute-done((f32[56,128]{1,0:T(8,128)S(1)}, f32[56,128]{1,0:T(8,128)S(1)}, u32[]{:S(2)}, u32[]{:S(2)}) %collective-permute-start.9) | collective-permute-done | bytes 28704 | tf_op jit(solution)/shard_map/ppermute | solution.py:38
  20.9 1.9 %collective-permute-done.10.right = f32[56,128]{1,0:T(8,128)S(1)} collective-permute-done((f32[56,128]{1,0:T(8,128)S(1)}, f32[56,128]{1,0:T(8,128)S(1)}, u32[]{:S(2)}, u32[]{:S(2)}) %collective-permute-start.10) | collective-permute-done | bytes 28704 | tf_op jit(solution)/shard_map/ppermute | solution.py:38
  22.8 1.6 %collective-permute-start.12 = (f32[56,128]{1,0:T(8,128)S(1)}, f32[56,128]{1,0:T(8,128)S(1)}, u32[]{:S(2)}, u32[]{:S(2)}) collective-permute-start(f32[56,128]{1,0:T(8,128)S(1)} %add_add_fusion.refs_0_), channel_id=1, source_target_pairs={{0,1},{1,0},{2,3},{3,2},{4,7},{5,6},{6,5},{7,4},{8,9},{9,8},{10,11... | collective-permute-start | bytes 86024 | tf_op jit(solution)/shard_map/ppermute | solution.py:38
  24.4 2.6 %collective-permute-start.11 = (f32[56,128]{1,0:T(8,128)S(1)}, f32[56,128]{1,0:T(8,128)S(1)}, u32[]{:S(2)}, u32[]{:S(2)}) collective-permute-start(f32[56,128]{1,0:T(8,128)S(1)} %add_add_fusion.refs_0_), channel_id=1, source_target_pairs={{0,2},{1,3},{2,0},{3,1},{4,6},{5,7},{6,4},{7,5},{8,10},{9,11},{10,... | collective-permute-start | bytes 86024 | tf_op jit(solution)/shard_map/ppermute | solution.py:38
  27.0 1.4 %shard_map.185 = (f32[400,256]{1,0:T(8,128)}, f32[1,256]{1,0:T(1,128)}, f32[400,256]{1,0:T(8,128)}, f32[1,256]{1,0:T(1,128)}) custom-call(f32[408,256]{1,0:T(8,128)S(1)} %get-tuple-element.51.moved, f32[400,256]{1,0:T(8,128)S(1)} %collective-permute-done.4.spare, f32[1,256]{1,0:T(1,128)S(1)} %get-tuple-element.60.spare_state, s32[2,2,256]{2,1,0:T(2,128)S(1)} %copy-done.2, ...), custom_call_target="tpu_custom_call" | custom-call | flops 262144000 | bytes 2323456 | tf_op jit(solution)/shard_map/pallas_call | solution.py:321
  28.4 1.0 %collective-permute-done.11.refs_1_ = f32[56,128]{1,0:T(8,128)S(1)} collective-permute-done((f32[56,128]{1,0:T(8,128)S(1)}, f32[56,128]{1,0:T(8,128)S(1)}, u32[]{:S(2)}, u32[]{:S(2)}) %collective-permute-start.11) | collective-permute-done | bytes 28704 | tf_op jit(solution)/shard_map/ppermute | solution.py:38
  29.4 0.7 %shard_map.187 = (f32[16,400]{1,0:T(8,128)}, f32[16,400]{1,0:T(8,128)}) custom-call(f32[16,400]{1,0:T(8,128)S(1)} %bitcast.14, f32[16,400]{1,0:T(8,128)S(1)} %bitcast.15, f32[56,128]{1,0:T(8,128)S(1)} %add_add_fusion.refs_0_, f32[56,128]{1,0:T(8,128)S(1)} %collective-permute-done.11.refs_1_, f32[56,128]{1,0:T(8,128)S(1)} %collective-permute-done.12.refs_2_, ...), custom_call_target="tpu_custom_call" | custom-call | flops 6400 | bytes 165888 | tf_op jit(solution)/shard_map/pallas_call | solution.py:321
  (32 shorter events, 0.2 us)
Async XLA Ops:
  0.6 13.9 %collective-permute-start.4 = (f32[400,256]{1,0:T(8,128)}, f32[400,256]{1,0:T(8,128)S(1)}, u32[]{:S(2)}, u32[]{:S(2)}) collective-permute-start(f32[400,256]{1,0:T(8,128)} %param.16), channel_id=1, source_target_pairs={{0,1},{1,0},{2,3},{3,2},{4,5},{5,4},{6,7},{7,6},{8,9},{9,8},{10,11... | collective-permute-start | bytes 1228808 | tf_op jit(solution)/shard_map/ppermute | solution.py:23
  3.8 10.4 %collective-permute-start = (f32[216,256]{1,0:T(8,128)S(1)}, f32[216,256]{1,0:T(8,128)S(1)}, u32[]{:S(2)}, u32[]{:S(2)}) collective-permute-start(f32[216,256]{1,0:T(8,128)S(1)} %get-tuple-element.40), channel_id=1, source_target_pairs={{0,4},{4,8},{8,12},{12,16},{16,20},{20,24},{24,28},{28,0},{1,5},{5... | collective-permute-start | bytes 663560 | tf_op jit(solution)/shard_map/ppermute | solution.py:28
  6.3 8.0 %collective-permute-start.1 = (f32[208,256]{1,0:T(8,128)S(1)}, f32[208,256]{1,0:T(8,128)S(1)}, u32[]{:S(2)}, u32[]{:S(2)}) collective-permute-start(f32[208,256]{1,0:T(8,128)S(1)} %get-tuple-element.41), channel_id=1, source_target_pairs={{0,4},{4,8},{8,12},{12,16},{16,20},{20,24},{24,28},{28,0},{1,5},{5... | collective-permute-start | bytes 638984 | tf_op jit(solution)/shard_map/ppermute | solution.py:28
  6.3 3.6 %copy-start = (f32[400,256]{1,0:T(8,128)S(1)}, f32[400,256]{1,0:T(8,128)}, u32[]{:S(2)}) copy-start(f32[400,256]{1,0:T(8,128)} %dst.1) | copy-start | bytes 1228804
  6.3 3.6 %copy-start.1 = (f32[400,16]{0,1:T(8,128)S(1)}, f32[400,16]{0,1:T(8,128)}, u32[]{:S(2)}) copy-start(f32[400,16]{0,1:T(8,128)} %param.18) | copy-start | bytes 76804
  6.3 3.6 %copy-start.7 = (f32[256]{0:T(256)S(1)}, f32[256]{0:T(256)}, u32[]{:S(2)}) copy-start(f32[256]{0:T(256)} %param.15) | copy-start | bytes 3076
  6.3 3.6 %copy-start.8 = (f32[256]{0:T(256)S(1)}, f32[256]{0:T(256)}, u32[]{:S(2)}) copy-start(f32[256]{0:T(256)} %param.17) | copy-start | bytes 3076
  9.3 4.9 %collective-permute-start.2 = (f32[208,256]{1,0:T(8,128)S(1)}, f32[208,256]{1,0:T(8,128)S(1)}, u32[]{:S(2)}, u32[]{:S(2)}) collective-permute-start(f32[208,256]{1,0:T(8,128)S(1)} %get-tuple-element.45), channel_id=1, source_target_pairs={{0,4},{1,5},{2,6},{3,7},{4,0},{5,1},{6,2},{7,3},{8,12},{9,13},{10,... | collective-permute-start | bytes 638984 | tf_op jit(solution)/shard_map/ppermute | solution.py:38
  9.4 0.7 %copy-start.5 = (s32[2,512]{1,0:T(2,128)S(1)}, s32[2,512]{1,0:T(2,128)}, u32[]{:S(2)}) copy-start(s32[2,512]{1,0:T(2,128)} %negs.1) | copy-start | bytes 12292
  9.4 2.6 %collective-permute-start.3 = (f32[200,256]{1,0:T(8,128)S(1)}, f32[200,256]{1,0:T(8,128)S(1)}, u32[]{:S(2)}, u32[]{:S(2)}) collective-permute-start(f32[200,256]{1,0:T(8,128)S(1)} %get-tuple-element.46), channel_id=1, source_target_pairs={{0,4},{1,5},{2,6},{3,7},{4,0},{5,1},{6,2},{7,3},{8,12},{9,13},{10,... | collective-permute-start | bytes 614408 | tf_op jit(solution)/shard_map/ppermute | solution.py:38
  9.9 0.7 %copy-start.2 = (s32[2,2,256]{2,1,0:T(2,128)S(1)}, s32[2,2,256]{2,1,0:T(2,128)}, u32[]{:S(2)}) copy-start(s32[2,2,256]{2,1,0:T(2,128)} %rows.3) | copy-start | bytes 12292
  9.9 0.7 %copy-start.4 = (s32[2,256]{1,0:T(2,128)S(1)}, s32[2,256]{1,0:T(2,128)}, u32[]{:S(2)}) copy-start(s32[2,256]{1,0:T(2,128)} %rels.3) | copy-start | bytes 6148
  9.9 0.7 %copy-start.6 = (s32[2,1]{0,1:T(1,128)S(1)}, s32[2,1]{0,1:T(1,128)}, u32[]{:S(2)}) copy-start(s32[2,1]{0,1:T(1,128)} %param.22) | copy-start | bytes 28
  12.0 4.4 %collective-permute-start.6 = (f32[40,256]{1,0:T(8,128)S(1)}, f32[40,256]{1,0:T(8,128)S(1)}, u32[]{:S(2)}, u32[]{:S(2)}) collective-permute-start(f32[40,256]{1,0:T(8,128)S(1)} %get-tuple-element.59), channel_id=1, source_target_pairs={{0,1},{1,0},{2,3},{3,2},{4,5},{5,4},{6,7},{7,6},{8,9},{9,8},{10,11... | collective-permute-start | bytes 122888 | tf_op jit(solution)/shard_map/ppermute | solution.py:23
  15.8 1.2 %collective-permute-start.5 = (f32[56,128]{1,0:T(8,128)S(1)}, f32[56,128]{1,0:T(8,128)S(1)}, u32[]{:S(2)}, u32[]{:S(2)}) collective-permute-start(f32[56,128]{1,0:T(8,128)S(1)} %get-tuple-element.58.own), channel_id=1, source_target_pairs={{0,4},{1,5},{2,6},{3,7},{4,0},{5,1},{6,2},{7,3},{8,12},{9,13},{10,... | collective-permute-start | bytes 86024 | tf_op jit(solution)/shard_map/ppermute | solution.py:38
  15.8 3.9 %collective-permute-start.7 = (f32[56,128]{1,0:T(8,128)S(1)}, f32[56,128]{1,0:T(8,128)S(1)}, u32[]{:S(2)}, u32[]{:S(2)}) collective-permute-start(f32[56,128]{1,0:T(8,128)S(1)} %get-tuple-element.58.own), channel_id=1, source_target_pairs={{0,8},{1,9},{2,10},{3,11},{4,12},{5,13},{6,14},{7,15},{8,0},{9,1},... | collective-permute-start | bytes 86024 | tf_op jit(solution)/shard_map/ppermute | solution.py:38
  17.0 3.9 %collective-permute-start.9 = (f32[56,128]{1,0:T(8,128)S(1)}, f32[56,128]{1,0:T(8,128)S(1)}, u32[]{:S(2)}, u32[]{:S(2)}) collective-permute-start(f32[56,128]{1,0:T(8,128)S(1)} %get-tuple-element.69), channel_id=1, source_target_pairs={{0,16},{1,17},{2,18},{3,19},{4,20},{5,21},{6,22},{7,23},{8,24},{9,... | collective-permute-start | bytes 86024 | tf_op jit(solution)/shard_map/ppermute | solution.py:38
  18.0 4.8 %collective-permute-start.10 = (f32[56,128]{1,0:T(8,128)S(1)}, f32[56,128]{1,0:T(8,128)S(1)}, u32[]{:S(2)}, u32[]{:S(2)}) collective-permute-start(f32[56,128]{1,0:T(8,128)S(1)} %get-tuple-element.69), channel_id=1, source_target_pairs={{0,24},{1,25},{2,26},{3,27},{4,28},{5,29},{6,30},{7,31},{8,16},{9,... | collective-permute-start | bytes 86024 | tf_op jit(solution)/shard_map/ppermute | solution.py:38
  19.7 3.0 %collective-permute-start.8 = (f32[56,128]{1,0:T(8,128)S(1)}, f32[56,128]{1,0:T(8,128)S(1)}, u32[]{:S(2)}, u32[]{:S(2)}) collective-permute-start(f32[56,128]{1,0:T(8,128)S(1)} %collective-permute-done.7), channel_id=1, source_target_pairs={{0,4},{1,5},{2,6},{3,7},{4,0},{5,1},{6,2},{7,3},{8,12},{9,13},{10,... | collective-permute-start | bytes 86024 | tf_op jit(solution)/shard_map/ppermute | solution.py:38
  22.8 4.2 %collective-permute-start.12 = (f32[56,128]{1,0:T(8,128)S(1)}, f32[56,128]{1,0:T(8,128)S(1)}, u32[]{:S(2)}, u32[]{:S(2)}) collective-permute-start(f32[56,128]{1,0:T(8,128)S(1)} %add_add_fusion.refs_0_), channel_id=1, source_target_pairs={{0,1},{1,0},{2,3},{3,2},{4,7},{5,6},{6,5},{7,4},{8,9},{9,8},{10,11... | collective-permute-start | bytes 86024 | tf_op jit(solution)/shard_map/ppermute | solution.py:38
  24.4 5.0 %collective-permute-start.11 = (f32[56,128]{1,0:T(8,128)S(1)}, f32[56,128]{1,0:T(8,128)S(1)}, u32[]{:S(2)}, u32[]{:S(2)}) collective-permute-start(f32[56,128]{1,0:T(8,128)S(1)} %add_add_fusion.refs_0_), channel_id=1, source_target_pairs={{0,2},{1,3},{2,0},{3,1},{4,6},{5,7},{6,4},{7,5},{8,10},{9,11},{10,... | collective-permute-start | bytes 86024 | tf_op jit(solution)/shard_map/ppermute | solution.py:38
  27.0 2.4 %collective-permute-start.13 = (f32[56,128]{1,0:T(8,128)S(1)}, f32[56,128]{1,0:T(8,128)S(1)}, u32[]{:S(2)}, u32[]{:S(2)}) collective-permute-start(f32[56,128]{1,0:T(8,128)S(1)} %collective-permute-done.12.refs_2_), channel_id=1, source_target_pairs={{0,4},{1,5},{2,6},{3,7},{4,0},{5,1},{6,2},{7,3},{8,12},{9,13},{10,... | collective-permute-start | bytes 86024 | tf_op jit(solution)/shard_map/ppermute | solution.py:38
  27.0 2.4 %copy-start.3 = (f32[400,16]{0,1:T(8,128)S(1)}, f32[400,16]{0,1:T(8,128)}, u32[]{:S(2)}) copy-start(f32[400,16]{0,1:T(8,128)} %param.19) | copy-start | bytes 76804

commit v10 on v9

--- a/solution.py
+++ b/solution.py
@@ -252,8 +252,9 @@
         hot_relations(0, rels, rel.shape[0]), halves(product[...]), NT
     )
     rel_cols_out[...] = dot_left(halves(rel[...]), hot_relations(1, rels, rel.shape[0]), TN)
-    columns = scale_out.shape[0]
-    scale_out[...], base_out[...] = coefficient_parts(1, columns, rows, counts, negs)
+    columns = scale_out.shape[1]
+    scale, base = coefficient_parts(1, columns, rows, counts, negs)
+    scale_out[...], base_out[...] = scale.T, base.T
     spare_out[...] = jnp.broadcast_to(spare_state[...], spare_out.shape)
 
 
@@ -268,7 +269,7 @@
     features, columns = src_cols_out.shape[0], moved.shape[1]
     src_hot = as_bf16(onehot(rows[1, 0:1, :], columns))
     src_cols = dot_left(halves(moved[0:features, :]), src_hot, NN)
-    high_out[...], low_out[...] = halves(src_cols * rel_cols[...])
+    high_out[...], low_out[...] = halves((src_cols * rel_cols[...]).T)
     src_cols_out[...] = src_cols
     moved_out[...] = moved
 
@@ -278,8 +279,9 @@
     coef_out, scaled_out, rel_out,
 ):
     rel_hot = hot_relations(1, rels, rel_first.shape[0])
-    coef = coefficients((high[...], low[...]), halves(spare[...].T), scale[...], base[...])
-    query_grad = dot_split(halves(spare[...]), halves(coef), NN)
+    table = halves(spare[...])
+    coef = coefficients(table, (high[...], low[...]), scale[...], base[...])
+    query_grad = dot_split(table, halves(coef), NT)
     pack(rel_out, rel_first[...] + dot_right(rel_hot, halves(query_grad * src_cols[...]), NT))
     coef_out[...] = coef
     scaled_out[...] = query_grad * rel_cols[...]
@@ -295,7 +297,7 @@
     src_out[...], src_acc[...] = row_step(
         moved[0:features, :], moved[features : features + 1, :], src_grad
     )
-    spare_grad = dot_split((high[...], low[...]), halves(coef[...]), NT)
+    spare_grad = dot_split((high[...], low[...]), halves(coef[...]), TN)
     spare_out[...], spare_acc[...] = row_step(spare[...], spare_state[...], spare_grad)
 
 
@@ -393,7 +395,7 @@
     moved, src_cols, high, low = call(
         functools.partial(second_gather_kernel, len(across)),
         [VMEM] * (len(across) + len(within) + 2),
-        [(features + 8, rows), (features, edges)] + [jax.ShapeDtypeStruct((features, edges), BF16)] * 2,
+        [(features + 8, rows), (features, edges)] + [jax.ShapeDtypeStruct((edges, features), BF16)] * 2,
         2 * work,
         [*across, *within, rel_cols, edge_rows],
     )

time: 30.3 us -> 30.2 us (level)
  transfers between devices with their start and end apart: 14 -> 14, of which waited for: 6 -> 6; matrix products, arithmetic and copies ran while one was open for 0% -> 0% of each run, Pallas kernels for 24% -> 25%
where the time goes in v10:
time: 30.2 us; the launch traced here: 30 us
  starting transfers between devices  13.7 us (45%)
  Pallas kernels  8.14 us (27%)
  waiting for transfers between devices  6.78 us (22%)
  between operations  0.75 us (2%)
  local copies, waits for them, and re-layouts  0.68 us (2%)
    pallas_call x9, Pallas kernels, call(): pl.pallas_call(kernel, in_specs=in_specs, out_specs=[VMEM] * len(outs), o...  8.14 us
    ppermute x10, starting transfers between devices, sent(): return lax.ppermute(array, ('src', 'dst'), pairs)  7.74 us
    ppermute x10, waiting for transfers between devices, sent(): return lax.ppermute(array, ('src', 'dst'), pairs)  4.9 us
    ppermute x2, starting transfers between devices, swapped(): lax.ppermute(array, axis, [(i, i ^ 1 << stride) for i in range(lax.axis_s...  3.4 us
    ppermute x2, starting transfers between devices, passed_along(): lax.ppermute(array, axis, [(i, (i + by) % count) for i in range(count)])  2.52 us
    ppermute x2, waiting for transfers between devices, passed_along(): lax.ppermute(array, axis, [(i, (i + by) % count) for i in range(count)])  1.87 us
    unnamed x18, local copies, waits for them, and re-layouts  0.68 us
  transfers between devices with their start and end apart: 14, of which 6 were waited for; matrix products, arithmetic and copies ran while one was open for 0% of the time, Pallas kernels for 25%

profile of v10, /device:TPU:0, one launch (start us, length us, event | category | flops | bytes accessed | tf_op | source)
XLA Modules:
  0.0 30.0 jit_solution(18042037693557210370)
XLA Ops:
  0.6 3.1 %collective-permute-start.4 = (f32[400,256]{1,0:T(8,128)}, f32[400,256]{1,0:T(8,128)S(1)}, u32[]{:S(2)}, u32[]{:S(2)}) collective-permute-start(f32[400,256]{1,0:T(8,128)} %param.16), channel_id=1, source_target_pairs={{0,1},{1,0},{2,3},{3,2},{4,5},{5,4},{6,7},{7,6},{8,9},{9,8},{10,11... | collective-permute-start | bytes 1228808 | tf_op jit(solution)/shard_map/ppermute | solution.py:23
  3.7 0.1 shard_map.179
  3.8 2.5 %collective-permute-start = (f32[216,256]{1,0:T(8,128)S(1)}, f32[216,256]{1,0:T(8,128)S(1)}, u32[]{:S(2)}, u32[]{:S(2)}) collective-permute-start(f32[216,256]{1,0:T(8,128)S(1)} %get-tuple-element.40), channel_id=1, source_target_pairs={{0,4},{4,8},{8,12},{12,16},{16,20},{20,24},{24,28},{28,0},{1,5},{5... | collective-permute-start | bytes 663560 | tf_op jit(solution)/shard_map/ppermute | solution.py:28
  6.3 3.0 %shard_map.180 = (f32[208,256]{1,0:T(8,128)S(1)}, f32[200,256]{1,0:T(8,128)S(1)}, f32[400,256]{1,0:T(8,128)S(1)}, f32[256,256]{1,0:T(8,128)S(1)}, f32[400,256]{1,0:T(8,128)S(1)}) custom-call(f32[400,256]{1,0:T(8,128)S(1)} %get-tuple-element.42.refs_0_, f32[256,256]{1,0:T(8,128)S(1)} %get-tuple-element.43.refs_1_, f32[400,256]{1,0:T(8,128)S(1)} %get-tuple-element.44.refs_2_, ...), custom_call_target="tpu_custom_call" | custom-call | flops 52428800 | bytes 1937416 | tf_op jit(solution)/shard_map/pallas_call | solution.py:323
  9.4 0.5 %collective-permute-start.3 = (f32[200,256]{1,0:T(8,128)S(1)}, f32[200,256]{1,0:T(8,128)S(1)}, u32[]{:S(2)}, u32[]{:S(2)}) collective-permute-start(f32[200,256]{1,0:T(8,128)S(1)} %get-tuple-element.46), channel_id=1, source_target_pairs={{0,4},{1,5},{2,6},{3,7},{4,0},{5,1},{6,2},{7,3},{8,12},{9,13},{10,... | collective-permute-start | bytes 614408 | tf_op jit(solution)/shard_map/ppermute | solution.py:38
  9.9 0.1 copy-done.5
  10.1 0.5 %copy-done.2 = s32[2,2,256]{2,1,0:T(2,128)S(1)} copy-done((s32[2,2,256]{2,1,0:T(2,128)S(1)}, s32[2,2,256]{2,1,0:T(2,128)}, u32[]{:S(2)}) %copy-start.2) | copy-done | bytes 4120
  10.6 1.4 %shard_map.181 = (f32[400,256]{1,0:T(8,128)}, f32[1,256]{1,0:T(1,128)}, f32[16,400]{1,0:T(8,128)S(1)}, f32[400,256]{1,0:T(8,128)S(1)}, f32[256,256]{1,0:T(8,128)...) custom-call(f32[400,256]{1,0:T(8,128)S(1)} %copy-done, f32[1,256]{1,0:T(1,128)S(1)} %bitcast.19, ...), custom_call_target="tpu_custom_call" | custom-call | flops 52428800 | bytes 1528840 | tf_op jit(solution)/shard_map/pallas_call | solution.py:323
  12.0 0.3 %collective-permute-start.6 = (f32[40,256]{1,0:T(8,128)S(1)}, f32[40,256]{1,0:T(8,128)S(1)}, u32[]{:S(2)}, u32[]{:S(2)}) collective-permute-start(f32[40,256]{1,0:T(8,128)S(1)} %get-tuple-element.59), channel_id=1, source_target_pairs={{0,1},{1,0},{2,3},{3,2},{4,5},{5,4},{6,7},{7,6},{8,9},{9,8},{10,11... | collective-permute-start | bytes 122888 | tf_op jit(solution)/shard_map/ppermute | solution.py:23
  12.3 1.9 %collective-permute-done.1.refs_1_ = f32[208,256]{1,0:T(8,128)S(1)} collective-permute-done((f32[208,256]{1,0:T(8,128)S(1)}, f32[208,256]{1,0:T(8,128)S(1)}, u32[]{:S(2)}, u32[]{:S(2)}) %collective-permute-start.1) | collective-permute-done | bytes 213024 | tf_op jit(solution)/shard_map/ppermute | solution.py:28
  14.2 0.4 %shard_map.182 = (f32[408,256]{1,0:T(8,128)S(1)}, f32[400,256]{1,0:T(8,128)S(1)}, bf16[256,400]{1,0:T(8,128)(2,1)S(1)}, bf16[256,400]{1,0:T(8,128)(2,1)S(1)}) custom-call(f32[216,256]{1,0:T(8,128)S(1)} %collective-permute-done.refs_0_, f32[208,256]{1,0:T(8,128)S(1)} %collective-permute-done.1.refs_1_, f32[208,256]{1,0:T(8,128)S(1)} %collective-permute-done.2.refs_2_, ...), custom_call_target="tpu_custom_call" | custom-call | flops 104857600 | bytes 1265664 | tf_op jit(solution)/shard_map/pallas_call | solution.py:323
  14.6 1.2 %shard_map.183 = (f32[256,256]{1,0:T(8,128)S(1)}, f32[400,256]{1,0:T(8,128)S(1)}, f32[56,128]{1,0:T(8,128)S(1)}) custom-call(f32[400,256]{1,0:T(8,128)S(1)} %collective-permute-done.4.spare, f32[400,256]{1,0:T(8,128)S(1)} %get-tuple-element.52.src_cols, bf16[256,400]{1,0:T(8,128)(2,1)S(1)} %get-tuple-element.53.high, ...), custom_call_target="tpu_custom_call" | custom-call | flops 524288000 | bytes 2599936 | tf_op jit(solution)/shard_map/pallas_call | solution.py:323
  15.8 0.5 %collective-permute-start.7 = (f32[56,128]{1,0:T(8,128)S(1)}, f32[56,128]{1,0:T(8,128)S(1)}, u32[]{:S(2)}, u32[]{:S(2)}) collective-permute-start(f32[56,128]{1,0:T(8,128)S(1)} %get-tuple-element.58.own), channel_id=1, source_target_pairs={{0,8},{1,9},{2,10},{3,11},{4,12},{5,13},{6,14},{7,15},{8,0},{9,1},... | collective-permute-start | bytes 86024 | tf_op jit(solution)/shard_map/ppermute | solution.py:38
  16.3 0.7 %collective-permute-done.5.other = f32[56,128]{1,0:T(8,128)S(1)} collective-permute-done((f32[56,128]{1,0:T(8,128)S(1)}, f32[56,128]{1,0:T(8,128)S(1)}, u32[]{:S(2)}, u32[]{:S(2)}) %collective-permute-start.5) | collective-permute-done | bytes 28704 | tf_op jit(solution)/shard_map/ppermute | solution.py:38
  17.0 0.9 %collective-permute-start.9 = (f32[56,128]{1,0:T(8,128)S(1)}, f32[56,128]{1,0:T(8,128)S(1)}, u32[]{:S(2)}, u32[]{:S(2)}) collective-permute-start(f32[56,128]{1,0:T(8,128)S(1)} %get-tuple-element.69), channel_id=1, source_target_pairs={{0,16},{1,17},{2,18},{3,19},{4,20},{5,21},{6,22},{7,23},{8,24},{9,... | collective-permute-start | bytes 86024 | tf_op jit(solution)/shard_map/ppermute | solution.py:38
  17.9 1.5 %collective-permute-start.10 = (f32[56,128]{1,0:T(8,128)S(1)}, f32[56,128]{1,0:T(8,128)S(1)}, u32[]{:S(2)}, u32[]{:S(2)}) collective-permute-start(f32[56,128]{1,0:T(8,128)S(1)} %get-tuple-element.69), channel_id=1, source_target_pairs={{0,24},{1,25},{2,26},{3,27},{4,28},{5,29},{6,30},{7,31},{8,16},{9,... | collective-permute-start | bytes 86024 | tf_op jit(solution)/shard_map/ppermute | solution.py:38
  19.4 0.3 collective-permute-done.7
  19.7 1.1 %collective-permute-done.9.left = f32[56,128]{1,0:T(8,128)S(1)} collective-permute-done((f32[56,128]{1,0:T(8,128)S(1)}, f32[56,128]{1,0:T(8,128)S(1)}, u32[]{:S(2)}, u32[]{:S(2)}) %collective-permute-start.9) | collective-permute-done | bytes 28704 | tf_op jit(solution)/shard_map/ppermute | solution.py:38
  20.9 1.8 %collective-permute-done.10.right = f32[56,128]{1,0:T(8,128)S(1)} collective-permute-done((f32[56,128]{1,0:T(8,128)S(1)}, f32[56,128]{1,0:T(8,128)S(1)}, u32[]{:S(2)}, u32[]{:S(2)}) %collective-permute-start.10) | collective-permute-done | bytes 28704 | tf_op jit(solution)/shard_map/ppermute | solution.py:38
  22.7 1.6 %collective-permute-start.12 = (f32[56,128]{1,0:T(8,128)S(1)}, f32[56,128]{1,0:T(8,128)S(1)}, u32[]{:S(2)}, u32[]{:S(2)}) collective-permute-start(f32[56,128]{1,0:T(8,128)S(1)} %add_add_fusion.refs_0_), channel_id=1, source_target_pairs={{0,1},{1,0},{2,3},{3,2},{4,7},{5,6},{6,5},{7,4},{8,9},{9,8},{10,11... | collective-permute-start | bytes 86024 | tf_op jit(solution)/shard_map/ppermute | solution.py:38
  24.4 2.6 %collective-permute-start.11 = (f32[56,128]{1,0:T(8,128)S(1)}, f32[56,128]{1,0:T(8,128)S(1)}, u32[]{:S(2)}, u32[]{:S(2)}) collective-permute-start(f32[56,128]{1,0:T(8,128)S(1)} %add_add_fusion.refs_0_), channel_id=1, source_target_pairs={{0,2},{1,3},{2,0},{3,1},{4,6},{5,7},{6,4},{7,5},{8,10},{9,11},{10,... | collective-permute-start | bytes 86024 | tf_op jit(solution)/shard_map/ppermute | solution.py:38
  27.0 1.4 %shard_map.185 = (f32[400,256]{1,0:T(8,128)}, f32[1,256]{1,0:T(1,128)}, f32[400,256]{1,0:T(8,128)}, f32[1,256]{1,0:T(1,128)}) custom-call(f32[408,256]{1,0:T(8,128)S(1)} %get-tuple-element.51.moved, f32[400,256]{1,0:T(8,128)S(1)} %collective-permute-done.4.spare, f32[1,256]{1,0:T(1,128)S(1)} %get-tuple-element.60.spare_state, s32[2,2,256]{2,1,0:T(2,128)S(1)} %copy-done.2, ...), custom_call_target="tpu_custom_call" | custom-call | flops 262144000 | bytes 2323456 | tf_op jit(solution)/shard_map/pallas_call | solution.py:323
  28.3 1.0 %collective-permute-done.11.refs_1_ = f32[56,128]{1,0:T(8,128)S(1)} collective-permute-done((f32[56,128]{1,0:T(8,128)S(1)}, f32[56,128]{1,0:T(8,128)S(1)}, u32[]{:S(2)}, u32[]{:S(2)}) %collective-permute-start.11) | collective-permute-done | bytes 28704 | tf_op jit(solution)/shard_map/ppermute | solution.py:38
  29.3 0.7 %shard_map.187 = (f32[16,400]{1,0:T(8,128)}, f32[16,400]{1,0:T(8,128)}) custom-call(f32[16,400]{1,0:T(8,128)S(1)} %bitcast.14, f32[16,400]{1,0:T(8,128)S(1)} %bitcast.15, f32[56,128]{1,0:T(8,128)S(1)} %add_add_fusion.refs_0_, f32[56,128]{1,0:T(8,128)S(1)} %collective-permute-done.11.refs_1_, f32[56,128]{1,0:T(8,128)S(1)} %collective-permute-done.12.refs_2_, ...), custom_call_target="tpu_custom_call" | custom-call | flops 6400 | bytes 165888 | tf_op jit(solution)/shard_map/pallas_call | solution.py:323
  (32 shorter events, 0.2 us)
Async XLA Ops:
  0.6 14.0 %collective-permute-start.4 = (f32[400,256]{1,0:T(8,128)}, f32[400,256]{1,0:T(8,128)S(1)}, u32[]{:S(2)}, u32[]{:S(2)}) collective-permute-start(f32[400,256]{1,0:T(8,128)} %param.16), channel_id=1, source_target_pairs={{0,1},{1,0},{2,3},{3,2},{4,5},{5,4},{6,7},{7,6},{8,9},{9,8},{10,11... | collective-permute-start | bytes 1228808 | tf_op jit(solution)/shard_map/ppermute | solution.py:23
  3.8 10.4 %collective-permute-start = (f32[216,256]{1,0:T(8,128)S(1)}, f32[216,256]{1,0:T(8,128)S(1)}, u32[]{:S(2)}, u32[]{:S(2)}) collective-permute-start(f32[216,256]{1,0:T(8,128)S(1)} %get-tuple-element.40), channel_id=1, source_target_pairs={{0,4},{4,8},{8,12},{12,16},{16,20},{20,24},{24,28},{28,0},{1,5},{5... | collective-permute-start | bytes 663560 | tf_op jit(solution)/shard_map/ppermute | solution.py:28
  6.3 8.0 %collective-permute-start.1 = (f32[208,256]{1,0:T(8,128)S(1)}, f32[208,256]{1,0:T(8,128)S(1)}, u32[]{:S(2)}, u32[]{:S(2)}) collective-permute-start(f32[208,256]{1,0:T(8,128)S(1)} %get-tuple-element.41), channel_id=1, source_target_pairs={{0,4},{4,8},{8,12},{12,16},{16,20},{20,24},{24,28},{28,0},{1,5},{5... | collective-permute-start | bytes 638984 | tf_op jit(solution)/shard_map/ppermute | solution.py:28
  6.3 3.6 %copy-start = (f32[400,256]{1,0:T(8,128)S(1)}, f32[400,256]{1,0:T(8,128)}, u32[]{:S(2)}) copy-start(f32[400,256]{1,0:T(8,128)} %dst.1) | copy-start | bytes 1228804
  6.3 3.6 %copy-start.1 = (f32[400,16]{0,1:T(8,128)S(1)}, f32[400,16]{0,1:T(8,128)}, u32[]{:S(2)}) copy-start(f32[400,16]{0,1:T(8,128)} %param.18) | copy-start | bytes 76804
  6.3 3.6 %copy-start.7 = (f32[256]{0:T(256)S(1)}, f32[256]{0:T(256)}, u32[]{:S(2)}) copy-start(f32[256]{0:T(256)} %param.15) | copy-start | bytes 3076
  6.3 3.6 %copy-start.8 = (f32[256]{0:T(256)S(1)}, f32[256]{0:T(256)}, u32[]{:S(2)}) copy-start(f32[256]{0:T(256)} %param.17) | copy-start | bytes 3076
  9.3 4.9 %collective-permute-start.2 = (f32[208,256]{1,0:T(8,128)S(1)}, f32[208,256]{1,0:T(8,128)S(1)}, u32[]{:S(2)}, u32[]{:S(2)}) collective-permute-start(f32[208,256]{1,0:T(8,128)S(1)} %get-tuple-element.45), channel_id=1, source_target_pairs={{0,4},{1,5},{2,6},{3,7},{4,0},{5,1},{6,2},{7,3},{8,12},{9,13},{10,... | collective-permute-start | bytes 638984 | tf_op jit(solution)/shard_map/ppermute | solution.py:38
  9.4 0.7 %copy-start.5 = (s32[2,512]{1,0:T(2,128)S(1)}, s32[2,512]{1,0:T(2,128)}, u32[]{:S(2)}) copy-start(s32[2,512]{1,0:T(2,128)} %negs.1) | copy-start | bytes 12292
  9.4 2.6 %collective-permute-start.3 = (f32[200,256]{1,0:T(8,128)S(1)}, f32[200,256]{1,0:T(8,128)S(1)}, u32[]{:S(2)}, u32[]{:S(2)}) collective-permute-start(f32[200,256]{1,0:T(8,128)S(1)} %get-tuple-element.46), channel_id=1, source_target_pairs={{0,4},{1,5},{2,6},{3,7},{4,0},{5,1},{6,2},{7,3},{8,12},{9,13},{10,... | collective-permute-start | bytes 614408 | tf_op jit(solution)/shard_map/ppermute | solution.py:38
  9.9 0.7 %copy-start.2 = (s32[2,2,256]{2,1,0:T(2,128)S(1)}, s32[2,2,256]{2,1,0:T(2,128)}, u32[]{:S(2)}) copy-start(s32[2,2,256]{2,1,0:T(2,128)} %rows.3) | copy-start | bytes 12292
  9.9 0.7 %copy-start.4 = (s32[2,256]{1,0:T(2,128)S(1)}, s32[2,256]{1,0:T(2,128)}, u32[]{:S(2)}) copy-start(s32[2,256]{1,0:T(2,128)} %rels.3) | copy-start | bytes 6148
  9.9 0.7 %copy-start.6 = (s32[2,1]{0,1:T(1,128)S(1)}, s32[2,1]{0,1:T(1,128)}, u32[]{:S(2)}) copy-start(s32[2,1]{0,1:T(1,128)} %param.22) | copy-start | bytes 28
  12.0 4.3 %collective-permute-start.6 = (f32[40,256]{1,0:T(8,128)S(1)}, f32[40,256]{1,0:T(8,128)S(1)}, u32[]{:S(2)}, u32[]{:S(2)}) collective-permute-start(f32[40,256]{1,0:T(8,128)S(1)} %get-tuple-element.59), channel_id=1, source_target_pairs={{0,1},{1,0},{2,3},{3,2},{4,5},{5,4},{6,7},{7,6},{8,9},{9,8},{10,11... | collective-permute-start | bytes 122888 | tf_op jit(solution)/shard_map/ppermute | solution.py:23
  15.8 1.2 %collective-permute-start.5 = (f32[56,128]{1,0:T(8,128)S(1)}, f32[56,128]{1,0:T(8,128)S(1)}, u32[]{:S(2)}, u32[]{:S(2)}) collective-permute-start(f32[56,128]{1,0:T(8,128)S(1)} %get-tuple-element.58.own), channel_id=1, source_target_pairs={{0,4},{1,5},{2,6},{3,7},{4,0},{5,1},{6,2},{7,3},{8,12},{9,13},{10,... | collective-permute-start | bytes 86024 | tf_op jit(solution)/shard_map/ppermute | solution.py:38
  15.8 3.9 %collective-permute-start.7 = (f32[56,128]{1,0:T(8,128)S(1)}, f32[56,128]{1,0:T(8,128)S(1)}, u32[]{:S(2)}, u32[]{:S(2)}) collective-permute-start(f32[56,128]{1,0:T(8,128)S(1)} %get-tuple-element.58.own), channel_id=1, source_target_pairs={{0,8},{1,9},{2,10},{3,11},{4,12},{5,13},{6,14},{7,15},{8,0},{9,1},... | collective-permute-start | bytes 86024 | tf_op jit(solution)/shard_map/ppermute | solution.py:38
  17.0 3.9 %collective-permute-start.9 = (f32[56,128]{1,0:T(8,128)S(1)}, f32[56,128]{1,0:T(8,128)S(1)}, u32[]{:S(2)}, u32[]{:S(2)}) collective-permute-start(f32[56,128]{1,0:T(8,128)S(1)} %get-tuple-element.69), channel_id=1, source_target_pairs={{0,16},{1,17},{2,18},{3,19},{4,20},{5,21},{6,22},{7,23},{8,24},{9,... | collective-permute-start | bytes 86024 | tf_op jit(solution)/shard_map/ppermute | solution.py:38
  17.9 4.8 %collective-permute-start.10 = (f32[56,128]{1,0:T(8,128)S(1)}, f32[56,128]{1,0:T(8,128)S(1)}, u32[]{:S(2)}, u32[]{:S(2)}) collective-permute-start(f32[56,128]{1,0:T(8,128)S(1)} %get-tuple-element.69), channel_id=1, source_target_pairs={{0,24},{1,25},{2,26},{3,27},{4,28},{5,29},{6,30},{7,31},{8,16},{9,... | collective-permute-start | bytes 86024 | tf_op jit(solution)/shard_map/ppermute | solution.py:38
  19.7 2.9 %collective-permute-start.8 = (f32[56,128]{1,0:T(8,128)S(1)}, f32[56,128]{1,0:T(8,128)S(1)}, u32[]{:S(2)}, u32[]{:S(2)}) collective-permute-start(f32[56,128]{1,0:T(8,128)S(1)} %collective-permute-done.7), channel_id=1, source_target_pairs={{0,4},{1,5},{2,6},{3,7},{4,0},{5,1},{6,2},{7,3},{8,12},{9,13},{10,... | collective-permute-start | bytes 86024 | tf_op jit(solution)/shard_map/ppermute | solution.py:38
  22.7 4.2 %collective-permute-start.12 = (f32[56,128]{1,0:T(8,128)S(1)}, f32[56,128]{1,0:T(8,128)S(1)}, u32[]{:S(2)}, u32[]{:S(2)}) collective-permute-start(f32[56,128]{1,0:T(8,128)S(1)} %add_add_fusion.refs_0_), channel_id=1, source_target_pairs={{0,1},{1,0},{2,3},{3,2},{4,7},{5,6},{6,5},{7,4},{8,9},{9,8},{10,11... | collective-permute-start | bytes 86024 | tf_op jit(solution)/shard_map/ppermute | solution.py:38
  24.4 5.0 %collective-permute-start.11 = (f32[56,128]{1,0:T(8,128)S(1)}, f32[56,128]{1,0:T(8,128)S(1)}, u32[]{:S(2)}, u32[]{:S(2)}) collective-permute-start(f32[56,128]{1,0:T(8,128)S(1)} %add_add_fusion.refs_0_), channel_id=1, source_target_pairs={{0,2},{1,3},{2,0},{3,1},{4,6},{5,7},{6,4},{7,5},{8,10},{9,11},{10,... | collective-permute-start | bytes 86024 | tf_op jit(solution)/shard_map/ppermute | solution.py:38
  26.9 2.4 %collective-permute-start.13 = (f32[56,128]{1,0:T(8,128)S(1)}, f32[56,128]{1,0:T(8,128)S(1)}, u32[]{:S(2)}, u32[]{:S(2)}) collective-permute-start(f32[56,128]{1,0:T(8,128)S(1)} %collective-permute-done.12.refs_2_), channel_id=1, source_target_pairs={{0,4},{1,5},{2,6},{3,7},{4,0},{5,1},{6,2},{7,3},{8,12},{9,13},{10,... | collective-permute-start | bytes 86024 | tf_op jit(solution)/shard_map/ppermute | solution.py:38
  26.9 2.4 %copy-start.3 = (f32[400,16]{0,1:T(8,128)S(1)}, f32[400,16]{0,1:T(8,128)}, u32[]{:S(2)}) copy-start(f32[400,16]{0,1:T(8,128)} %param.19) | copy-start | bytes 76804

commit v11 on v10

--- a/solution.py
+++ b/solution.py
@@ -175,7 +175,7 @@
 
 def row_step(table, state, gradient):
     new_state = state + jnp.sum(gradient * gradient, axis=0, keepdims=True) * (1.0 / table.shape[0])
-    return table - gradient * (ROW_RATE / jnp.sqrt(new_state)), new_state
+    return table - gradient * (ROW_RATE * lax.rsqrt(new_state)), new_state
 
 
 def hot_relations(round_id, edge_rel, rels):

time: 30.2 us -> 30.2 us (level)
  no operation moved by 1% of the time
where the time goes in v11:
time: 30.2 us; the launch traced here: 30 us
  starting transfers between devices  13.7 us (45%)
  Pallas kernels  8.14 us (27%)
  waiting for transfers between devices  6.78 us (22%)
  between operations  0.75 us (2%)
  local copies, waits for them, and re-layouts  0.68 us (2%)
    pallas_call x9, Pallas kernels, call(): pl.pallas_call(kernel, in_specs=in_specs, out_specs=[VMEM] * len(outs), o...  8.14 us
    ppermute x10, starting transfers between devices, sent(): return lax.ppermute(array, ('src', 'dst'), pairs)  7.74 us
    ppermute x10, waiting for transfers between devices, sent(): return lax.ppermute(array, ('src', 'dst'), pairs)  4.89 us
    ppermute x2, starting transfers between devices, swapped(): lax.ppermute(array, axis, [(i, i ^ 1 << stride) for i in range(lax.axis_s...  3.4 us
    ppermute x2, starting transfers between devices, passed_along(): lax.ppermute(array, axis, [(i, (i + by) % count) for i in range(count)])  2.51 us
    ppermute x2, waiting for transfers between devices, passed_along(): lax.ppermute(array, axis, [(i, (i + by) % count) for i in range(count)])  1.88 us
    unnamed x18, local copies, waits for them, and re-layouts  0.68 us
  transfers between devices with their start and end apart: 14, of which 6 were waited for; matrix products, arithmetic and copies ran while one was open for 0% of the time, Pallas kernels for 25%

profile of v11, /device:TPU:0, one launch (start us, length us, event | category | flops | bytes accessed | tf_op | source)
XLA Modules:
  0.0 30.0 jit_solution(10680851058186139408)
XLA Ops:
  0.6 3.1 %collective-permute-start.4 = (f32[400,256]{1,0:T(8,128)}, f32[400,256]{1,0:T(8,128)S(1)}, u32[]{:S(2)}, u32[]{:S(2)}) collective-permute-start(f32[400,256]{1,0:T(8,128)} %param.16), channel_id=1, source_target_pairs={{0,1},{1,0},{2,3},{3,2},{4,5},{5,4},{6,7},{7,6},{8,9},{9,8},{10,11... | collective-permute-start | bytes 1228808 | tf_op jit(solution)/shard_map/ppermute | solution.py:23
  3.7 0.1 shard_map.179
  3.8 2.4 %collective-permute-start = (f32[216,256]{1,0:T(8,128)S(1)}, f32[216,256]{1,0:T(8,128)S(1)}, u32[]{:S(2)}, u32[]{:S(2)}) collective-permute-start(f32[216,256]{1,0:T(8,128)S(1)} %get-tuple-element.40), channel_id=1, source_target_pairs={{0,4},{4,8},{8,12},{12,16},{16,20},{20,24},{24,28},{28,0},{1,5},{5... | collective-permute-start | bytes 663560 | tf_op jit(solution)/shard_map/ppermute | solution.py:28
  6.3 3.0 %shard_map.180 = (f32[208,256]{1,0:T(8,128)S(1)}, f32[200,256]{1,0:T(8,128)S(1)}, f32[400,256]{1,0:T(8,128)S(1)}, f32[256,256]{1,0:T(8,128)S(1)}, f32[400,256]{1,0:T(8,128)S(1)}) custom-call(f32[400,256]{1,0:T(8,128)S(1)} %get-tuple-element.42.refs_0_, f32[256,256]{1,0:T(8,128)S(1)} %get-tuple-element.43.refs_1_, f32[400,256]{1,0:T(8,128)S(1)} %get-tuple-element.44.refs_2_, ...), custom_call_target="tpu_custom_call" | custom-call | flops 52428800 | bytes 1937416 | tf_op jit(solution)/shard_map/pallas_call | solution.py:323
  9.4 0.5 %collective-permute-start.3 = (f32[200,256]{1,0:T(8,128)S(1)}, f32[200,256]{1,0:T(8,128)S(1)}, u32[]{:S(2)}, u32[]{:S(2)}) collective-permute-start(f32[200,256]{1,0:T(8,128)S(1)} %get-tuple-element.46), channel_id=1, source_target_pairs={{0,4},{1,5},{2,6},{3,7},{4,0},{5,1},{6,2},{7,3},{8,12},{9,13},{10,... | collective-permute-start | bytes 614408 | tf_op jit(solution)/shard_map/ppermute | solution.py:38
  9.9 0.1 copy-done.5
  10.1 0.5 %copy-done.2 = s32[2,2,256]{2,1,0:T(2,128)S(1)} copy-done((s32[2,2,256]{2,1,0:T(2,128)S(1)}, s32[2,2,256]{2,1,0:T(2,128)}, u32[]{:S(2)}) %copy-start.2) | copy-done | bytes 4120
  10.6 1.4 %shard_map.181 = (f32[400,256]{1,0:T(8,128)}, f32[1,256]{1,0:T(1,128)}, f32[16,400]{1,0:T(8,128)S(1)}, f32[400,256]{1,0:T(8,128)S(1)}, f32[256,256]{1,0:T(8,128)...) custom-call(f32[400,256]{1,0:T(8,128)S(1)} %copy-done, f32[1,256]{1,0:T(1,128)S(1)} %bitcast.19, ...), custom_call_target="tpu_custom_call" | custom-call | flops 52428800 | bytes 1528840 | tf_op jit(solution)/shard_map/pallas_call | solution.py:323
  12.0 0.3 %collective-permute-start.6 = (f32[40,256]{1,0:T(8,128)S(1)}, f32[40,256]{1,0:T(8,128)S(1)}, u32[]{:S(2)}, u32[]{:S(2)}) collective-permute-start(f32[40,256]{1,0:T(8,128)S(1)} %get-tuple-element.59), channel_id=1, source_target_pairs={{0,1},{1,0},{2,3},{3,2},{4,5},{5,4},{6,7},{7,6},{8,9},{9,8},{10,11... | collective-permute-start | bytes 122888 | tf_op jit(solution)/shard_map/ppermute | solution.py:23
  12.3 1.9 %collective-permute-done.1.refs_1_ = f32[208,256]{1,0:T(8,128)S(1)} collective-permute-done((f32[208,256]{1,0:T(8,128)S(1)}, f32[208,256]{1,0:T(8,128)S(1)}, u32[]{:S(2)}, u32[]{:S(2)}) %collective-permute-start.1) | collective-permute-done | bytes 213024 | tf_op jit(solution)/shard_map/ppermute | solution.py:28
  14.2 0.4 %shard_map.182 = (f32[408,256]{1,0:T(8,128)S(1)}, f32[400,256]{1,0:T(8,128)S(1)}, bf16[256,400]{1,0:T(8,128)(2,1)S(1)}, bf16[256,400]{1,0:T(8,128)(2,1)S(1)}) custom-call(f32[216,256]{1,0:T(8,128)S(1)} %collective-permute-done.refs_0_, f32[208,256]{1,0:T(8,128)S(1)} %collective-permute-done.1.refs_1_, f32[208,256]{1,0:T(8,128)S(1)} %collective-permute-done.2.refs_2_, ...), custom_call_target="tpu_custom_call" | custom-call | flops 104857600 | bytes 1265664 | tf_op jit(solution)/shard_map/pallas_call | solution.py:323
  14.6 1.2 %shard_map.183 = (f32[256,256]{1,0:T(8,128)S(1)}, f32[400,256]{1,0:T(8,128)S(1)}, f32[56,128]{1,0:T(8,128)S(1)}) custom-call(f32[400,256]{1,0:T(8,128)S(1)} %collective-permute-done.4.spare, f32[400,256]{1,0:T(8,128)S(1)} %get-tuple-element.52.src_cols, bf16[256,400]{1,0:T(8,128)(2,1)S(1)} %get-tuple-element.53.high, ...), custom_call_target="tpu_custom_call" | custom-call | flops 524288000 | bytes 2599936 | tf_op jit(solution)/shard_map/pallas_call | solution.py:323
  15.8 0.5 %collective-permute-start.7 = (f32[56,128]{1,0:T(8,128)S(1)}, f32[56,128]{1,0:T(8,128)S(1)}, u32[]{:S(2)}, u32[]{:S(2)}) collective-permute-start(f32[56,128]{1,0:T(8,128)S(1)} %get-tuple-element.58.own), channel_id=1, source_target_pairs={{0,8},{1,9},{2,10},{3,11},{4,12},{5,13},{6,14},{7,15},{8,0},{9,1},... | collective-permute-start | bytes 86024 | tf_op jit(solution)/shard_map/ppermute | solution.py:38
  16.3 0.7 %collective-permute-done.5.other = f32[56,128]{1,0:T(8,128)S(1)} collective-permute-done((f32[56,128]{1,0:T(8,128)S(1)}, f32[56,128]{1,0:T(8,128)S(1)}, u32[]{:S(2)}, u32[]{:S(2)}) %collective-permute-start.5) | collective-permute-done | bytes 28704 | tf_op jit(solution)/shard_map/ppermute | solution.py:38
  17.0 0.9 %collective-permute-start.9 = (f32[56,128]{1,0:T(8,128)S(1)}, f32[56,128]{1,0:T(8,128)S(1)}, u32[]{:S(2)}, u32[]{:S(2)}) collective-permute-start(f32[56,128]{1,0:T(8,128)S(1)} %get-tuple-element.69), channel_id=1, source_target_pairs={{0,16},{1,17},{2,18},{3,19},{4,20},{5,21},{6,22},{7,23},{8,24},{9,... | collective-permute-start | bytes 86024 | tf_op jit(solution)/shard_map/ppermute | solution.py:38
  17.9 1.5 %collective-permute-start.10 = (f32[56,128]{1,0:T(8,128)S(1)}, f32[56,128]{1,0:T(8,128)S(1)}, u32[]{:S(2)}, u32[]{:S(2)}) collective-permute-start(f32[56,128]{1,0:T(8,128)S(1)} %get-tuple-element.69), channel_id=1, source_target_pairs={{0,24},{1,25},{2,26},{3,27},{4,28},{5,29},{6,30},{7,31},{8,16},{9,... | collective-permute-start | bytes 86024 | tf_op jit(solution)/shard_map/ppermute | solution.py:38
  19.4 0.3 collective-permute-done.7
  19.7 1.1 %collective-permute-done.9.left = f32[56,128]{1,0:T(8,128)S(1)} collective-permute-done((f32[56,128]{1,0:T(8,128)S(1)}, f32[56,128]{1,0:T(8,128)S(1)}, u32[]{:S(2)}, u32[]{:S(2)}) %collective-permute-start.9) | collective-permute-done | bytes 28704 | tf_op jit(solution)/shard_map/ppermute | solution.py:38
  20.9 1.8 %collective-permute-done.10.right = f32[56,128]{1,0:T(8,128)S(1)} collective-permute-done((f32[56,128]{1,0:T(8,128)S(1)}, f32[56,128]{1,0:T(8,128)S(1)}, u32[]{:S(2)}, u32[]{:S(2)}) %collective-permute-start.10) | collective-permute-done | bytes 28704 | tf_op jit(solution)/shard_map/ppermute | solution.py:38
  22.7 1.6 %collective-permute-start.12 = (f32[56,128]{1,0:T(8,128)S(1)}, f32[56,128]{1,0:T(8,128)S(1)}, u32[]{:S(2)}, u32[]{:S(2)}) collective-permute-start(f32[56,128]{1,0:T(8,128)S(1)} %add_add_fusion.refs_0_), channel_id=1, source_target_pairs={{0,1},{1,0},{2,3},{3,2},{4,7},{5,6},{6,5},{7,4},{8,9},{9,8},{10,11... | collective-permute-start | bytes 86024 | tf_op jit(solution)/shard_map/ppermute | solution.py:38
  24.4 2.6 %collective-permute-start.11 = (f32[56,128]{1,0:T(8,128)S(1)}, f32[56,128]{1,0:T(8,128)S(1)}, u32[]{:S(2)}, u32[]{:S(2)}) collective-permute-start(f32[56,128]{1,0:T(8,128)S(1)} %add_add_fusion.refs_0_), channel_id=1, source_target_pairs={{0,2},{1,3},{2,0},{3,1},{4,6},{5,7},{6,4},{7,5},{8,10},{9,11},{10,... | collective-permute-start | bytes 86024 | tf_op jit(solution)/shard_map/ppermute | solution.py:38
  27.0 1.4 %shard_map.185 = (f32[400,256]{1,0:T(8,128)}, f32[1,256]{1,0:T(1,128)}, f32[400,256]{1,0:T(8,128)}, f32[1,256]{1,0:T(1,128)}) custom-call(f32[408,256]{1,0:T(8,128)S(1)} %get-tuple-element.51.moved, f32[400,256]{1,0:T(8,128)S(1)} %collective-permute-done.4.spare, f32[1,256]{1,0:T(1,128)S(1)} %get-tuple-element.60.spare_state, s32[2,2,256]{2,1,0:T(2,128)S(1)} %copy-done.2, ...), custom_call_target="tpu_custom_call" | custom-call | flops 262144000 | bytes 2323456 | tf_op jit(solution)/shard_map/pallas_call | solution.py:323
  28.4 1.0 %collective-permute-done.11.refs_1_ = f32[56,128]{1,0:T(8,128)S(1)} collective-permute-done((f32[56,128]{1,0:T(8,128)S(1)}, f32[56,128]{1,0:T(8,128)S(1)}, u32[]{:S(2)}, u32[]{:S(2)}) %collective-permute-start.11) | collective-permute-done | bytes 28704 | tf_op jit(solution)/shard_map/ppermute | solution.py:38
  29.3 0.7 %shard_map.187 = (f32[16,400]{1,0:T(8,128)}, f32[16,400]{1,0:T(8,128)}) custom-call(f32[16,400]{1,0:T(8,128)S(1)} %bitcast.14, f32[16,400]{1,0:T(8,128)S(1)} %bitcast.15, f32[56,128]{1,0:T(8,128)S(1)} %add_add_fusion.refs_0_, f32[56,128]{1,0:T(8,128)S(1)} %collective-permute-done.11.refs_1_, f32[56,128]{1,0:T(8,128)S(1)} %collective-permute-done.12.refs_2_, ...), custom_call_target="tpu_custom_call" | custom-call | flops 6400 | bytes 165888 | tf_op jit(solution)/shard_map/pallas_call | solution.py:323
  (32 shorter events, 0.2 us)
Async XLA Ops:
  0.6 14.0 %collective-permute-start.4 = (f32[400,256]{1,0:T(8,128)}, f32[400,256]{1,0:T(8,128)S(1)}, u32[]{:S(2)}, u32[]{:S(2)}) collective-permute-start(f32[400,256]{1,0:T(8,128)} %param.16), channel_id=1, source_target_pairs={{0,1},{1,0},{2,3},{3,2},{4,5},{5,4},{6,7},{7,6},{8,9},{9,8},{10,11... | collective-permute-start | bytes 1228808 | tf_op jit(solution)/shard_map/ppermute | solution.py:23
  3.8 10.4 %collective-permute-start = (f32[216,256]{1,0:T(8,128)S(1)}, f32[216,256]{1,0:T(8,128)S(1)}, u32[]{:S(2)}, u32[]{:S(2)}) collective-permute-start(f32[216,256]{1,0:T(8,128)S(1)} %get-tuple-element.40), channel_id=1, source_target_pairs={{0,4},{4,8},{8,12},{12,16},{16,20},{20,24},{24,28},{28,0},{1,5},{5... | collective-permute-start | bytes 663560 | tf_op jit(solution)/shard_map/ppermute | solution.py:28
  6.2 8.0 %collective-permute-start.1 = (f32[208,256]{1,0:T(8,128)S(1)}, f32[208,256]{1,0:T(8,128)S(1)}, u32[]{:S(2)}, u32[]{:S(2)}) collective-permute-start(f32[208,256]{1,0:T(8,128)S(1)} %get-tuple-element.41), channel_id=1, source_target_pairs={{0,4},{4,8},{8,12},{12,16},{16,20},{20,24},{24,28},{28,0},{1,5},{5... | collective-permute-start | bytes 638984 | tf_op jit(solution)/shard_map/ppermute | solution.py:28
  6.3 3.6 %copy-start = (f32[400,256]{1,0:T(8,128)S(1)}, f32[400,256]{1,0:T(8,128)}, u32[]{:S(2)}) copy-start(f32[400,256]{1,0:T(8,128)} %dst.1) | copy-start | bytes 1228804
  6.3 3.6 %copy-start.1 = (f32[400,16]{0,1:T(8,128)S(1)}, f32[400,16]{0,1:T(8,128)}, u32[]{:S(2)}) copy-start(f32[400,16]{0,1:T(8,128)} %param.18) | copy-start | bytes 76804
  6.3 3.6 %copy-start.7 = (f32[256]{0:T(256)S(1)}, f32[256]{0:T(256)}, u32[]{:S(2)}) copy-start(f32[256]{0:T(256)} %param.15) | copy-start | bytes 3076
  6.3 3.6 %copy-start.8 = (f32[256]{0:T(256)S(1)}, f32[256]{0:T(256)}, u32[]{:S(2)}) copy-start(f32[256]{0:T(256)} %param.17) | copy-start | bytes 3076
  9.3 4.9 %collective-permute-start.2 = (f32[208,256]{1,0:T(8,128)S(1)}, f32[208,256]{1,0:T(8,128)S(1)}, u32[]{:S(2)}, u32[]{:S(2)}) collective-permute-start(f32[208,256]{1,0:T(8,128)S(1)} %get-tuple-element.45), channel_id=1, source_target_pairs={{0,4},{1,5},{2,6},{3,7},{4,0},{5,1},{6,2},{7,3},{8,12},{9,13},{10,... | collective-permute-start | bytes 638984 | tf_op jit(solution)/shard_map/ppermute | solution.py:38
  9.4 0.7 %copy-start.5 = (s32[2,512]{1,0:T(2,128)S(1)}, s32[2,512]{1,0:T(2,128)}, u32[]{:S(2)}) copy-start(s32[2,512]{1,0:T(2,128)} %negs.1) | copy-start | bytes 12292
  9.4 2.6 %collective-permute-start.3 = (f32[200,256]{1,0:T(8,128)S(1)}, f32[200,256]{1,0:T(8,128)S(1)}, u32[]{:S(2)}, u32[]{:S(2)}) collective-permute-start(f32[200,256]{1,0:T(8,128)S(1)} %get-tuple-element.46), channel_id=1, source_target_pairs={{0,4},{1,5},{2,6},{3,7},{4,0},{5,1},{6,2},{7,3},{8,12},{9,13},{10,... | collective-permute-start | bytes 614408 | tf_op jit(solution)/shard_map/ppermute | solution.py:38
  9.9 0.7 %copy-start.2 = (s32[2,2,256]{2,1,0:T(2,128)S(1)}, s32[2,2,256]{2,1,0:T(2,128)}, u32[]{:S(2)}) copy-start(s32[2,2,256]{2,1,0:T(2,128)} %rows.3) | copy-start | bytes 12292
  9.9 0.7 %copy-start.4 = (s32[2,256]{1,0:T(2,128)S(1)}, s32[2,256]{1,0:T(2,128)}, u32[]{:S(2)}) copy-start(s32[2,256]{1,0:T(2,128)} %rels.3) | copy-start | bytes 6148
  9.9 0.7 %copy-start.6 = (s32[2,1]{0,1:T(1,128)S(1)}, s32[2,1]{0,1:T(1,128)}, u32[]{:S(2)}) copy-start(s32[2,1]{0,1:T(1,128)} %param.22) | copy-start | bytes 28
  12.0 4.3 %collective-permute-start.6 = (f32[40,256]{1,0:T(8,128)S(1)}, f32[40,256]{1,0:T(8,128)S(1)}, u32[]{:S(2)}, u32[]{:S(2)}) collective-permute-start(f32[40,256]{1,0:T(8,128)S(1)} %get-tuple-element.59), channel_id=1, source_target_pairs={{0,1},{1,0},{2,3},{3,2},{4,5},{5,4},{6,7},{7,6},{8,9},{9,8},{10,11... | collective-permute-start | bytes 122888 | tf_op jit(solution)/shard_map/ppermute | solution.py:23
  15.8 1.2 %collective-permute-start.5 = (f32[56,128]{1,0:T(8,128)S(1)}, f32[56,128]{1,0:T(8,128)S(1)}, u32[]{:S(2)}, u32[]{:S(2)}) collective-permute-start(f32[56,128]{1,0:T(8,128)S(1)} %get-tuple-element.58.own), channel_id=1, source_target_pairs={{0,4},{1,5},{2,6},{3,7},{4,0},{5,1},{6,2},{7,3},{8,12},{9,13},{10,... | collective-permute-start | bytes 86024 | tf_op jit(solution)/shard_map/ppermute | solution.py:38
  15.8 3.9 %collective-permute-start.7 = (f32[56,128]{1,0:T(8,128)S(1)}, f32[56,128]{1,0:T(8,128)S(1)}, u32[]{:S(2)}, u32[]{:S(2)}) collective-permute-start(f32[56,128]{1,0:T(8,128)S(1)} %get-tuple-element.58.own), channel_id=1, source_target_pairs={{0,8},{1,9},{2,10},{3,11},{4,12},{5,13},{6,14},{7,15},{8,0},{9,1},... | collective-permute-start | bytes 86024 | tf_op jit(solution)/shard_map/ppermute | solution.py:38
  17.0 3.9 %collective-permute-start.9 = (f32[56,128]{1,0:T(8,128)S(1)}, f32[56,128]{1,0:T(8,128)S(1)}, u32[]{:S(2)}, u32[]{:S(2)}) collective-permute-start(f32[56,128]{1,0:T(8,128)S(1)} %get-tuple-element.69), channel_id=1, source_target_pairs={{0,16},{1,17},{2,18},{3,19},{4,20},{5,21},{6,22},{7,23},{8,24},{9,... | collective-permute-start | bytes 86024 | tf_op jit(solution)/shard_map/ppermute | solution.py:38
  17.9 4.8 %collective-permute-start.10 = (f32[56,128]{1,0:T(8,128)S(1)}, f32[56,128]{1,0:T(8,128)S(1)}, u32[]{:S(2)}, u32[]{:S(2)}) collective-permute-start(f32[56,128]{1,0:T(8,128)S(1)} %get-tuple-element.69), channel_id=1, source_target_pairs={{0,24},{1,25},{2,26},{3,27},{4,28},{5,29},{6,30},{7,31},{8,16},{9,... | collective-permute-start | bytes 86024 | tf_op jit(solution)/shard_map/ppermute | solution.py:38
  19.7 2.9 %collective-permute-start.8 = (f32[56,128]{1,0:T(8,128)S(1)}, f32[56,128]{1,0:T(8,128)S(1)}, u32[]{:S(2)}, u32[]{:S(2)}) collective-permute-start(f32[56,128]{1,0:T(8,128)S(1)} %collective-permute-done.7), channel_id=1, source_target_pairs={{0,4},{1,5},{2,6},{3,7},{4,0},{5,1},{6,2},{7,3},{8,12},{9,13},{10,... | collective-permute-start | bytes 86024 | tf_op jit(solution)/shard_map/ppermute | solution.py:38
  22.7 4.2 %collective-permute-start.12 = (f32[56,128]{1,0:T(8,128)S(1)}, f32[56,128]{1,0:T(8,128)S(1)}, u32[]{:S(2)}, u32[]{:S(2)}) collective-permute-start(f32[56,128]{1,0:T(8,128)S(1)} %add_add_fusion.refs_0_), channel_id=1, source_target_pairs={{0,1},{1,0},{2,3},{3,2},{4,7},{5,6},{6,5},{7,4},{8,9},{9,8},{10,11... | collective-permute-start | bytes 86024 | tf_op jit(solution)/shard_map/ppermute | solution.py:38
  24.4 5.0 %collective-permute-start.11 = (f32[56,128]{1,0:T(8,128)S(1)}, f32[56,128]{1,0:T(8,128)S(1)}, u32[]{:S(2)}, u32[]{:S(2)}) collective-permute-start(f32[56,128]{1,0:T(8,128)S(1)} %add_add_fusion.refs_0_), channel_id=1, source_target_pairs={{0,2},{1,3},{2,0},{3,1},{4,6},{5,7},{6,4},{7,5},{8,10},{9,11},{10,... | collective-permute-start | bytes 86024 | tf_op jit(solution)/shard_map/ppermute | solution.py:38
  26.9 2.4 %collective-permute-start.13 = (f32[56,128]{1,0:T(8,128)S(1)}, f32[56,128]{1,0:T(8,128)S(1)}, u32[]{:S(2)}, u32[]{:S(2)}) collective-permute-start(f32[56,128]{1,0:T(8,128)S(1)} %collective-permute-done.12.refs_2_), channel_id=1, source_target_pairs={{0,4},{1,5},{2,6},{3,7},{4,0},{5,1},{6,2},{7,3},{8,12},{9,13},{10,... | collective-permute-start | bytes 86024 | tf_op jit(solution)/shard_map/ppermute | solution.py:38
  26.9 2.4 %copy-start.3 = (f32[400,16]{0,1:T(8,128)S(1)}, f32[400,16]{0,1:T(8,128)}, u32[]{:S(2)}) copy-start(f32[400,16]{0,1:T(8,128)} %param.19) | copy-start | bytes 76804
